TPU v7x, 32 devices: a whole 2x2x4 slice. The times are simulated.
32 devices in a mesh: expert: 8 (over z, y), hidden: 4 (over x, core).
Axes of the slice: x: 2, y: 2, z: 4, core: 2. Of those that a mesh axis runs over, the one named last changes fastest.
Arguments:
- inputs: bfloat16 [8192, 1024], P(('expert', 'hidden')), may hold values from -6 to 6
- first_gain: float32 [1024], replicated, may hold values from 0.1 to 1.9
- query_weight: bfloat16 [1024, 1024], replicated, may hold values from -0.25 to 0.25
- key_weight: bfloat16 [1024, 512], replicated, may hold values from -0.25 to 0.25
- value_weight: bfloat16 [1024, 512], replicated, may hold values from -0.1875 to 0.1875
- out_weight: bfloat16 [1024, 1024], replicated, may hold values from -0.75 to 0.75
- second_gain: float32 [1024], replicated, may hold values from 0.1 to 1.9
- router_weight: bfloat16 [1024, 32], replicated, may hold values from -0.09375 to 0.09375
- gate_weight: bfloat16 [32, 512, 1024], P('expert', 'hidden'), may hold values from -0.1875 to 0.1875
- up_weight: bfloat16 [32, 512, 1024], P('expert', 'hidden'), may hold values from -0.1875 to 0.1875
- down_weight: bfloat16 [32, 512, 1024], P('expert', 'hidden'), may hold values from -1 to 1
- routes: int32 [8192, 8], P(('expert', 'hidden')), may hold values from 0 to 31, all different within a row
- segments: int32 [8192], P(('expert', 'hidden')), may hold values from 0 to 3, as said below
- cotangent: bfloat16 [8192, 1024], P(('expert', 'hidden')), may hold values from -6 to 6
Outputs:
- block_out: bfloat16 [8192, 1024], P(('expert', 'hidden'))
- input_grad: bfloat16 [8192, 1024], P(('expert', 'hidden'))
- first_gain_grad: float32 [1024], P(('expert', 'hidden'))
- query_grad: float32 [1024, 1024], P(('expert', 'hidden'))
- key_grad: float32 [1024, 512], P(('expert', 'hidden'))
- value_grad: float32 [1024, 512], P(('expert', 'hidden'))
- out_weight_grad: float32 [1024, 1024], P(('expert', 'hidden'))
- second_gain_grad: float32 [1024], P(('expert', 'hidden'))
- router_grad: float32 [1024, 32], P(('expert', 'hidden'))
- gate_grad: float32 [32, 512, 1024], P('expert', 'hidden')
- up_grad: float32 [32, 512, 1024], P('expert', 'hidden')
- down_grad: float32 [32, 512, 1024], P('expert', 'hidden')
Inputs may be any that keep to these rules, and one draw needn't show every extreme that they name: `routes`: each row names 8 different experts. `segments`: along each sequence of 1024 tokens the ids start at 0, never fall, and end at 3.
All inputs are finite; a program needn't handle non-finite values.
Results may differ from a plain program's by a relative error of at most 0.018.
Values may be sent and summed in bfloat16 or wider, within the bound.
No kernel may reach another device: no remote copies, remote signals or barrier semaphores. Data moves between devices by JAX's collectives and lax.ppermute only.
A program may use at most 192 MiB of HBM per device.

v0:
```python
import jax
import jax.numpy as jnp
from jax import lax
from jax.sharding import PartitionSpec as P

HEADS = 16
KV_HEADS = 8
HEAD_DIM = 64
EXPERTS = 32
CAP = 128


epsilon = 1e-06
rope_base = 10000.0
masked_score = -1e30


def rms_norm(values, gain_vector):
    factor = lax.rsqrt(jnp.mean(values * values, axis=-1, keepdims=True) + epsilon)
    return values * factor * gain_vector


def rotary(values, angles_at, head_size):
    half_size = head_size // 2
    spectrum = rope_base ** (-jnp.arange(half_size, dtype=jnp.float32) * 2.0 / head_size)
    angles = angles_at[:, None] * spectrum[None, :]
    cosine = jnp.cos(angles)[:, None, :]
    sine_of = jnp.sin(angles)[:, None, :]
    front = values[..., :half_size]
    back_half = values[..., half_size:]
    return jnp.concatenate(
        [front * cosine - back_half * sine_of, back_half * cosine + front * sine_of], axis=-1
    )


def swiglu(gate_value, up_value):
    return jax.nn.silu(gate_value) * up_value


def expert_forward(expert_rows, full_gate, full_up, full_down):
    gate_value = jnp.einsum(
        "rjd,jfd->rjf", expert_rows, full_gate, preferred_element_type=jnp.float32
    )
    up_value = jnp.einsum("rjd,jfd->rjf", expert_rows, full_up, preferred_element_type=jnp.float32)
    active = swiglu(gate_value, up_value).astype(jnp.bfloat16)
    result = jnp.einsum(
        "rjf,jfd->rjd", active, full_down, preferred_element_type=jnp.float32
    ).astype(jnp.bfloat16)
    return (gate_value, up_value, active, result)


def expert_backward(
    expert_rows, gate_value, up_value, active, incoming, full_gate, full_up, full_down
):
    active_grad = jnp.einsum(
        "rjd,jfd->rjf", incoming, full_down, preferred_element_type=jnp.float32
    )
    down_part = jnp.einsum("rjf,rjd->jfd", active, incoming, preferred_element_type=jnp.float32)
    unused, swiglu_back = jax.vjp(swiglu, gate_value, up_value)
    gate_back, up_back = swiglu_back(active_grad)
    gate_back = gate_back.astype(jnp.bfloat16)
    up_back = up_back.astype(jnp.bfloat16)
    gate_part = jnp.einsum(
        "rjf,rjd->jfd", gate_back, expert_rows, preferred_element_type=jnp.float32
    )
    up_part = jnp.einsum("rjf,rjd->jfd", up_back, expert_rows, preferred_element_type=jnp.float32)
    row_grads = jnp.einsum("rjf,jfd->rjd", gate_back, full_gate, preferred_element_type=jnp.float32)
    row_grads = row_grads + jnp.einsum(
        "rjf,jfd->rjd", up_back, full_up, preferred_element_type=jnp.float32
    )
    return (row_grads.astype(jnp.bfloat16), gate_part, up_part, down_part)


def local(
    inputs,
    first_gain,
    query_weight,
    key_weight,
    value_weight,
    out_weight,
    second_gain,
    router_weight,
    gate_weight,
    up_weight,
    down_weight,
    routes,
    segments,
    cotangent,
):
    token_count = inputs.shape[0]
    width = inputs.shape[1]
    group_size = HEADS // KV_HEADS
    attention_scale = HEAD_DIM ** (-0.5)
    hidden_index = lax.axis_index("hidden")
    full_gate, full_up, full_down = (
        lax.all_gather(gate_weight, "hidden", axis=1, tiled=True),
        lax.all_gather(up_weight, "hidden", axis=1, tiled=True),
        lax.all_gather(down_weight, "hidden", axis=1, tiled=True),
    )
    source = inputs.astype(jnp.float32)
    normed_low = rms_norm(source, first_gain).astype(jnp.bfloat16)
    query_lin = jnp.dot(normed_low, query_weight, preferred_element_type=jnp.float32)
    key_lin = jnp.dot(normed_low, key_weight, preferred_element_type=jnp.float32)
    value_lin = jnp.dot(normed_low, value_weight, preferred_element_type=jnp.float32)
    offsets = hidden_index * token_count + jnp.arange(token_count, dtype=jnp.int32)
    angles_at = offsets.astype(jnp.float32)
    queries = rotary(query_lin.reshape(token_count, HEADS, HEAD_DIM), angles_at, HEAD_DIM).astype(
        jnp.bfloat16
    )
    keys_here = rotary(
        key_lin.reshape(token_count, KV_HEADS, HEAD_DIM), angles_at, HEAD_DIM
    ).astype(jnp.bfloat16)
    keys_here = keys_here.reshape(token_count, KV_HEADS * HEAD_DIM)
    values_here = value_lin.astype(jnp.bfloat16)
    keys_all, values_all = (
        lax.all_gather(keys_here, "hidden", axis=0, tiled=True),
        lax.all_gather(values_here, "hidden", axis=0, tiled=True),
    )
    segment_all = lax.all_gather(segments, "hidden", axis=0, tiled=True)
    seq_length = keys_all.shape[0]
    key_head_rows = keys_all.reshape(seq_length, KV_HEADS, HEAD_DIM)
    value_head_rows = values_all.reshape(seq_length, KV_HEADS, HEAD_DIM)
    query_head_rows = queries.reshape(token_count, KV_HEADS, group_size, HEAD_DIM)
    allowed = (segments[:, None] == segment_all[None, :]) & (
        jnp.arange(seq_length, dtype=jnp.int32)[None, :] <= offsets[:, None]
    )
    attention_scores = (
        jnp.einsum(
            "nbkc,qbc->bknq", query_head_rows, key_head_rows, preferred_element_type=jnp.float32
        )
        * attention_scale
    )
    attention_scores = jnp.where(allowed, attention_scores, masked_score)
    row_peak = jnp.max(attention_scores, axis=-1, keepdims=True)
    exponent = jnp.exp(attention_scores - row_peak)
    totals = jnp.sum(exponent, axis=-1, keepdims=True)
    log_total = row_peak + jnp.log(totals)
    probabilities_lowered = (exponent / totals).astype(jnp.bfloat16)
    attended = jnp.einsum(
        "ozvn,nob->vozb", probabilities_lowered, value_head_rows, preferred_element_type=jnp.float32
    )
    attended = attended.reshape(token_count, HEADS * HEAD_DIM).astype(jnp.bfloat16)
    hidden = source + jnp.dot(attended, out_weight, preferred_element_type=jnp.float32)
    ffn_low = rms_norm(hidden, second_gain).astype(jnp.bfloat16)
    logits = jnp.dot(ffn_low, router_weight, preferred_element_type=jnp.float32)
    chosen = jnp.take_along_axis(logits, routes, axis=1)
    gates = jax.nn.softmax(chosen, axis=-1)
    picked = routes[:, :, None] == jnp.arange(EXPERTS, dtype=jnp.int32)[None, None, :]
    expert_loads = jnp.sum(picked.astype(jnp.int32), axis=1)
    earlier = jnp.cumsum(expert_loads, axis=0) - expert_loads
    slot_ids = jnp.take_along_axis(earlier, routes, axis=1)
    local_count = gate_weight.shape[0]
    groups = lax.axis_size("expert")
    buffer_rows = EXPERTS * CAP
    target = jnp.where(
        slot_ids < CAP,
        (routes // local_count * CAP + slot_ids) * local_count + routes % local_count,
        buffer_rows,
    )
    owners = jnp.broadcast_to(jnp.arange(token_count, dtype=jnp.int32)[:, None], routes.shape)
    source_row = (
        jnp.full((buffer_rows,), token_count, jnp.int32)
        .at[target.reshape(-1)]
        .set(owners.reshape(-1), mode="drop")
    )
    padded = jnp.concatenate([ffn_low, jnp.zeros((1, width), jnp.bfloat16)], axis=0)
    outgoing = jnp.take(padded, source_row, axis=0).reshape(groups, CAP * local_count, width)
    outer_grad = cotangent.astype(jnp.float32)

    def pick_rows(buffer):
        flat_rows = jnp.concatenate(
            [buffer.reshape(buffer_rows, width), jnp.zeros((1, width), buffer.dtype)], axis=0
        )
        return jnp.take(flat_rows, target, axis=0)

    def row_layout(arrived_block):
        return arrived_block.reshape(groups * CAP, local_count, width)

    def block_layout(row_block):
        return row_block.reshape(groups, CAP * local_count, width)

    arrived = lax.all_to_all(outgoing, "expert", split_axis=0, concat_axis=0, tiled=True)
    expert_rows = row_layout(arrived)
    gate_value, up_value, active, result = expert_forward(
        expert_rows, full_gate, full_up, full_down
    )
    returned = lax.all_to_all(
        block_layout(result), "expert", split_axis=0, concat_axis=0, tiled=True
    )
    pair_out = pick_rows(returned)
    pair_grads = (gates[:, :, None] * outer_grad[:, None, :]).astype(jnp.bfloat16)
    placed = (
        jnp.zeros((buffer_rows, width), jnp.bfloat16)
        .at[target.reshape(-1)]
        .set(pair_grads.reshape(-1, width), mode="drop")
    )
    arrived_grads = lax.all_to_all(
        placed.reshape(groups, CAP * local_count, width),
        "expert",
        split_axis=0,
        concat_axis=0,
        tiled=True,
    )
    rows_back, gate_part, up_part, down_part = expert_backward(
        expert_rows,
        gate_value,
        up_value,
        active,
        row_layout(arrived_grads),
        full_gate,
        full_up,
        full_down,
    )
    returned_grads = lax.all_to_all(
        block_layout(rows_back), "expert", split_axis=0, concat_axis=0, tiled=True
    )
    pair_back = pick_rows(returned_grads)
    pair_values = pair_out.astype(jnp.float32)
    block_out = (hidden + jnp.sum(gates[:, :, None] * pair_values, axis=1)).astype(jnp.bfloat16)
    gate_slopes = jnp.sum(outer_grad[:, None, :] * pair_values, axis=-1)
    unused, softmax_back = jax.vjp(lambda values: jax.nn.softmax(values, axis=-1), chosen)
    (chosen_grad,) = softmax_back(gate_slopes)
    logit_grad = jnp.sum(picked.astype(jnp.float32) * chosen_grad[:, :, None], axis=1).astype(
        jnp.bfloat16
    )
    router_part = jnp.einsum("td,te->de", ffn_low, logit_grad, preferred_element_type=jnp.float32)
    ffn_grad = jnp.sum(pair_back.astype(jnp.float32), axis=1)
    ffn_grad = ffn_grad + jnp.einsum(
        "te,de->td", logit_grad, router_weight, preferred_element_type=jnp.float32
    )
    unused, second_back = jax.vjp(rms_norm, hidden, second_gain)
    hidden_part, second_gain_part = second_back(ffn_grad)
    hidden_grad = outer_grad + hidden_part
    branch_grad = hidden_grad.astype(jnp.bfloat16)
    out_part = jnp.einsum("tk,td->kd", attended, branch_grad, preferred_element_type=jnp.float32)
    attention_output_grad = jnp.einsum(
        "td,kd->tk", branch_grad, out_weight, preferred_element_type=jnp.float32
    )
    attention_output_grad = attention_output_grad.astype(jnp.bfloat16).reshape(
        token_count, KV_HEADS, group_size, HEAD_DIM
    )
    attention_scores = (
        jnp.einsum(
            "nbkc,qbc->bknq", query_head_rows, key_head_rows, preferred_element_type=jnp.float32
        )
        * attention_scale
    )
    probs = jnp.where(
        allowed, jnp.exp(jnp.where(allowed, attention_scores, masked_score) - log_total), 0.0
    )
    probabilities_lowered = probs.astype(jnp.bfloat16)
    probs_grad = jnp.einsum(
        "nbkc,qbc->bknq", attention_output_grad, value_head_rows, preferred_element_type=jnp.float32
    )
    inner_sum = jnp.sum(probs * probs_grad, axis=-1, keepdims=True)
    logit_score_gradient = (probs * (probs_grad - inner_sum)).astype(jnp.bfloat16)
    query_turned = (
        jnp.einsum(
            "ozvn,nob->vozb",
            logit_score_gradient,
            key_head_rows,
            preferred_element_type=jnp.float32,
        )
        * attention_scale
    )
    key_turned = (
        jnp.einsum(
            "unia,iunk->auk",
            logit_score_gradient,
            query_head_rows,
            preferred_element_type=jnp.float32,
        )
        * attention_scale
    )
    value_full = jnp.einsum(
        "unia,iunk->auk",
        probabilities_lowered,
        attention_output_grad,
        preferred_element_type=jnp.float32,
    )
    key_sum, value_sum = (
        lax.psum_scatter(
            key_turned.reshape(seq_length, KV_HEADS * HEAD_DIM).astype(jnp.bfloat16),
            "hidden",
            scatter_dimension=0,
            tiled=True,
        ).astype(jnp.float32),
        lax.psum_scatter(
            value_full.reshape(seq_length, KV_HEADS * HEAD_DIM).astype(jnp.bfloat16),
            "hidden",
            scatter_dimension=0,
            tiled=True,
        ).astype(jnp.float32),
    )
    query_lin_grad = rotary(
        query_turned.reshape(token_count, HEADS, HEAD_DIM), -angles_at, HEAD_DIM
    )
    query_lin_grad = query_lin_grad.reshape(token_count, HEADS * HEAD_DIM).astype(jnp.bfloat16)
    key_lin_grad = rotary(key_sum.reshape(token_count, KV_HEADS, HEAD_DIM), -angles_at, HEAD_DIM)
    key_lin_grad = key_lin_grad.reshape(token_count, KV_HEADS * HEAD_DIM).astype(jnp.bfloat16)
    value_lin_grad = value_sum.astype(jnp.bfloat16)
    query_part = jnp.einsum(
        "td,tk->dk", normed_low, query_lin_grad, preferred_element_type=jnp.float32
    )
    key_part = jnp.einsum("td,tk->dk", normed_low, key_lin_grad, preferred_element_type=jnp.float32)
    value_part = jnp.einsum(
        "td,tk->dk", normed_low, value_lin_grad, preferred_element_type=jnp.float32
    )
    normed_grad = jnp.einsum(
        "tk,dk->td", query_lin_grad, query_weight, preferred_element_type=jnp.float32
    )
    normed_grad = normed_grad + jnp.einsum(
        "tk,dk->td", key_lin_grad, key_weight, preferred_element_type=jnp.float32
    )
    normed_grad = normed_grad + jnp.einsum(
        "tk,dk->td", value_lin_grad, value_weight, preferred_element_type=jnp.float32
    )
    unused, first_back = jax.vjp(rms_norm, source, first_gain)
    source_part, first_gain_part = first_back(normed_grad)
    input_grad = (hidden_grad + source_part).astype(jnp.bfloat16)
    weight_sums = (
        lax.psum_scatter(query_part, ("expert", "hidden"), scatter_dimension=0, tiled=True),
        lax.psum_scatter(key_part, ("expert", "hidden"), scatter_dimension=0, tiled=True),
        lax.psum_scatter(value_part, ("expert", "hidden"), scatter_dimension=0, tiled=True),
        lax.psum_scatter(out_part, ("expert", "hidden"), scatter_dimension=0, tiled=True),
        lax.psum_scatter(router_part, ("expert", "hidden"), scatter_dimension=0, tiled=True),
        lax.psum_scatter(first_gain_part, ("expert", "hidden"), scatter_dimension=0, tiled=True),
        lax.psum_scatter(second_gain_part, ("expert", "hidden"), scatter_dimension=0, tiled=True),
    )
    expert_sums = (
        lax.psum_scatter(
            gate_part.astype(jnp.bfloat16), "hidden", scatter_dimension=1, tiled=True
        ).astype(jnp.float32),
        lax.psum_scatter(
            up_part.astype(jnp.bfloat16), "hidden", scatter_dimension=1, tiled=True
        ).astype(jnp.float32),
        lax.psum_scatter(
            down_part.astype(jnp.bfloat16), "hidden", scatter_dimension=1, tiled=True
        ).astype(jnp.float32),
    )
    return (
        block_out,
        input_grad,
        weight_sums[5],
        weight_sums[0],
        weight_sums[1],
        weight_sums[2],
        weight_sums[3],
        weight_sums[6],
        weight_sums[4],
        expert_sums[0],
        expert_sums[1],
        expert_sums[2],
    )


def solution(mesh):
    in_specs = (
        P(("expert", "hidden"), None),
        P(),
        P(),
        P(),
        P(),
        P(),
        P(),
        P(),
        P("expert", "hidden", None),
        P("expert", "hidden", None),
        P("expert", "hidden", None),
        P(("expert", "hidden"), None),
        P(("expert", "hidden")),
        P(("expert", "hidden"), None),
    )
    out_specs = (
        P(("expert", "hidden"), None),
        P(("expert", "hidden"), None),
        P(("expert", "hidden")),
        P(("expert", "hidden"), None),
        P(("expert", "hidden"), None),
        P(("expert", "hidden"), None),
        P(("expert", "hidden"), None),
        P(("expert", "hidden")),
        P(("expert", "hidden"), None),
        P("expert", "hidden", None),
        P("expert", "hidden", None),
        P("expert", "hidden", None),
    )
    return jax.shard_map(local, mesh=mesh, in_specs=in_specs, out_specs=out_specs, check_vma=False)
```

profile of v0, /device:TPU:0, one launch (start us, length us, event | category | flops | bytes accessed | tf_op | source)
XLA Modules:
  0.0 1940.2 jit_solution(14887877814564008466)
XLA Ops:
  26.8 13.6 gather_fusion.2
  69.1 16.8 gather_fusion.1
  94.6 18.4 gather_fusion
  128.9 15.4 scatter_custom_fusion.1
  144.3 166.0 %all-to-all-done = bf16[8,512,1024]{2,1,0:T(8,128)(2,1)} async-done(((bf16[8,512,1024]{2,1,0:T(8,128)(2,1)}), bf16[8,512,1024]{2,1,0:T(8,128)(2,1)}, u32[]{:S(2)}, u32[]{:S(2)}) %all-to-all-start) | async-done | bytes 8388640 | tf_op jit(solution)/shard_map/all_to_all | solution.py:182
  316.4 13.3 reshape.390
  329.8 168.1 %all-to-all-done.2 = bf16[8,512,1024]{2,1,0:T(8,128)(2,1)} async-done(((bf16[8,512,1024]{2,1,0:T(8,128)(2,1)}), bf16[8,512,1024]{2,1,0:T(8,128)(2,1)}, u32[]{:S(2)}, u32[]{:S(2)}) %all-to-all-start.2) | async-done | bytes 8388640 | tf_op jit(solution)/shard_map/all_to_all | solution.py:197
  497.9 13.1 reshape.394
  511.0 13.1 fusion.30
  524.0 13.1 fusion.32
  537.1 20.5 %fusion.12 = (bf16[1024,4,512]{2,0,1:T(8,128)(2,1)}, bf16[1024,4,512]{2,0,1:T(8,128)(2,1)}, bf16[1024,4,512]{2,0,1:T(8,128)(2,1)}) fusion(f32[4,1024,512]{2,1,0:T(8,128)} %fusion.32, f32[4,1024,512]{2,1,0:T(8,128)} %fusion.30, bf16[4,512,1024]{2,1,0:T(8,128)(2,1)} %all-gather.15.cloned.1.call-done, bf16[1024,4,1024]{2,1,0:T(4,128)(2,1)} %reshape.394), kind=kOutput, calls=%fused_computation.30 | convolution fusion | flops 4328521728 | bytes 41943040 | tf_op jit(solution)/shard_map/rjd,jfd->rjf/dot_general | solution.py:55
  565.6 23.0 %copy.191 = bf16[1024,4,1024]{2,1,0:T(4,128)(2,1)} copy(bf16[1024,4,1024]{2,0,1:T(8,128)(2,1)S(1)} %convert_bitcast_fusion) | data formatting | bytes 16777216 | tf_op jit(solution)/shard_map/convert_element_type | solution.py:48
  588.6 12.5 reshape.391
  606.1 13.7 fusion.105
  619.8 16.0 fusion.34
  648.0 12.5 reshape.395
  660.6 127.5 %all-to-all-done.1 = bf16[8,512,1024]{2,1,0:T(8,128)(2,1)} async-done(((bf16[8,512,1024]{2,1,0:T(8,128)(2,1)}), bf16[8,512,1024]{2,1,0:T(8,128)(2,1)}, u32[]{:S(2)}, u32[]{:S(2)}) %all-to-all-start.1) | async-done | bytes 8388640 | tf_op jit(solution)/shard_map/all_to_all | solution.py:187
  802.7 172.5 %all-to-all-done.3 = bf16[8,512,1024]{2,1,0:T(8,128)(2,1)} async-done(((bf16[8,512,1024]{2,1,0:T(8,128)(2,1)}), bf16[8,512,1024]{2,1,0:T(8,128)(2,1)}, u32[]{:S(2)}, u32[]{:S(2)}) %all-to-all-start.3) | async-done | bytes 8388640 | tf_op jit(solution)/shard_map/all_to_all | solution.py:214
  982.8 15.4 gather_fusion.3
  998.3 15.5 gather_fusion.4
  1053.6 12.8 fusion.2
  1073.2 12.4 fusion.46
  1085.9 12.6 fusion.43
  1131.2 21.8 %reduce-scatter.29.cloned.1.call-done = bf16[4,128,1024]{2,1,0:T(8,128)(2,1)} async-done(((bf16[4,512,1024]{2,1,0:T(8,128)(2,1)}), bf16[4,128,1024]{2,1,0:T(8,128)(2,1)}) %reduce-scatter.29.cloned.1.call-update) | async-done | bytes 1048592 | tf_op jit(solution)/shard_map/reduce_scatter | solution.py:337
  1155.8 44.5 %reduce-scatter.27.cloned.1.call-done = bf16[4,128,1024]{2,1,0:T(8,128)(2,1)} async-done(((bf16[4,512,1024]{2,1,0:T(8,128)(2,1)}), bf16[4,128,1024]{2,1,0:T(8,128)(2,1)}) %reduce-scatter.27.cloned.1.call-update) | async-done | bytes 1048592 | tf_op jit(solution)/shard_map/reduce_scatter | solution.py:334
  1203.0 44.1 %reduce-scatter.25.cloned.1.call-done = bf16[4,128,1024]{2,1,0:T(8,128)(2,1)} async-done(((bf16[4,512,1024]{2,1,0:T(8,128)(2,1)}), bf16[4,128,1024]{2,1,0:T(8,128)(2,1)}) %reduce-scatter.25.cloned.1.call-update) | async-done | bytes 1048592 | tf_op jit(solution)/shard_map/reduce_scatter | solution.py:331
  1255.8 39.4 %all-reduce.5 = (f32[1024]{0:T(1024)S(1)}, f32[1024]{0:T(1024)S(1)}) all-reduce(f32[1024]{0:T(1024)S(1)} %get-tuple-element.17, f32[1024]{0:T(1024)S(1)} %get-tuple-element.15), channel_id=4, replica_groups=mesh['expert'=8,'hidden'=4] {'expert','hidden'}, use_global_device_ids=true, to_apply=%region_22.24.clone | all-reduce | flops 2048 | bytes 16384
  1299.0 85.2 %reduce-scatter.23.cloned.1.call-done = f32[32,32]{1,0:T(8,128)} async-done(((f32[1024,32]{1,0:T(8,128)}), f32[32,32]{1,0:T(8,128)}) %reduce-scatter.23.cloned.1.call-update) | async-done | bytes 4112 | tf_op jit(solution)/shard_map/reduce_scatter | solution.py:326
  1384.2 135.0 %reduce-scatter.19.cloned.1.call-done = f32[32,512]{1,0:T(8,128)} async-done(((f32[1024,512]{1,0:T(8,128)}), f32[32,512]{1,0:T(8,128)}) %reduce-scatter.19.cloned.1.call-update) | async-done | bytes 65552 | tf_op jit(solution)/shard_map/reduce_scatter | solution.py:324
  1519.2 135.3 %reduce-scatter.17.cloned.1.call-done = f32[32,512]{1,0:T(8,128)} async-done(((f32[1024,512]{1,0:T(8,128)}), f32[32,512]{1,0:T(8,128)}) %reduce-scatter.17.cloned.1.call-update) | async-done | bytes 65552 | tf_op jit(solution)/shard_map/reduce_scatter | solution.py:323
  1654.4 139.5 %reduce-scatter.21.cloned.1.call-done = f32[32,1024]{1,0:T(8,128)} async-done(((f32[1024,1024]{1,0:T(8,128)}), f32[32,1024]{1,0:T(8,128)}) %reduce-scatter.21.cloned.1.call-update) | async-done | bytes 131088 | tf_op jit(solution)/shard_map/reduce_scatter | solution.py:325
  1793.9 139.4 %reduce-scatter.15.cloned.1.call-done = f32[32,1024]{1,0:T(8,128)} async-done(((f32[1024,1024]{1,0:T(8,128)}), f32[32,1024]{1,0:T(8,128)}) %reduce-scatter.15.cloned.1.call-update) | async-done | bytes 131088 | tf_op jit(solution)/shard_map/reduce_scatter | solution.py:322
  (234 shorter events, 223.0 us)
Async XLA Ops:
  7.2 59.6 %copy-start = (bf16[1024,1024]{1,0:T(8,128)(2,1)S(1)}, bf16[1024,1024]{1,0:T(8,128)(2,1)}, u32[]{:S(2)}) copy-start(bf16[1024,1024]{1,0:T(8,128)(2,1)} %param.21) | copy-start | bytes 6291460
  7.2 19.3 copy-start.25
  7.2 19.1 copy-start.43
  7.2 33.5 %all-gather.9.cloned.1.call-start = ((), (), s32[]{:S(2)}) async-start(), calls=%async_computation.15 | async-start | bytes 1310720 | tf_op jit(solution)/shard_map/all_gather | solution.py:116
  12.4 45.0 %all-gather.7.cloned.1.call-start = ((), (), s32[]{:S(2)}) async-start(), calls=%async_computation.14 | async-start | bytes 1310720 | tf_op jit(solution)/shard_map/all_gather | solution.py:117
  67.7 18.2 copy-start.42
  67.7 18.2 copy-start.39
  68.8 25.7 %copy-start.8 = (bf16[256,1024]{1,0:T(8,128)(2,1)}, bf16[256,1024]{1,0:T(8,128)(2,1)S(1)}, u32[]{:S(2)}) copy-start(bf16[256,1024]{1,0:T(8,128)(2,1)S(1)} %multiply_convert_fusion) | copy-start | bytes 1572868
  86.1 42.5 %copy-start.31 = (pred[256,8]{0,1:T(8,128)(4,1)}, pred[256,8]{0,1:T(8,128)(4,1)S(1)}, u32[]{:S(2)}) copy-start(pred[256,8]{0,1:T(8,128)(4,1)S(1)} %get-tuple-element.23) | copy-start | bytes 6148
  86.1 42.5 %copy-start.37 = (f32[256]{0:T(256)}, f32[256]{0:T(256)S(1)}, u32[]{:S(2)}) copy-start(f32[256]{0:T(256)S(1)} %get-tuple-element.22) | copy-start | bytes 3076
  120.2 190.0 %all-to-all-start = ((bf16[8,512,1024]{2,1,0:T(8,128)(2,1)}), bf16[8,512,1024]{2,1,0:T(8,128)(2,1)}, u32[]{:S(2)}, u32[]{:S(2)}) async-start(bf16[8,512,1024]{2,1,0:T(8,128)(2,1)} %broadcast_select_fusion), calls=%async_computation | async-start | bytes 16777216 | tf_op jit(solution)/shard_map/all_to_all | solution.py:182
  126.6 384.3 %all-gather.13.cloned.1.call-start = ((), (), s32[]{:S(2)}) async-start(), calls=%async_computation.17 | async-start | bytes 5242880 | tf_op jit(solution)/shard_map/all_gather | solution.py:97
  128.5 181.7 %copy-start.7 = (f32[256,1024]{1,0:T(8,128)}, f32[256,1024]{1,0:T(8,128)S(1)}, u32[]{:S(2)}) copy-start(f32[256,1024]{1,0:T(8,128)S(1)} %convert_element_type.163) | copy-start | bytes 3145732
  128.6 665.3 %copy-start.38 = (f32[256]{0:T(256)}, f32[256]{0:T(256)S(1)}, u32[]{:S(2)}) copy-start(f32[256]{0:T(256)S(1)} %fusion.82) | copy-start | bytes 3076
  310.2 187.7 %all-to-all-start.2 = ((bf16[8,512,1024]{2,1,0:T(8,128)(2,1)}), bf16[8,512,1024]{2,1,0:T(8,128)(2,1)}, u32[]{:S(2)}, u32[]{:S(2)}) async-start(bf16[8,512,1024]{2,1,0:T(8,128)(2,1)} %bitcast.173), calls=%async_computation.2 | async-start | bytes 16777216 | tf_op jit(solution)/shard_map/all_to_all | solution.py:197
  315.2 208.8 %all-gather.11.cloned.1.call-start = ((), (), s32[]{:S(2)}) async-start(), calls=%async_computation.16 | async-start | bytes 5242880 | tf_op jit(solution)/shard_map/all_gather | solution.py:96
  315.8 221.3 %all-gather.15.cloned.1.call-start = ((), (), s32[]{:S(2)}) async-start(), calls=%async_computation.18 | async-start | bytes 5242880 | tf_op jit(solution)/shard_map/all_gather | solution.py:98
  601.1 187.0 %all-to-all-start.1 = ((bf16[8,512,1024]{2,1,0:T(8,128)(2,1)}), bf16[8,512,1024]{2,1,0:T(8,128)(2,1)}, u32[]{:S(2)}, u32[]{:S(2)}) async-start(bf16[8,512,1024]{2,1,0:T(8,128)(2,1)} %reshape.391), calls=%async_computation.1 | async-start | bytes 16777216 | tf_op jit(solution)/shard_map/all_to_all | solution.py:187
  660.6 134.0 %copy-start.30 = (f32[8,2,256]{2,1,0:T(2,128)S(1)}, f32[8,2,256]{2,1,0:T(2,128)}, u32[]{:S(2)}) copy-start(f32[8,2,256]{2,1,0:T(2,128)} %copy-done.29) | copy-start | bytes 49156
  660.6 134.0 %copy-start.33 = (f32[8,2,256]{2,1,0:T(2,128)S(1)}, f32[8,2,256]{2,1,0:T(2,128)}, u32[]{:S(2)}) copy-start(f32[8,2,256]{2,1,0:T(2,128)} %copy-done.32) | copy-start | bytes 49156
  788.1 187.1 %all-to-all-start.3 = ((bf16[8,512,1024]{2,1,0:T(8,128)(2,1)}), bf16[8,512,1024]{2,1,0:T(8,128)(2,1)}, u32[]{:S(2)}, u32[]{:S(2)}) async-start(bf16[8,512,1024]{2,1,0:T(8,128)(2,1)} %reshape.395), calls=%async_computation.3 | async-start | bytes 16777216 | tf_op jit(solution)/shard_map/all_to_all | solution.py:214
  793.1 319.5 %reduce-scatter.13.cloned.1.call-start = ((), (), s32[]{:S(2)}) async-start(), calls=%async_computation.20 | async-start | bytes 1310720 | tf_op jit(solution)/shard_map/reduce_scatter | solution.py:288
  1053.5 62.1 %reduce-scatter.11.cloned.1.call-start = ((), (), s32[]{:S(2)}) async-start(), calls=%async_computation.19 | async-start | bytes 1310720 | tf_op jit(solution)/shard_map/reduce_scatter | solution.py:282
  1073.2 79.8 %reduce-scatter.29.cloned.1.call-start = ((), (), s32[]{:S(2)}) async-start(), calls=%async_computation.28 | async-start | bytes 5242880 | tf_op jit(solution)/shard_map/reduce_scatter | solution.py:337
  1085.7 114.6 %reduce-scatter.27.cloned.1.call-start = ((), (), s32[]{:S(2)}) async-start(), calls=%async_computation.27 | async-start | bytes 5242880 | tf_op jit(solution)/shard_map/reduce_scatter | solution.py:334
  1098.6 148.5 %reduce-scatter.25.cloned.1.call-start = ((), (), s32[]{:S(2)}) async-start(), calls=%async_computation.26 | async-start | bytes 5242880 | tf_op jit(solution)/shard_map/reduce_scatter | solution.py:331
  1111.0 273.2 %reduce-scatter.23.cloned.1.call-start = ((), (), s32[]{:S(2)}) async-start(), calls=%async_computation.25 | async-start | bytes 540672 | tf_op jit(solution)/shard_map/reduce_scatter | solution.py:326
  1112.3 406.9 %reduce-scatter.19.cloned.1.call-start = ((), (), s32[]{:S(2)}) async-start(), calls=%async_computation.23 | async-start | bytes 2162688 | tf_op jit(solution)/shard_map/reduce_scatter | solution.py:324
  1115.6 538.9 %reduce-scatter.17.cloned.1.call-start = ((), (), s32[]{:S(2)}) async-start(), calls=%async_computation.22 | async-start | bytes 2162688 | tf_op jit(solution)/shard_map/reduce_scatter | solution.py:323
  1118.8 675.1 %reduce-scatter.21.cloned.1.call-start = ((), (), s32[]{:S(2)}) async-start(), calls=%async_computation.24 | async-start | bytes 4325376 | tf_op jit(solution)/shard_map/reduce_scatter | solution.py:325
  1122.9 810.4 %reduce-scatter.15.cloned.1.call-start = ((), (), s32[]{:S(2)}) async-start(), calls=%async_computation.21 | async-start | bytes 4325376 | tf_op jit(solution)/shard_map/reduce_scatter | solution.py:322
  1155.8 140.6 %copy-start.41 = (f32[256]{0:T(256)S(1)}, f32[256]{0:T(256)}, u32[]{:S(2)}) copy-start(f32[256]{0:T(256)} %copy-done.40) | copy-start | bytes 3076
  (31 other events, 309.5 us)
Sparse Core Ops, SparseCore 0:
  12.6 19.5 all-gather.8
  34.3 16.7 all-gather.6
  129.0 35.8 all-gather.12
  317.3 35.7 all-gather.10
  354.5 34.4 all-gather.14
  1053.6 24.0 reduce-scatter.12
  1081.0 24.8 reduce-scatter.10
  1108.4 44.4 reduce-scatter.28
  1155.7 44.5 reduce-scatter.26
  1202.6 44.4 reduce-scatter.24
  1250.1 134.0 reduce-scatter.22
  1386.9 132.2 reduce-scatter.18
  1522.1 132.3 reduce-scatter.16
  1657.1 136.7 reduce-scatter.20
  1796.6 136.6 reduce-scatter.14
where the time goes:
time: 1950 us; the launch traced here: 1940 us
  waiting for transfers between devices  1380 us (71%)
  local copies, waits for them, and re-layouts  200 us (10%)
  matrix products  196 us (10%)
  other arithmetic  78.8 us (4%)
  blocking collectives  45.7 us (2%)
  starting transfers between devices  23.4 us (1%)
    all_to_all x1, waiting for transfers between devices, local(): lax.all_to_all(block_layout(rows_back), 'expert', split_axis=0, concat_ax...  173 us
    all_to_all x1, waiting for transfers between devices, local(): lax.all_to_all(placed.reshape(groups, CAP * local_count, width), 'expert'...  168 us
    all_to_all x1, waiting for transfers between devices, local(): lax.all_to_all(outgoing, 'expert', split_axis=0, concat_axis=0, tiled=True)  166 us
    reduce_scatter x1, waiting for transfers between devices, local(): lax.psum_scatter(out_part, ('expert', 'hidden'), scatter_dimension=0, til...  139 us
    reduce_scatter x1, waiting for transfers between devices, local(): lax.psum_scatter(query_part, ('expert', 'hidden'), scatter_dimension=0, t...  139 us
    reduce_scatter x1, waiting for transfers between devices, local(): lax.psum_scatter(key_part, ('expert', 'hidden'), scatter_dimension=0, til...  135 us
    reduce_scatter x1, waiting for transfers between devices, local(): lax.psum_scatter(value_part, ('expert', 'hidden'), scatter_dimension=0, t...  135 us
    all_to_all x1, waiting for transfers between devices, local(): lax.all_to_all(block_layout(result), 'expert', split_axis=0, concat_axis=...  128 us
  transfers between devices with their start and end apart: 19, of which 12 were waited for; matrix products, arithmetic and copies ran while one was open for 14% of the time, Pallas kernels for 0%

commit v1 on v0

v1 whole, which is shorter than its diff:
```python
import functools

import jax
import jax.numpy as jnp
from jax import lax
from jax.experimental import pallas as pl
from jax.experimental.pallas import tpu as pltpu
from jax.sharding import PartitionSpec as P

HEADS = 16
KV_HEADS = 8
HEAD_DIM = 64
EXPERTS = 32
CAP = 128
KV = KV_HEADS * HEAD_DIM
SIDE = 128
TILE = 256
CHUNK = 8

epsilon = 1e-06
rope_base = 10000.0
masked_score = -1e30
bf16 = jnp.bfloat16
f32 = jnp.float32
ANY = pl.BlockSpec(memory_space=pl.ANY)
SMEM = pl.BlockSpec(memory_space=pltpu.SMEM)
VMEM = pl.BlockSpec(memory_space=pltpu.VMEM)
MIB = 1024 * 1024


def dot(a, b, ca, cb):
    return lax.dot_general(a, b, (((ca,), (cb,)), ((), ())), preferred_element_type=f32)


def rms(values):
    return lax.rsqrt(jnp.mean(values * values, axis=-1, keepdims=True) + epsilon)


def norm_back(grad, values, gain):
    q = rms(values)
    w = grad * gain
    back = q * w - values * (q * q * q) * jnp.mean(w * values, axis=-1, keepdims=True)
    return back, grad * values * q


def turn(u, cosine, sine):
    lane = lax.broadcasted_iota(jnp.int32, u.shape, 1)
    half = HEAD_DIM // 2
    partner = jnp.where(
        lane % HEAD_DIM < half, pltpu.roll(u, 2 * HEAD_DIM - half, 1), pltpu.roll(u, half, 1)
    )
    return u * cosine + partner * sine


def struct(shape, dtype=bf16):
    return jax.ShapeDtypeStruct(shape, dtype)


def call(body, outs, ins, scratch=(), smem=0, name=None, mib=40, flops=10**6, nbytes=10**4):
    return pl.pallas_call(
        body,
        out_shape=outs,
        in_specs=[SMEM] * smem + [VMEM] * (len(ins) - smem),
        out_specs=jax.tree.map(lambda _: VMEM, outs),
        scratch_shapes=list(scratch),
        compiler_params=pltpu.CompilerParams(vmem_limit_bytes=mib * MIB),
        cost_estimate=pl.CostEstimate(flops=flops, bytes_accessed=nbytes, transcendentals=0),
        name=name,
    )(*ins)


def route_body(routes, cot, out):
    tokens, width = cot.shape
    lane = lax.broadcasted_iota(jnp.int32, (tokens, 128), 1)
    named = jnp.zeros((tokens, 128), f32)
    for i in range(routes.shape[1]):
        named = named + jnp.where(lane == routes[:, i : i + 1], 1.0, 0.0)
    row = lax.broadcasted_iota(jnp.int32, (tokens, tokens), 0)
    col = lax.broadcasted_iota(jnp.int32, (tokens, tokens), 1)
    earlier = dot(jnp.where(row > col, 1.0, 0.0).astype(bf16), named.astype(bf16), 1, 0)
    code = jnp.where(named > 0.0, jnp.where(earlier < CAP, earlier, -1.0), -2.0)
    out[:tokens, :] = cot[...]
    out[tokens:, :tokens] = code.T[:EXPERTS].astype(bf16)
    out[tokens:, tokens:] = jnp.zeros((EXPERTS, width - tokens), bf16)


def project_kv_body(place, x, gain, wk, wv, spectrum, seg, kv_out, n_out, c_out, s_out):
    tokens = x.shape[0]
    source = x[...].astype(f32)
    normed = (source * rms(source) * gain[...]).astype(bf16)
    n_out[...] = normed
    at = lax.broadcasted_iota(jnp.int32, (tokens, 128), 0) + place[0]
    lane = lax.broadcasted_iota(jnp.int32, (tokens, 128), 1)
    angles = at.astype(f32) * spectrum[...]
    c = jnp.cos(angles)
    s = jnp.sin(angles)
    s = jnp.where(lane % HEAD_DIM < HEAD_DIM // 2, -s, s)
    c_out[...] = c
    s_out[...] = s
    k = dot(normed, wk[...], 1, 0)
    for i in range(0, KV, 128):
        kv_out[:, i : i + 128] = turn(k[:, i : i + 128], c, s).astype(bf16)
    kv_out[:, KV : 2 * KV] = dot(normed, wv[...], 1, 0).astype(bf16)
    kv_out[:, 2 * KV :] = jnp.broadcast_to(seg[...].astype(f32), (SIDE, tokens)).T.astype(bf16)


def project_q_body(normed, wq, c, s, q_out):
    q = dot(normed[...], wq[...], 1, 0)
    for i in range(0, q.shape[1], 128):
        turned = turn(q[:, i : i + 128], c[...], s[...]).astype(bf16)
        q_out[:, i : i + 128] = turned * bf16(HEAD_DIM**-0.5)


def fill_bias(places, kvs, bias):
    tokens = kvs[0].shape[0]
    mine = kvs[0][:, 2 * KV :].astype(f32)[:, :1]
    row = lax.broadcasted_iota(jnp.int32, (tokens, tokens), 0) + places[0]
    col = lax.broadcasted_iota(jnp.int32, (tokens, tokens), 1)
    for b, kv in enumerate(kvs):
        theirs = kv[:, 2 * KV :].astype(f32).T[:1, :]
        keep = (mine == theirs) & (col + places[b] <= row)
        bias[b] = jnp.where(keep, 0.0, masked_score)


def pair_rows(values, j):
    return jnp.concatenate(
        [values[:, 128 * j : 128 * j + HEAD_DIM], values[:, 128 * j + HEAD_DIM : 128 * j + 128]], 0
    )


def pair_columns(values, tokens):
    return jnp.concatenate([values[:tokens], values[tokens:]], 1)


def scores_of(q2, kv, bias, j):
    tokens = kv.shape[0]
    s = dot(q2, kv[:, HEAD_DIM * j : HEAD_DIM * (j + 1)], 1, 1)
    return (s.reshape(2, tokens, tokens) + bias[None]).reshape(2 * tokens, tokens)


def attend_body(
    nb, places, x, q, *refs
):
    kvs, (wo, gain, router, routes, hid_out, ffn_out, att_out, lse_out, gates_out, bias) = (
        refs[:nb],
        refs[nb:],
    )
    tokens = x.shape[0]
    fill_bias(places, kvs, bias)
    lane = lax.broadcasted_iota(jnp.int32, (tokens, 128), 1)
    lse = jnp.zeros((tokens, 128), f32)
    for j in range(KV_HEADS):
        q2 = pair_rows(q, j)
        s = [scores_of(q2, kv, bias[b], j) for b, kv in enumerate(kvs)]
        peak = functools.reduce(
            jnp.maximum, [jnp.max(t, axis=1, keepdims=True) for t in s]
        )
        p = [jnp.exp(t - peak) for t in s]
        total = sum(jnp.sum(t, axis=1, keepdims=True) for t in p)
        o = sum(
            dot(t.astype(bf16), kv[:, KV + HEAD_DIM * j : KV + HEAD_DIM * (j + 1)], 1, 0)
            for t, kv in zip(p, kvs)
        )
        att_out[:, 128 * j : 128 * j + 128] = pair_columns(o / total, tokens).astype(bf16)
        log_total = peak + jnp.log(total)
        lse = jnp.where(lane == 2 * j, log_total[:tokens], lse)
        lse = jnp.where(lane == 2 * j + 1, log_total[tokens:], lse)
    lse_out[...] = lse
    hidden = x[...].astype(f32) + dot(att_out[...], wo[...], 1, 0)
    hid_out[...] = hidden
    ffn = (hidden * rms(hidden) * gain[...]).astype(bf16)
    ffn_out[...] = ffn
    lane = lax.broadcasted_iota(jnp.int32, (tokens, SIDE), 1)
    named = jnp.zeros((tokens, SIDE), f32)
    for i in range(routes.shape[1]):
        named = named + jnp.where(lane == routes[:, i : i + 1], 1.0, 0.0)
    gates_out[...] = gates_of(dot(ffn, router[...], 1, 0), named, 1)


def gates_of(logits, named, axis):
    logits = jnp.where(named > 0.0, logits, masked_score)
    peak = jnp.max(logits, axis=axis, keepdims=True)
    raised = jnp.where(named > 0.0, jnp.exp(logits - peak), 0.0)
    return raised / jnp.sum(raised, axis=axis, keepdims=True)


def hidden_back_body(
    n, *refs
):
    row_sum = sum(r[...].astype(f32) for r in refs[:n])
    (hid, gates, cot, gain, router, wo, hgrad_out, branch_out, lg_out, gp_out, do_out) = refs[n:]
    width = hid.shape[1]
    side = row_sum[:, width:]
    lane = lax.broadcasted_iota(jnp.int32, side.shape, 1)
    slopes = jnp.where(lane < EXPERTS, side + pltpu.roll(side, SIDE - EXPERTS, 1), 0.0)
    g = gates[...]
    logit_grad = (g * (slopes - jnp.sum(g * slopes, axis=1, keepdims=True))).astype(bf16)
    lg_out[...] = logit_grad
    ffn_grad = row_sum[:, :width] + dot(logit_grad, router[...], 1, 1)
    back, share = norm_back(ffn_grad, hid[...], gain[...])
    gp_out[...] = share.astype(bf16)
    hidden_grad = cot[...].astype(f32) + back
    hgrad_out[...] = hidden_grad
    branch = hidden_grad.astype(bf16)
    branch_out[...] = branch
    do_out[...] = dot(branch, wo[...], 1, 1).astype(bf16)


def attention_back_body(nb, places, do_s, q, *refs):
    kvs = refs[:nb]
    (lse, cosine, sine, dq_out) = refs[nb : nb + 4]
    dkv = refs[nb + 4 : 2 * nb + 4]
    bias = refs[2 * nb + 4]
    tokens = q.shape[0]
    fill_bias(places, kvs, bias)
    c, s = cosine[...], sine[...]
    for j in range(KV_HEADS):
        q2 = pair_rows(q, j)
        do2 = pair_rows(do_s, j)
        lse2 = jnp.concatenate([lse[:, 2 * j : 2 * j + 1], lse[:, 2 * j + 1 : 2 * j + 2]], 0)
        p, dp = [], []
        inner = jnp.zeros((2 * tokens, 1), f32)
        for b, kv in enumerate(kvs):
            pb = jnp.exp(scores_of(q2, kv, bias[b], j) - lse2)
            db = dot(do2, kv[:, KV + HEAD_DIM * j : KV + HEAD_DIM * (j + 1)], 1, 1)
            inner = inner + jnp.sum(pb * db, axis=1, keepdims=True)
            p.append(pb)
            dp.append(db)
        dq2 = jnp.zeros((2 * tokens, HEAD_DIM), f32)
        for b, kv in enumerate(kvs):
            ds = (p[b] * (dp[b] - inner)).astype(bf16)
            dq2 = dq2 + dot(ds, kv[:, HEAD_DIM * j : HEAD_DIM * (j + 1)], 1, 0)
            dkv[b][:, HEAD_DIM * j : HEAD_DIM * (j + 1)] = dot(ds, q2, 0, 0).astype(bf16)
            dkv[b][:, KV + HEAD_DIM * j : KV + HEAD_DIM * (j + 1)] = dot(
                p[b].astype(bf16), do2, 0, 0
            ).astype(bf16)
        dq = pair_columns(dq2, tokens) * HEAD_DIM**-0.5
        dq_out[:, 128 * j : 128 * j + 128] = turn(dq, c, -s).astype(bf16)


def finish_body(
    ka, kb, dq, wq, wk, wv, hgrad, x, gain, cosine, sine, in_out, dkv_out, gp_out
):
    total = ka[...].astype(f32) + kb[...].astype(f32)
    c, s = cosine[...], sine[...]
    for at in range(0, KV, 128):
        dkv_out[:, at : at + 128] = turn(total[:, at : at + 128], c, -s).astype(bf16)
    dkv_out[:, KV:] = total[:, KV:].astype(bf16)
    grad = dot(dq[...], wq[...], 1, 1)
    grad = grad + dot(dkv_out[:, :KV], wk[...], 1, 1) + dot(dkv_out[:, KV:], wv[...], 1, 1)
    back, share = norm_back(grad, x[...].astype(f32), gain[...])
    gp_out[...] = share.astype(bf16)
    in_out[...] = (hgrad[...] + back).astype(bf16)


def weight_body(groups, parts, n_side, me, left, right, *refs):
    sides, (near, far, held) = refs[: 2 * n_side], refs[2 * n_side :]
    width = right.shape[1]

    def put(values, lo, hi):
        v = values.reshape(groups, parts, -1, hi - lo)
        for h in range(parts):
            held[h, :, :, lo:hi] = v[:, h].astype(bf16)

    for at in range(0, width, 512):
        put(dot(left[...], right[:, at : at + 512], 0, 0), at, at + 512)
    if n_side:
        put(
            sum(dot(sides[2 * i][...], sides[2 * i + 1][...], 0, 0) for i in range(n_side)),
            width,
            width + SIDE,
        )
    for m in range(parts):
        (far if m % 2 else near)[m // 2] = held[me[0] ^ m]


def expert_body(blocks, tokens, base, *refs):
    xs, cs = refs[:blocks], refs[blocks : 2 * blocks]
    router, wg_ref, wu_ref, wd_ref = refs[2 * blocks : 2 * blocks + 4]
    refs = refs[2 * blocks + 4 :]
    rows_out = refs[:blocks]
    acts_out, x_out, pg_out, so_out, slots_out, offs_out = refs[blocks : blocks + 6]
    (x_s, c_s, g_t, s_t, xg, cg, so, acts, gs, rg, stage, ob, offs, last, sems, tile_sems) = refs[
        blocks + 6 :
    ]
    e = pl.program_id(0)
    count = pl.num_programs(0)
    width = x_s.shape[2]
    hid = acts.shape[1] // 3
    slot_iota = lax.broadcasted_iota(jnp.int32, (CAP, tokens), 0).astype(f32)
    expert = base[0] + e

    def loads(b):
        return (
            pltpu.make_async_copy(xs[b], x_s.at[b], sems.at[b]),
            pltpu.make_async_copy(cs[b], c_s.at[b], sems.at[blocks + b]),
        )

    def tile_copies(i, at):
        rows = pl.ds(pl.multiple_of(i * TILE, TILE), TILE)
        pairs = ((acts, acts_out), (xg, x_out), (cg, pg_out), (so, so_out))
        return [
            pltpu.make_async_copy(a.at[rows, :], o.at[at, rows, :], tile_sems.at[n, i])
            for n, (a, o) in enumerate(pairs)
        ]

    def wait_tiles(at):
        def wait_one(i, carry):
            for copy in tile_copies(i, at):
                copy.wait()
            return carry

        lax.fori_loop(0, last[0], wait_one, 0)

    @pl.when(e == 0)
    def _():
        for b in range(blocks):
            for load in loads(b):
                load.start()

    @pl.when(e > 0)
    def _():
        wait_tiles(e - 1)

    off = jnp.int32(0)
    for b in range(blocks):

        @pl.when(e == 0)
        def _(b=b):
            for load in loads(b):
                load.wait()
            code = c_s[b, tokens:, :tokens].astype(f32)
            s_t[b] = code
            g_t[b] = gates_of(
                dot(router[...], x_s[b], 1, 1), jnp.where(code > -1.5, 1.0, 0.0), 0
            )

        off = pl.multiple_of(off, 16)
        rows = pl.ds(off, CAP)
        mine = pl.ds(expert, 1)
        slots, gates = s_t[b, mine, :], g_t[b, mine, :]
        slots_out[0, b] = slots
        hit = slot_iota == slots
        pick = jnp.where(hit, 1.0, 0.0).astype(bf16)
        xg[rows, :] = dot(pick, x_s[b], 1, 0).astype(bf16)
        cg[rows, :] = dot(pick, c_s[b, :tokens, :], 1, 0).astype(bf16)
        gate = jnp.sum(jnp.where(hit, gates, 0.0), axis=1, keepdims=True)
        gs[rows, :] = jnp.broadcast_to(gate, (CAP, 128))
        kept = jnp.sum(jnp.where(slots > -0.5, 1, 0))
        offs[e, b] = off
        offs_out[e, b] = off
        off = off + (kept + 15) // 16 * 16
    offs_out[e, blocks] = off
    tail = pl.ds(pl.multiple_of(off, 16), TILE)
    xg[tail, :] = jnp.zeros((TILE, width), bf16)
    cg[tail, :] = jnp.zeros((TILE, width), bf16)
    gs[tail, :] = jnp.zeros((TILE, 128), f32)
    lane = lax.broadcasted_iota(jnp.int32, (TILE, SIDE), 1)

    def step(i, carry):
        rows = pl.ds(pl.multiple_of(i * TILE, TILE), TILE)
        w_gate = wg_ref[...].reshape(hid, width)
        w_up = wu_ref[...].reshape(hid, width)
        w_down = wd_ref[...].reshape(hid, width)
        x = xg[rows, :]
        c = cg[rows, :].astype(f32)
        gate = gs[rows, :][:, :1]
        gate_value = dot(x, w_gate, 1, 1)
        up_value = dot(x, w_up, 1, 1)
        sig = 1.0 / (1.0 + jnp.exp(-gate_value))
        silu = gate_value * sig
        active = (silu * up_value).astype(bf16)
        acts[rows, 2 * hid :] = active
        result = dot(active, w_down, 1, 0).astype(bf16).astype(f32)
        slope = jnp.sum(result * c, axis=1, keepdims=True)
        high = slope.astype(bf16).astype(f32)
        low = slope - high
        so[rows, :] = (gate * result).astype(bf16)
        pair_grad = (gate * c).astype(bf16)
        cg[rows, :] = pair_grad
        active_grad = dot(pair_grad, w_down, 1, 1)
        gate_back = (active_grad * up_value * (sig * (1.0 + gate_value * (1.0 - sig)))).astype(bf16)
        up_back = (active_grad * silu).astype(bf16)
        acts[rows, :hid] = gate_back
        acts[rows, hid : 2 * hid] = up_back
        for copy in tile_copies(i, e):
            copy.start()
        rg[e, rows, width:] = jnp.where(
            lane == expert, high, jnp.where(lane == expert + EXPERTS, low, 0.0)
        ).astype(bf16)
        rg[e, rows, :width] = (dot(gate_back, w_gate, 1, 0) + dot(up_back, w_up, 1, 0)).astype(bf16)
        return carry

    steps = pl.cdiv(off, TILE)
    lax.fori_loop(0, steps, step, 0)
    last[0] = steps
    rg[e, pl.ds(pl.multiple_of(steps * TILE, TILE), CAP), :] = jnp.zeros((CAP, width + SIDE), bf16)

    @pl.when(e == count - 1)
    def _():
        local_count = rg.shape[0]
        stores = []
        for b in range(blocks):
            picks = []
            for k in range(local_count):
                stage[b % 2, k * CAP : (k + 1) * CAP, :] = rg[
                    k, pl.ds(pl.multiple_of(offs[k, b], 16), CAP), :
                ]
                hit = slot_iota == s_t[b, pl.ds(base[0] + k, 1), :]
                picks.append(jnp.where(hit, 1.0, 0.0).astype(bf16))
            ob[b] = dot(jnp.concatenate(picks, 0), stage[b % 2], 0, 0).astype(bf16)
            stores.append(pltpu.make_async_copy(ob.at[b], rows_out[b], sems.at[b]))
            stores[b].start()
        wait_tiles(e)
        for store in stores:
            store.wait()


def expert_grad_body(first, offs, acts, xg, pg, out):
    e = pl.program_id(0) + first
    blocks = offs.shape[1] - 1
    steps = pl.cdiv(offs[e, blocks], TILE)
    parts, _, _, part, width = out.shape
    hid = parts * part

    @pl.when(steps == 0)
    def _():
        out[...] = jnp.zeros_like(out)

    for n in range(1, xg.shape[1] // TILE + 1):

        @pl.when(steps == n)
        def _(n=n):
            for i, right in enumerate((xg, xg, pg)):
                for h in range(parts):
                    at = i * hid + h * part
                    out[h, 0, i] = dot(
                        acts[0, : n * TILE, at : at + part], right[0, : n * TILE, :], 0, 0
                    ).astype(bf16)


def expert_sum_body(blocks, tokens, offs, so, slots, *refs):
    outs, stage = refs[:blocks], refs[blocks]
    local_count, width = so.shape[0], so.shape[2]
    slot_iota = lax.broadcasted_iota(jnp.int32, (CAP, tokens), 0).astype(f32)
    place = lax.broadcasted_iota(jnp.int32, (CAP, width), 0)
    for b in range(blocks):
        picks = []
        for k in range(local_count):
            off = pl.multiple_of(offs[k, b], 16)
            values = so[k, pl.ds(off, CAP), :]
            stage[b % 2, k * CAP : (k + 1) * CAP, :] = jnp.where(
                place < offs[k, blocks] - off, values.astype(f32), 0.0
            ).astype(bf16)
            picks.append(jnp.where(slot_iota == slots[k, b], 1.0, 0.0).astype(bf16))
        outs[b][...] = dot(jnp.concatenate(picks, 0), stage[b % 2], 0, 0).astype(bf16)


def expert_call(base, rows, grads, router, weights):
    hidden_parts, matrices, part, width = weights.shape
    local_count = matrices // 3
    blocks, tokens = len(rows), rows[0].shape[0]
    hid = hidden_parts * part
    most = blocks * CAP
    room = most + TILE

    def weight_spec(m):
        return pl.BlockSpec(
            (hidden_parts, 1, part, width), lambda e: (0, m * local_count + e, 0, 0)
        )

    got = pl.pallas_call(
        functools.partial(expert_body, blocks, tokens),
        grid=(local_count,),
        out_shape=[struct((tokens, width + SIDE))] * blocks
        + [
            struct((local_count, room, 3 * hid)),
            struct((local_count, room, width)),
            struct((local_count, room, width)),
            struct((local_count, room, width)),
            struct((local_count, blocks, 1, tokens), f32),
            struct((local_count, blocks + 1), jnp.int32),
        ],
        in_specs=[SMEM] + [ANY] * (2 * blocks) + [VMEM] + [weight_spec(m) for m in range(3)],
        out_specs=[ANY] * (blocks + 4)
        + [pl.BlockSpec((1, blocks, 1, tokens), lambda e: (e, 0, 0, 0)), SMEM],
        scratch_shapes=[
            pltpu.VMEM((blocks, tokens, width), bf16),
            pltpu.VMEM((blocks, tokens + EXPERTS, width), bf16),
            pltpu.VMEM((blocks, EXPERTS, tokens), f32),
            pltpu.VMEM((blocks, EXPERTS, tokens), f32),
            pltpu.VMEM((room, width), bf16),
            pltpu.VMEM((room, width), bf16),
            pltpu.VMEM((room, width), bf16),
            pltpu.VMEM((room, 3 * hid), bf16),
            pltpu.VMEM((room, 128), f32),
            pltpu.VMEM((local_count, room, width + SIDE), bf16),
            pltpu.VMEM((2, local_count * CAP, width + SIDE), bf16),
            pltpu.VMEM((blocks, tokens, width + SIDE), bf16),
            pltpu.SMEM((local_count, blocks), jnp.int32),
            pltpu.SMEM((1,), jnp.int32),
            pltpu.SemaphoreType.DMA((2 * blocks,)),
            pltpu.SemaphoreType.DMA((4, room // TILE)),
        ],
        compiler_params=pltpu.CompilerParams(vmem_limit_bytes=58 * MIB),
        cost_estimate=pl.CostEstimate(
            flops=10**6, bytes_accessed=10**4, transcendentals=0
        ),
        name="experts",
    )(base, *rows, *grads, router, weights, weights, weights)
    rows_back, (acts, xg, pg, so, slots, offs) = got[:blocks], got[blocks:]

    def grads_of(first, number, acts):
        return pl.pallas_call(
            functools.partial(expert_grad_body, first),
            grid=(number,),
            out_shape=struct((hidden_parts, number, 3, part, width)),
            in_specs=[SMEM]
            + [
                pl.BlockSpec((1, most, n), lambda e: (e + first, 0, 0))
                for n in (3 * hid, width, width)
            ],
            out_specs=pl.BlockSpec((hidden_parts, 1, 3, part, width), lambda e: (0, e, 0, 0, 0)),
            compiler_params=pltpu.CompilerParams(vmem_limit_bytes=48 * MIB),
            cost_estimate=pl.CostEstimate(flops=10**6, bytes_accessed=10**4, transcendentals=0),
            name="expert_grads",
        )(offs, acts, xg, pg)

    def outs_of(so):
        return call(
            functools.partial(expert_sum_body, blocks, tokens),
            [struct((tokens, width))] * blocks,
            (offs, so, slots),
            scratch=[pltpu.VMEM((2, local_count * CAP, width), bf16)],
            smem=1,
            name="expert_sum",
            flops=10**6,
            nbytes=10**4,
        )

    return rows_back, acts, so, grads_of, outs_of


def after(values, first):
    return lax.optimization_barrier((values, first))


def flip(values, axis, bit):
    n = lax.axis_size(axis)
    return lax.ppermute(values, axis, [(i, i ^ bit) for i in range(n)])


def gather_hidden(block):
    blocks, marks = [block], [0]
    bit = lax.axis_size("hidden") // 2
    while bit:
        blocks, marks = blocks + [flip(b, "hidden", bit) for b in blocks], marks + [m ^ bit for m in marks]
        bit //= 2
    return blocks, marks


def sum_hidden(keep):
    bit = 1
    n = lax.axis_size("hidden")
    while bit < n:
        far = {m: flip(keep[m], "hidden", bit) for m in keep if m & bit}
        near = {m: keep[m] for m in keep if not m & bit}
        if 2 * bit == n:
            return near[0], far[bit]
        keep = {m: (near[m].astype(f32) + far[m ^ bit].astype(f32)).astype(bf16) for m in near}
        bit *= 2


def shift(values, by):
    n = lax.axis_size("expert")
    return lax.ppermute(values, "expert", [(i, (i + 2 * by) % n) for i in range(n)])


def gather_expert(block, before=()):
    n = lax.axis_size("expert")
    if n != 8:
        whole = lax.all_gather(block, "expert", axis=0, tiled=False)
        return [whole[i] for i in range(n)], before
    side = flip(block, "expert", 1)
    up = shift(block, 1)
    down = shift(block, -1)
    up_after, (side, *before) = after(up, [side, *before])
    far = shift(up_after, 1)
    line = [up, far, down]
    return [block] + line + [side] + [flip(b, "expert", 1) for b in line], before


def take_add(near, got, first):
    n, rest = near.shape[0] // 2, near.shape[1:]
    spec = pl.BlockSpec((1,) + rest, lambda i: (2 * i + first,) + (0,) * len(rest))
    return pl.pallas_call(
        add_body,
        grid=(n,),
        out_shape=struct((n,) + rest),
        in_specs=[spec, spec],
        out_specs=pl.BlockSpec((1,) + rest, lambda i: (i,) + (0,) * len(rest)),
        compiler_params=pltpu.CompilerParams(vmem_limit_bytes=40 * MIB),
        cost_estimate=pl.CostEstimate(flops=10**6, bytes_accessed=10**4, transcendentals=0),
        name="take_add",
    )(near, got)


def sum_parts(near, far):
    return sum_parts_end(near, *sum_parts_begin(near, flip(far, "hidden", 1)))


def sum_parts_begin(near, got):
    return got, (take_add(near, got, 1) if got.shape[0] > 1 else None)


def sum_parts_end(near, got, far):
    bit = 2
    left = [near]
    while got.shape[0] > 1:
        if got.shape[0] > 2:
            near = take_add(near, got, 0)
            left = [near]
        else:
            left = [near[0], got[0]]
        got = flip(far, "hidden", bit)
        bit *= 2
        if got.shape[0] > 1:
            far = take_add(near, got, 1)
    return left, got[0]


def add_body(a, b, out):
    out[...] = (a[...].astype(f32) + b[...].astype(f32)).astype(bf16)


def add(a, b):
    return call(add_body, struct(a.shape), (a, b), name="add")


def sum_expert(parts):
    n = lax.axis_size("expert")
    if n != 8:
        return [
            lax.psum_scatter(jnp.concatenate(parts, 0), "expert", scatter_dimension=0, tiled=True)
        ]
    line = [None] * 4
    for k in (2, 1, 3, 0):
        line[k] = add(parts[k], flip(parts[4 + k], "expert", 1))
    near = add(line[1], shift(line[2], -1))
    return [line[0], shift(near, -1), shift(line[3], 1)]


def sum_expert_beside(parts, begin, works):
    flip_2 = flip(parts[6], "expert", 1)
    held = begin()
    flip_2, held = after(flip_2, held)
    far = add(parts[2], flip_2)

    far, held = works[0](far, held)
    side, _ = after(parts[5], flip_2)
    flip_1 = flip(side, "expert", 1)
    turn_1 = shift(far, -1)
    (flip_1, turn_1), held = after([flip_1, turn_1], held)
    near = add(add(parts[1], flip_1), turn_1)

    near, held = works[1](near, held)
    side, _ = after(parts[7], [flip_1, turn_1])
    flip_3 = flip(side, "expert", 1)
    result_a = shift(near, -1)
    (flip_3, result_a), held = after([flip_3, result_a], held)
    line_3 = add(parts[3], flip_3)

    line_3, held = works[2](line_3, held)
    side, _ = after(parts[4], [flip_3, result_a])
    flip_0 = flip(side, "expert", 1)
    result_b = shift(line_3, 1)
    (flip_0, result_b), held = after([flip_0, result_b], held)
    return [add(parts[0], flip_0), result_a, result_b], held


def local(
    inputs,
    first_gain,
    query_weight,
    key_weight,
    value_weight,
    out_weight,
    second_gain,
    router_weight,
    gate_weight,
    up_weight,
    down_weight,
    routes,
    segments,
    cotangent,
):
    tokens, width = inputs.shape
    hidden_index = lax.axis_index("hidden")
    expert_index = lax.axis_index("expert")
    groups = lax.axis_size("expert")
    hidden_parts = lax.axis_size("hidden")
    local_count = gate_weight.shape[0]
    gain_one, gain_two = first_gain[None, :], second_gain[None, :]
    router = jnp.pad(router_weight, ((0, 0), (0, SIDE - EXPERTS)))
    spectrum = rope_base ** (-jnp.arange(HEAD_DIM // 2, dtype=f32) * 2.0 / HEAD_DIM)
    me = hidden_index.astype(jnp.int32).reshape(1)

    grad_rows = call(
        route_body,
        struct((tokens + EXPERTS, width)),
        (routes, cotangent),
        name="route",
        flops=10**6,
        nbytes=10**4,
    )
    grads, _ = gather_expert(grad_rows)
    kv, normed, cosine, sine = call(
        project_kv_body,
        (
            struct((tokens, 2 * KV + SIDE)),
            struct((tokens, width)),
            struct((tokens, 128), f32),
            struct((tokens, 128), f32),
        ),
        (
            me * tokens,
            inputs,
            gain_one,
            key_weight,
            value_weight,
            jnp.tile(spectrum, 4)[None, :],
            segments[None, :],
        ),
        smem=1,
        name="project_kv",
        flops=10**6,
        nbytes=10**4,
    )
    q = call(
        project_q_body,
        struct((tokens, width)),
        (normed, query_weight, cosine, sine),
        name="project_q",
        flops=10**6,
        nbytes=10**4,
    )
    kvs, marks = gather_hidden(kv)
    nb = len(kvs)
    weights = jnp.concatenate([gate_weight, up_weight, down_weight], axis=0)
    weights, (kvs[1], grads[1], grads[4]) = after(weights, [kvs[1], grads[1], grads[4]])
    weights_all = lax.all_gather(weights, "hidden", axis=0, tiled=False)
    places = jnp.stack([(hidden_index ^ m) * tokens for m in marks]).astype(jnp.int32)
    hidden, ffn, att, lse, gates = call(
        functools.partial(attend_body, nb),
        (
            struct((tokens, width), f32),
            struct((tokens, width)),
            struct((tokens, width)),
            struct((tokens, 128), f32),
            struct((tokens, SIDE), f32),
        ),
        (places, inputs, q, *kvs, out_weight, gain_two, router, routes),
        scratch=[pltpu.VMEM((nb, tokens, tokens), f32)],
        smem=1,
        name="attend",
        flops=10**6,
        nbytes=10**4,
    )
    if groups == 8:
        first = [1, 2, 3, 4, 5, 7]
        ffn_out, held = after(ffn, [grads[i] for i in first])
        for i, g in zip(first, held):
            grads[i] = g
        rows, (grads[6],) = gather_expert(ffn_out, (grads[6],))
    else:
        rows, _ = gather_expert(ffn)

    first_expert = (expert_index * local_count).astype(jnp.int32)
    rows_back, todo = [], []
    chunk = min(CHUNK, groups)
    router_rows = router_weight.T
    for i in range(0, groups, chunk):
        r, *rest = expert_call(
            first_expert.reshape(1),
            rows[i : i + chunk],
            grads[i : i + chunk],
            router_rows,
            weights_all,
        )
        rows_back += r
        todo.append(rest)
    half_count = (local_count + 1) // 2

    def weight_grads(first, number, held):
        parts = [grads_of(first, number, a) for (_, _, grads_of, _), a in zip(todo, held)]
        return parts[0] if len(parts) == 1 else sum(p.astype(f32) for p in parts).astype(bf16)

    def matrix_sum(part):
        return lax.psum_scatter(part, "hidden", scatter_dimension=0, tiled=False)

    def token_sums(held):
        return [o for (_, _, _, outs_of), so in zip(todo, held) for o in outs_of(so)]

    all_acts, all_so = [t[0] for t in todo], [t[1] for t in todo]
    rest_count = local_count - half_count
    if groups == 8 and rest_count:

        def begin():
            return weight_grads(0, half_count, all_acts)

        def work_2(values, held):
            dw_halves.append(matrix_sum(held))
            values, acts = after(values, all_acts)
            return values, weight_grads(half_count, rest_count, acts)

        def work_3(values, held):
            dw_halves.append(matrix_sum(held))
            values, so = after(values, all_so)
            return values, token_sums(so)

        dw_halves = []
        row_parts, outs = sum_expert_beside(
            rows_back, begin, (work_2, work_3, lambda values, held: (values, held))
        )
        row_parts[0], outs = after(row_parts[0], outs)
    else:
        row_parts = sum_expert(rows_back)
        dw_halves = [matrix_sum(weight_grads(0, local_count, all_acts))]
        outs = token_sums(all_so)

    hidden_grad, branch, logit_grad, gain_share, out_grad = call(
        functools.partial(hidden_back_body, len(row_parts)),
        (
            struct((tokens, width), f32),
            struct((tokens, width)),
            struct((tokens, SIDE)),
            struct((tokens, width)),
            struct((tokens, width)),
        ),
        (*row_parts, hidden, gates, cotangent, gain_two, router, out_weight),
        name="hidden_back",
    )

    def weight_parts(left, right, sides=()):
        n = right.shape[1] + (SIDE if sides else 0)
        rows_each = width // groups // hidden_parts
        shape = (hidden_parts // 2, groups, rows_each, n)
        return call(
            functools.partial(weight_body, groups, hidden_parts, len(sides)),
            (struct(shape), struct(shape)),
            (me, left, right, *[v for pair in sides for v in pair]),
            scratch=[pltpu.VMEM((hidden_parts, groups, rows_each, n), bf16)],
            smem=1,
            name="weight_grad",
        )

    def sum_over_mesh(near, got, far):
        left, got = sum_parts_end(near, got, far)
        half = sum([v.astype(f32) for v in left], got.astype(f32)).astype(bf16)
        got = lax.all_to_all(half, "expert", split_axis=0, concat_axis=0, tiled=True)
        return jnp.sum(got.astype(f32), axis=0)

    def across(near, far):
        return (near, *sum_parts_begin(near, flip(far, "hidden", 1)))

    spot = jnp.broadcast_to(
        (jnp.arange(SIDE, dtype=jnp.int32) == EXPERTS).astype(bf16)[None, :], (tokens, SIDE)
    )
    first_parts = weight_parts(att, branch, ((ffn, logit_grad), (gain_share, spot)))
    first_parts = across(*first_parts)
    out_grad, first_parts = after(out_grad, first_parts)
    first_sums = sum_over_mesh(*first_parts)
    dq, *dkvs = call(
        functools.partial(attention_back_body, nb),
        [struct((tokens, width))] + [struct((tokens, 2 * KV))] * nb,
        (places, out_grad, q, *kvs, lse, cosine, sine),
        scratch=[pltpu.VMEM((nb, tokens, tokens), f32)],
        smem=1,
        name="attention_back",
    )
    ka, kb = sum_hidden(dict(zip(marks, dkvs)))
    dw_sum = jnp.concatenate(dw_halves, 0).astype(f32)
    query_near, query_got, query_far = across(*weight_parts(normed, dq))
    query_far, kb = after(query_far, kb)
    query_sum = sum_over_mesh(query_near, query_got, query_far)
    input_grad, dkv, gain_share_one = call(
        finish_body,
        (struct((tokens, width)), struct((tokens, 2 * KV)), struct((tokens, width))),
        (
            ka,
            kb,
            dq,
            query_weight,
            key_weight,
            value_weight,
            hidden_grad,
            inputs,
            gain_one,
            cosine,
            sine,
        ),
        name="finish",
        flops=10**6,
        nbytes=10**4,
    )
    last_sums = sum_over_mesh(*across(*weight_parts(normed, dkv, ((gain_share_one, spot),))))
    moe = sum_expert(outs)
    block_out = (hidden + sum(m.astype(f32) for m in moe)).astype(bf16)
    return (
        block_out,
        input_grad,
        last_sums[:, 2 * KV + EXPERTS],
        query_sum,
        last_sums[:, :KV],
        last_sums[:, KV : 2 * KV],
        first_sums[:, :width],
        first_sums[:, width + EXPERTS],
        first_sums[:, width : width + EXPERTS],
        dw_sum[:, 0],
        dw_sum[:, 1],
        dw_sum[:, 2],
    )


def solution(mesh):
    tokens = P(("expert", "hidden"), None)
    flat = P(("expert", "hidden"))
    units = P("expert", "hidden", None)
    in_specs = (tokens,) + (P(),) * 7 + (units,) * 3 + (tokens, flat, tokens)
    out_specs = (tokens, tokens, flat) + (tokens,) * 4 + (flat, tokens) + (units,) * 3
    return jax.shard_map(local, mesh=mesh, in_specs=in_specs, out_specs=out_specs, check_vma=False)
```

time: 1950 us -> 430 us (0.22)
  waiting for transfers between devices: 1380 us -> 177 us
  matrix products: 196 us -> 0 us
  local copies, waits for them, and re-layouts: 200 us -> 23.2 us
  Pallas kernels: 0 us -> 128 us
  other arithmetic: 78.8 us -> 15.2 us
  starting transfers between devices: 23.4 us -> 71.8 us
  blocking collectives: 45.7 us -> 0 us
    reduce_scatter x10 -> x2, waiting for transfers between devices: 745 us -> 0.01 us  [matrix_sum(): return lax.psum_scatter(part, 'hidden', scatter_dimension=0, tiled=False)]
    all_to_all x4 -> x3, waiting for transfers between devices: 634 us -> 5.01 us  [sum_over_mesh(): lax.all_to_all(half, 'expert', split_axis=0, concat_axis=0, tiled=True)]
    dot_general x30 -> x0, matrix products: 196 us -> none  [the longest x1 20.5 us: expert_backward(): jnp.einsum('rjd,jfd->rjf', incoming, full_down, preferred_element_type=jn...]
    ppermute x0 -> x40, waiting for transfers between devices: none -> 171 us  [the longest x28 97 us: flip(): return lax.ppermute(values, axis, [(i, i ^ bit) for i in range(n)])]
    pallas_call x0 -> x27, Pallas kernels: none -> 128 us  [the longest x21 61.6 us: call(): pl.pallas_call(body, out_shape=outs, in_specs=[SMEM] * smem + [VMEM] * (l...]
    gather x11 -> x0, local copies, waits for them, and re-layouts: 80.2 us -> none  [the longest x2 30.9 us: pick_rows(): return jnp.take(flat_rows, target, axis=0)]
    ppermute x0 -> x40, starting transfers between devices: none -> 59.5 us  [the longest x28 33 us: flip(): return lax.ppermute(values, axis, [(i, i ^ bit) for i in range(n)])]
    reshape x6 -> x0, local copies, waits for them, and re-layouts: 51.7 us -> none  [the longest x2 26.4 us: row_layout(): return arrived_block.reshape(groups * CAP, local_count, width)]
  transfers between devices with their start and end apart: 19 -> 46, of which waited for: 12 -> 20; matrix products, arithmetic and copies ran while one was open for 14% -> 4% of each run, Pallas kernels for 0% -> 19%
where the time goes in v1:
time: 430 us
  waiting for transfers between devices  177 us (41%)
  Pallas kernels  128 us (30%)
  starting transfers between devices  71.8 us (17%)
  local copies, waits for them, and re-layouts  23.2 us (5%)
  other arithmetic  15.2 us (4%)
  between operations  14.8 us (3%)
    ppermute x28, waiting for transfers between devices, flip(): return lax.ppermute(values, axis, [(i, i ^ bit) for i in range(n)])  97 us
    ppermute x12, waiting for transfers between devices, shift(): lax.ppermute(values, 'expert', [(i, (i + 2 * by) % n) for i in range(n)])  74.4 us
    pallas_call x21, Pallas kernels, call(): pl.pallas_call(body, out_shape=outs, in_specs=[SMEM] * smem + [VMEM] * (l...  61.6 us
    pallas_call x1, Pallas kernels, expert_call(): pl.pallas_call(functools.partial(expert_body, blocks, tokens), grid=(loca...  45.3 us
    ppermute x28, starting transfers between devices, flip(): return lax.ppermute(values, axis, [(i, i ^ bit) for i in range(n)])  33 us
    ppermute x12, starting transfers between devices, shift(): lax.ppermute(values, 'expert', [(i, (i + 2 * by) % n) for i in range(n)])  26.4 us
    pallas_call x2, Pallas kernels, grads_of(): pl.pallas_call(functools.partial(expert_grad_body, first), grid=(number,)...  20.9 us
    unnamed x138, local copies, waits for them, and re-layouts  15.8 us
  transfers between devices with their start and end apart: 46, of which 20 were waited for; matrix products, arithmetic and copies ran while one was open for 4% of the time, Pallas kernels for 19%

profile of v1, /device:TPU:0, one launch (start us, length us, event | category | flops | bytes accessed | tf_op | source)
XLA Modules:
  0.0 429.6 jit_solution(7492430850407476403)
XLA Ops:
  9.8 3.1 collective-permute-start.1
  21.7 2.9 pad_maximum_fusion
  24.5 3.8 collective-permute-done.1.refs_9_
  28.3 6.6 %collective-permute-done.refs_1_ = bf16[256,1152]{1,0:T(8,128)(2,1)} collective-permute-done((bf16[256,1152]{1,0:T(8,128)(2,1)}, bf16[256,1152]{1,0:T(8,128)(2,1)}, u32[]{:S(2)}, u32[]{:S(2)}) %collective-permute-start) | collective-permute-done | bytes 589856 | tf_op jit(solution)/shard_map/ppermute | solution.py:550
  39.1 12.2 %collective-permute-done.6.refs_11_ = bf16[288,1024]{1,0:T(8,128)(2,1)} collective-permute-done((bf16[288,1024]{1,0:T(8,128)(2,1)S(1)}, bf16[288,1024]{1,0:T(8,128)(2,1)}, u32[]{:S(2)}, u32[]{:S(2)}) %collective-permute-start.6) | collective-permute-done | bytes 589856 | tf_op jit(solution)/shard_map/ppermute | solution.py:576
  55.7 7.8 %collective-permute-done.5.refs_10_ = bf16[288,1024]{1,0:T(8,128)(2,1)} collective-permute-done((bf16[288,1024]{1,0:T(8,128)(2,1)}, bf16[288,1024]{1,0:T(8,128)(2,1)}, u32[]{:S(2)}, u32[]{:S(2)}) %collective-permute-start.5) | collective-permute-done | bytes 589856 | tf_op jit(solution)/shard_map/ppermute | solution.py:576
  64.1 14.2 %attend.1 = (f32[256,1024]{1,0:T(8,128)S(1)}, bf16[256,1024]{1,0:T(8,128)(2,1)S(1)}, bf16[256,1024]{1,0:T(8,128)(2,1)S(1)}, f32[256,128]{1,0:T(8,128)S(1)}, f32[256,128]{1,0:T(8,128)S(1)}) custom-call(s32[4]{0:T(128)S(1)} %pad_add_fusion.places, bf16[256,1024]{1,0:T(8,128)(2,1)S(1)} %copy-done.4, bf16[256,1024]{1,0:T(8,128)(2,1)S(1)} %project_q.1.q, ...), custom_call_target="tpu_custom_call" | custom-call | flops 1000000 | bytes 10000 | tf_op jit(solution)/shard_map/attend/pallas_call | solution.py:60
  83.5 3.4 collective-permute-start.13
  86.8 11.4 %collective-permute-done.9.refs_1_ = bf16[256,1024]{1,0:T(8,128)(2,1)} collective-permute-done((bf16[256,1024]{1,0:T(8,128)(2,1)S(1)}, bf16[256,1024]{1,0:T(8,128)(2,1)}, u32[]{:S(2)}, u32[]{:S(2)}) %collective-permute-start.9) | collective-permute-done | bytes 524320 | tf_op jit(solution)/shard_map/ppermute | solution.py:576
  98.3 6.9 %collective-permute-start.12 = (bf16[256,1024]{1,0:T(8,128)(2,1)}, bf16[256,1024]{1,0:T(8,128)(2,1)}, u32[]{:S(2)}, u32[]{:S(2)}) collective-permute-start(bf16[256,1024]{1,0:T(8,128)(2,1)} %collective-permute-done.9.refs_1_), channel_id=1, source_target_pairs={{0,8},{4,12},{8,16},{12,20},{16,24},{20,28},{24,0},{28,4},{1,9},{5... | collective-permute-start | bytes 1572872 | tf_op jit(solution)/shard_map/ppermute | solution.py:576
  110.0 8.2 %collective-permute-done.12.refs_2_ = bf16[256,1024]{1,0:T(8,128)(2,1)} collective-permute-done((bf16[256,1024]{1,0:T(8,128)(2,1)}, bf16[256,1024]{1,0:T(8,128)(2,1)}, u32[]{:S(2)}, u32[]{:S(2)}) %collective-permute-start.12) | collective-permute-done | bytes 524320 | tf_op jit(solution)/shard_map/ppermute | solution.py:576
  119.6 9.8 %collective-permute-done.16.refs_7_ = bf16[256,1024]{1,0:T(8,128)(2,1)} collective-permute-done((bf16[256,1024]{1,0:T(8,128)(2,1)}, bf16[256,1024]{1,0:T(8,128)(2,1)}, u32[]{:S(2)}, u32[]{:S(2)}) %collective-permute-start.16) | collective-permute-done | bytes 524320 | tf_op jit(solution)/shard_map/ppermute | solution.py:550
  129.4 7.8 %collective-permute-done.15.refs_6_ = bf16[256,1024]{1,0:T(8,128)(2,1)} collective-permute-done((bf16[256,1024]{1,0:T(8,128)(2,1)}, bf16[256,1024]{1,0:T(8,128)(2,1)}, u32[]{:S(2)}, u32[]{:S(2)}) %collective-permute-start.15) | collective-permute-done | bytes 524320 | tf_op jit(solution)/shard_map/ppermute | solution.py:550
  137.2 45.3 %experts.1 = (bf16[256,1152]{1,0:T(8,128)(2,1)}, bf16[256,1152]{1,0:T(8,128)(2,1)}, bf16[256,1152]{1,0:T(8,128)(2,1)}, bf16[256,1152]{1,0:T(8,128)(2,1)}, bf16[2...) custom-call(s32[1]{0:T(128)} %bitcast.8.base, ...), custom_call_target="tpu_custom_call" | custom-call | flops 1000000 | bytes 10000 | tf_op jit(solution)/shard_map/experts/pallas_call | solution.py:472
  182.5 4.0 collective-permute-start.17
  187.2 9.0 %expert_grads.2 = bf16[4,2,3,128,1024]{4,3,2,1,0:T(8,128)(2,1)} custom-call(s32[4,9]{1,0:T(4,128)S(1)} %copy-done.51, bf16[4,1280,1536]{2,1,0:T(8,128)(2,1)} %get-tuple-element.160.acts, bf16[4,1280,1024]{2,1,0:T(8,128)(2,1)} %get-tuple-element.154.xg, bf16[4,1280,1024]{2,1,0:T(8,128)(2,1)} %get-tuple-element.155.pg), custom_call_target="tpu_custom_call" | custom-call | flops 1000000 | bytes 10000 | tf_op jit(solution)/shard_map/expert_grads/pallas_call | solution.py:514
  201.2 11.9 %expert_grads.3 = bf16[4,2,3,128,1024]{4,3,2,1,0:T(8,128)(2,1)} custom-call(s32[4,9]{1,0:T(4,128)S(1)} %copy-done.52, bf16[4,1280,1536]{2,1,0:T(8,128)(2,1)} %get-tuple-element.160.acts, bf16[4,1280,1024]{2,1,0:T(8,128)(2,1)} %get-tuple-element.154.xg, bf16[4,1280,1024]{2,1,0:T(8,128)(2,1)} %get-tuple-element.155.pg), custom_call_target="tpu_custom_call" | custom-call | flops 1000000 | bytes 10000 | tf_op jit(solution)/shard_map/expert_grads/pallas_call | solution.py:514
  218.4 7.1 %expert_sum.1 = (bf16[256,1024]{1,0:T(8,128)(2,1)S(1)}, bf16[256,1024]{1,0:T(8,128)(2,1)S(1)}, bf16[256,1024]{1,0:T(8,128)(2,1)S(1)}, bf16[256,1024]{1,0:T(8,128...) custom-call(s32[4,9]{1,0:T(4,128)S(1)} %copy-done.52, ...), custom_call_target="tpu_custom_call" | custom-call | flops 1000000 | bytes 10000 | tf_op jit(solution)/shard_map/expert_sum/pallas_call | solution.py:60
  228.0 6.2 %collective-permute-done.21.refs_1_ = bf16[256,1152]{1,0:T(8,128)(2,1)S(1)} collective-permute-done((bf16[256,1152]{1,0:T(8,128)(2,1)S(1)}, bf16[256,1152]{1,0:T(8,128)(2,1)S(1)}, u32[]{:S(2)}, u32[]{:S(2)}) %collective-permute-start.21) | collective-permute-done | bytes 589856 | tf_op jit(solution)/shard_map/ppermute | solution.py:576
  236.6 9.6 %collective-permute-done.23.refs_2_ = bf16[256,1152]{1,0:T(8,128)(2,1)S(1)} collective-permute-done((bf16[256,1152]{1,0:T(8,128)(2,1)S(1)}, bf16[256,1152]{1,0:T(8,128)(2,1)S(1)}, u32[]{:S(2)}, u32[]{:S(2)}) %collective-permute-start.23) | collective-permute-done | bytes 589856 | tf_op jit(solution)/shard_map/ppermute | solution.py:576
  252.8 16.3 %attention_back.1 = (bf16[256,1024]{1,0:T(8,128)(2,1)S(1)}, bf16[256,1024]{1,0:T(8,128)(2,1)S(1)}, bf16[256,1024]{1,0:T(8,128)(2,1)S(1)}, bf16[256,1024]{1,0:T(8,128)(2,1)S(1)}, bf16[256,1024]{1,0:T(8,128)(2,1)S(1)}) custom-call(s32[4]{0:T(128)S(1)} %pad_add_fusion.places, bf16[256,1024]{1,0:T(8,128)(2,1)S(1)} %get-tuple-element.216.do_s, ...), custom_call_target="tpu_custom_call" | custom-call | flops 1000000 | bytes 10000 | tf_op jit(solution)/shard_map/attention_back/pallas_call | solution.py:60
  270.8 3.1 collective-permute-start.39
  274.8 42.5 %collective-permute-done.35.kb = bf16[256,1024]{1,0:T(8,128)(2,1)S(1)} collective-permute-done((bf16[256,1024]{1,0:T(8,128)(2,1)S(1)}, bf16[256,1024]{1,0:T(8,128)(2,1)S(1)}, u32[]{:S(2)}, u32[]{:S(2)}) %collective-permute-start.35) | collective-permute-done | bytes 524320 | tf_op jit(solution)/shard_map/ppermute | solution.py:550
  323.1 4.2 all-to-all-start.2
  333.8 14.7 %collective-permute-done.26.b = bf16[256,1024]{1,0:T(8,128)(2,1)S(1)} collective-permute-done((bf16[256,1024]{1,0:T(8,128)(2,1)}, bf16[256,1024]{1,0:T(8,128)(2,1)S(1)}, u32[]{:S(2)}, u32[]{:S(2)}) %collective-permute-start.26) | collective-permute-done | bytes 524320 | tf_op jit(solution)/shard_map/ppermute | solution.py:550
  349.4 3.3 collective-permute-start.27
  356.5 4.4 %all-to-all-start.1 = ((bf16[8,32,1024]{2,1,0:T(8,128)(2,1)}), bf16[8,32,1024]{2,1,0:T(8,128)(2,1)}, u32[]{:S(2)}, u32[]{:S(2)}) async-start(bf16[8,32,1024]{2,1,0:T(8,128)(2,1)} %fusion.2), calls=%async_computation.1 | async-start | bytes 1048576 | tf_op jit(solution)/shard_map/all_to_all | solution.py:860
  363.0 12.3 %collective-permute-done.29.b = bf16[256,1024]{1,0:T(8,128)(2,1)} collective-permute-done((bf16[256,1024]{1,0:T(8,128)(2,1)}, bf16[256,1024]{1,0:T(8,128)(2,1)}, u32[]{:S(2)}, u32[]{:S(2)}) %collective-permute-start.29) | collective-permute-done | bytes 524320 | tf_op jit(solution)/shard_map/ppermute | solution.py:550
  386.3 3.5 all-to-all-start
  391.0 3.2 collective-permute-done.30
  394.2 9.8 %collective-permute-done.28 = bf16[256,1024]{1,0:T(8,128)(2,1)} collective-permute-done((bf16[256,1024]{1,0:T(8,128)(2,1)}, bf16[256,1024]{1,0:T(8,128)(2,1)}, u32[]{:S(2)}, u32[]{:S(2)}) %collective-permute-start.28) | collective-permute-done | bytes 524320 | tf_op jit(solution)/shard_map/ppermute | solution.py:576
  411.2 5.0 %all-to-all-done = bf16[8,32,1152]{2,1,0:T(8,128)(2,1)S(1)} async-done(((bf16[8,32,1152]{2,1,0:T(8,128)(2,1)}), bf16[8,32,1152]{2,1,0:T(8,128)(2,1)S(1)}, u32[]{:S(2)}, u32[]{:S(2)}) %all-to-all-start) | async-done | bytes 589856 | tf_op jit(solution)/shard_map/all_to_all | solution.py:860
  (252 shorter events, 101.5 us)
Async XLA Ops:
  7.2 130.0 %all-gather.3.cloned.1.call-start = ((), (), s32[]{:S(2)}) async-start(), calls=%async_computation.7 | async-start | bytes 15728640 | tf_op jit(solution)/shard_map/all_gather | solution.py:751
  9.8 18.5 %collective-permute-start.1 = (bf16[288,1024]{1,0:T(8,128)(2,1)S(1)}, bf16[288,1024]{1,0:T(8,128)(2,1)}, u32[]{:S(2)}, u32[]{:S(2)}) collective-permute-start(bf16[288,1024]{1,0:T(8,128)(2,1)S(1)} %route.1.refs_8_), channel_id=1, source_target_pairs={{0,8},{4,12},{8,16},{12,20},{16,24},{20,28},{24,0},{28,4},{1,9},{5... | collective-permute-start | bytes 1769480 | tf_op jit(solution)/shard_map/ppermute | solution.py:576
  35.0 382.7 %reduce-scatter.3.cloned.1.call-start = ((), (), s32[]{:S(2)}) async-start(), calls=%async_computation.5 | async-start | bytes 7864320 | tf_op jit(solution)/shard_map/reduce_scatter | solution.py:799
  37.5 26.0 %collective-permute-start.5 = (bf16[288,1024]{1,0:T(8,128)(2,1)}, bf16[288,1024]{1,0:T(8,128)(2,1)}, u32[]{:S(2)}, u32[]{:S(2)}) collective-permute-start(bf16[288,1024]{1,0:T(8,128)(2,1)} %collective-permute-done.1.refs_9_), channel_id=1, source_target_pairs={{0,8},{4,12},{8,16},{12,20},{16,24},{20,28},{24,0},{28,4},{1,9},{5... | collective-permute-start | bytes 1769480 | tf_op jit(solution)/shard_map/ppermute | solution.py:576
  38.0 26.0 %collective-permute-start.3 = (bf16[256,1152]{1,0:T(8,128)(2,1)}, bf16[256,1152]{1,0:T(8,128)(2,1)}, u32[]{:S(2)}, u32[]{:S(2)}) collective-permute-start(bf16[256,1152]{1,0:T(8,128)(2,1)} %get-tuple-element.128.refs_0_), channel_id=1, source_target_pairs={{0,1},{1,0},{2,3},{3,2},{4,5},{5,4},{6,7},{7,6},{8,9},{9,8},{10,11... | collective-permute-start | bytes 1769480 | tf_op jit(solution)/shard_map/ppermute | solution.py:550
  38.1 26.0 %collective-permute-start.4 = (bf16[256,1152]{1,0:T(8,128)(2,1)}, bf16[256,1152]{1,0:T(8,128)(2,1)}, u32[]{:S(2)}, u32[]{:S(2)}) collective-permute-start(bf16[256,1152]{1,0:T(8,128)(2,1)} %collective-permute-done.refs_1_), channel_id=1, source_target_pairs={{0,1},{1,0},{2,3},{3,2},{4,5},{5,4},{6,7},{7,6},{8,9},{9,8},{10,11... | collective-permute-start | bytes 1769480 | tf_op jit(solution)/shard_map/ppermute | solution.py:550
  38.6 42.8 %collective-permute-start.7 = (bf16[288,1024]{1,0:T(8,128)(2,1)}, bf16[288,1024]{1,0:T(8,128)(2,1)}, u32[]{:S(2)}, u32[]{:S(2)}) collective-permute-start(bf16[288,1024]{1,0:T(8,128)(2,1)} %collective-permute-done.1.refs_9_), channel_id=1, source_target_pairs={{0,4},{4,0},{8,12},{12,8},{16,20},{20,16},{24,28},{28,24},{1,5},{5... | collective-permute-start | bytes 1769480 | tf_op jit(solution)/shard_map/ppermute | solution.py:550
  51.3 30.1 %collective-permute-start.8 = (bf16[288,1024]{1,0:T(8,128)(2,1)}, bf16[288,1024]{1,0:T(8,128)(2,1)}, u32[]{:S(2)}, u32[]{:S(2)}) collective-permute-start(bf16[288,1024]{1,0:T(8,128)(2,1)} %collective-permute-done.6.refs_11_), channel_id=1, source_target_pairs={{0,4},{4,0},{8,12},{12,8},{16,20},{20,16},{24,28},{28,24},{1,5},{5... | collective-permute-start | bytes 1769480 | tf_op jit(solution)/shard_map/ppermute | solution.py:550
  63.5 34.8 %collective-permute-start.11 = (bf16[288,1024]{1,0:T(8,128)(2,1)}, bf16[288,1024]{1,0:T(8,128)(2,1)S(1)}, u32[]{:S(2)}, u32[]{:S(2)}) collective-permute-start(bf16[288,1024]{1,0:T(8,128)(2,1)} %collective-permute-done.5.refs_10_), channel_id=1, source_target_pairs={{0,4},{4,0},{8,12},{12,8},{16,20},{20,16},{24,28},{28,24},{1,5},{5... | collective-permute-start | bytes 1769480 | tf_op jit(solution)/shard_map/ppermute | solution.py:550
  81.4 16.9 %collective-permute-start.9 = (bf16[256,1024]{1,0:T(8,128)(2,1)S(1)}, bf16[256,1024]{1,0:T(8,128)(2,1)}, u32[]{:S(2)}, u32[]{:S(2)}) collective-permute-start(bf16[256,1024]{1,0:T(8,128)(2,1)S(1)} %get-tuple-element.136.refs_0_), channel_id=1, source_target_pairs={{0,8},{4,12},{8,16},{12,20},{16,24},{20,28},{24,0},{28,4},{1,9},{5... | collective-permute-start | bytes 1572872 | tf_op jit(solution)/shard_map/ppermute | solution.py:576
  83.5 25.9 %collective-permute-start.13 = (bf16[256,1024]{1,0:T(8,128)(2,1)S(1)}, bf16[256,1024]{1,0:T(8,128)(2,1)}, u32[]{:S(2)}, u32[]{:S(2)}) collective-permute-start(bf16[256,1024]{1,0:T(8,128)(2,1)S(1)} %get-tuple-element.136.refs_0_), channel_id=1, source_target_pairs={{0,24},{4,28},{8,0},{12,4},{16,8},{20,12},{24,16},{28,20},{1,25},{... | collective-permute-start | bytes 1572872 | tf_op jit(solution)/shard_map/ppermute | solution.py:576
  98.3 20.0 %collective-permute-start.12 = (bf16[256,1024]{1,0:T(8,128)(2,1)}, bf16[256,1024]{1,0:T(8,128)(2,1)}, u32[]{:S(2)}, u32[]{:S(2)}) collective-permute-start(bf16[256,1024]{1,0:T(8,128)(2,1)} %collective-permute-done.9.refs_1_), channel_id=1, source_target_pairs={{0,8},{4,12},{8,16},{12,20},{16,24},{20,28},{24,0},{28,4},{1,9},{5... | collective-permute-start | bytes 1572872 | tf_op jit(solution)/shard_map/ppermute | solution.py:576
  109.4 20.0 %collective-permute-start.16 = (bf16[256,1024]{1,0:T(8,128)(2,1)}, bf16[256,1024]{1,0:T(8,128)(2,1)}, u32[]{:S(2)}, u32[]{:S(2)}) collective-permute-start(bf16[256,1024]{1,0:T(8,128)(2,1)} %collective-permute-done.13.refs_3_), channel_id=1, source_target_pairs={{0,4},{4,0},{8,12},{12,8},{16,20},{20,16},{24,28},{28,24},{1,5},{5... | collective-permute-start | bytes 1572872 | tf_op jit(solution)/shard_map/ppermute | solution.py:550
  118.2 19.0 %collective-permute-start.15 = (bf16[256,1024]{1,0:T(8,128)(2,1)}, bf16[256,1024]{1,0:T(8,128)(2,1)}, u32[]{:S(2)}, u32[]{:S(2)}) collective-permute-start(bf16[256,1024]{1,0:T(8,128)(2,1)} %collective-permute-done.12.refs_2_), channel_id=1, source_target_pairs={{0,4},{4,0},{8,12},{12,8},{16,20},{20,16},{24,28},{28,24},{1,5},{5... | collective-permute-start | bytes 1572872 | tf_op jit(solution)/shard_map/ppermute | solution.py:550
  196.4 221.3 %reduce-scatter.5.cloned.1.call-start = ((), (), s32[]{:S(2)}) async-start(), calls=%async_computation.6 | async-start | bytes 7864320 | tf_op jit(solution)/shard_map/reduce_scatter | solution.py:799
  216.7 17.4 %collective-permute-start.21 = (bf16[256,1152]{1,0:T(8,128)(2,1)S(1)}, bf16[256,1152]{1,0:T(8,128)(2,1)S(1)}, u32[]{:S(2)}, u32[]{:S(2)}) collective-permute-start(bf16[256,1152]{1,0:T(8,128)(2,1)S(1)} %add.101), channel_id=1, source_target_pairs={{0,24},{4,28},{8,0},{12,4},{16,8},{20,12},{24,16},{28,20},{1,25},{... | collective-permute-start | bytes 1769480 | tf_op jit(solution)/shard_map/ppermute | solution.py:576
  216.8 17.3 %collective-permute-start.20 = (bf16[256,1152]{1,0:T(8,128)(2,1)S(1)}, bf16[256,1152]{1,0:T(8,128)(2,1)S(1)}, u32[]{:S(2)}, u32[]{:S(2)}) collective-permute-start(bf16[256,1152]{1,0:T(8,128)(2,1)S(1)} %copy-done.67), channel_id=1, source_target_pairs={{0,4},{4,0},{8,12},{12,8},{16,20},{20,16},{24,28},{28,24},{1,5},{5... | collective-permute-start | bytes 1769480 | tf_op jit(solution)/shard_map/ppermute | solution.py:550
  270.8 51.3 %collective-permute-start.39 = (bf16[1,8,32,1152]{3,2,1,0:T(8,128)(2,1)S(1)}, bf16[1,8,32,1152]{3,2,1,0:T(8,128)(2,1)S(1)}, u32[]{:S(2)}, u32[]{:S(2)}) collective-permute-start(bf16[1,8,32,1152]{3,2,1,0:T(8,128)(2,1)S(1)} %take_add.3), channel_id=1, source_target_pairs={{0,2},{1,3},{2,0},{3,1},{4,6},{5,7},{6,4},{7,5},{8,10},{9,11},{10,... | collective-permute-start | bytes 1769480 | tf_op jit(solution)/shard_map/ppermute | solution.py:550
  274.1 43.2 %collective-permute-start.35 = (bf16[256,1024]{1,0:T(8,128)(2,1)S(1)}, bf16[256,1024]{1,0:T(8,128)(2,1)S(1)}, u32[]{:S(2)}, u32[]{:S(2)}) collective-permute-start(bf16[256,1024]{1,0:T(8,128)(2,1)S(1)} %add_convert_fusion.3), channel_id=1, source_target_pairs={{0,2},{1,3},{2,0},{3,1},{4,6},{5,7},{6,4},{7,5},{8,10},{9,11},{10,... | collective-permute-start | bytes 1572872 | tf_op jit(solution)/shard_map/ppermute | solution.py:550
  322.1 30.6 %collective-permute-start.36 = (bf16[2,8,32,1152]{3,2,1,0:T(8,128)(2,1)}, bf16[2,8,32,1152]{3,2,1,0:T(8,128)(2,1)S(1)}, u32[]{:S(2)}, u32[]{:S(2)}) collective-permute-start(bf16[2,8,32,1152]{3,2,1,0:T(8,128)(2,1)} %get-tuple-element.231), channel_id=1, source_target_pairs={{0,1},{1,0},{2,3},{3,2},{4,5},{5,4},{6,7},{7,6},{8,9},{9,8},{10,11... | collective-permute-start | bytes 3538952 | tf_op jit(solution)/shard_map/ppermute | solution.py:550
  323.1 33.4 %all-to-all-start.2 = ((bf16[8,32,1152]{2,1,0:T(8,128)(2,1)}), bf16[8,32,1152]{2,1,0:T(8,128)(2,1)}, u32[]{:S(2)}, u32[]{:S(2)}) async-start(bf16[8,32,1152]{2,1,0:T(8,128)(2,1)} %fusion.1), calls=%async_computation.2 | async-start | bytes 1179648 | tf_op jit(solution)/shard_map/all_to_all | solution.py:860
  327.4 21.1 %collective-permute-start.26 = (bf16[256,1024]{1,0:T(8,128)(2,1)}, bf16[256,1024]{1,0:T(8,128)(2,1)S(1)}, u32[]{:S(2)}, u32[]{:S(2)}) collective-permute-start(bf16[256,1024]{1,0:T(8,128)(2,1)} %copy-done.60), channel_id=1, source_target_pairs={{0,4},{4,0},{8,12},{12,8},{16,20},{20,16},{24,28},{28,24},{1,5},{5... | collective-permute-start | bytes 1572872 | tf_op jit(solution)/shard_map/ppermute | solution.py:550
  329.3 26.1 %collective-permute-start.38 = (bf16[1,8,32,1024]{3,2,1,0:T(8,128)(2,1)S(1)}, bf16[1,8,32,1024]{3,2,1,0:T(8,128)(2,1)S(1)}, u32[]{:S(2)}, u32[]{:S(2)}) collective-permute-start(bf16[1,8,32,1024]{3,2,1,0:T(8,128)(2,1)S(1)} %copy-done.45), channel_id=1, source_target_pairs={{0,2},{1,3},{2,0},{3,1},{4,6},{5,7},{6,4},{7,5},{8,10},{9,11},{10,... | collective-permute-start | bytes 1572872 | tf_op jit(solution)/shard_map/ppermute | solution.py:550
  331.7 47.0 %collective-permute-start.25 = (bf16[256,1024]{1,0:T(8,128)(2,1)}, bf16[256,1024]{1,0:T(8,128)(2,1)}, u32[]{:S(2)}, u32[]{:S(2)}) collective-permute-start(bf16[256,1024]{1,0:T(8,128)(2,1)} %copy-done.58), channel_id=1, source_target_pairs={{0,4},{4,0},{8,12},{12,8},{16,20},{20,16},{24,28},{28,24},{1,5},{5... | collective-permute-start | bytes 1572872 | tf_op jit(solution)/shard_map/ppermute | solution.py:550
  332.0 43.3 %collective-permute-start.29 = (bf16[256,1024]{1,0:T(8,128)(2,1)}, bf16[256,1024]{1,0:T(8,128)(2,1)}, u32[]{:S(2)}, u32[]{:S(2)}) collective-permute-start(bf16[256,1024]{1,0:T(8,128)(2,1)} %copy-done.59), channel_id=1, source_target_pairs={{0,4},{4,0},{8,12},{12,8},{16,20},{20,16},{24,28},{28,24},{1,5},{5... | collective-permute-start | bytes 1572872 | tf_op jit(solution)/shard_map/ppermute | solution.py:550
  349.4 30.5 %collective-permute-start.27 = (bf16[256,1024]{1,0:T(8,128)(2,1)}, bf16[256,1024]{1,0:T(8,128)(2,1)}, u32[]{:S(2)}, u32[]{:S(2)}) collective-permute-start(bf16[256,1024]{1,0:T(8,128)(2,1)} %add.106), channel_id=1, source_target_pairs={{0,24},{4,28},{8,0},{12,4},{16,8},{20,12},{24,16},{28,20},{1,25},{... | collective-permute-start | bytes 1572872 | tf_op jit(solution)/shard_map/ppermute | solution.py:576
  352.8 31.4 %collective-permute-start.37 = (bf16[1,8,32,1152]{3,2,1,0:T(8,128)(2,1)S(1)}, bf16[1,8,32,1152]{3,2,1,0:T(8,128)(2,1)}, u32[]{:S(2)}, u32[]{:S(2)}) collective-permute-start(bf16[1,8,32,1152]{3,2,1,0:T(8,128)(2,1)S(1)} %take_add.5), channel_id=1, source_target_pairs={{0,2},{1,3},{2,0},{3,1},{4,6},{5,7},{6,4},{7,5},{8,10},{9,11},{10,... | collective-permute-start | bytes 1769480 | tf_op jit(solution)/shard_map/ppermute | solution.py:550
  356.5 29.8 %all-to-all-start.1 = ((bf16[8,32,1024]{2,1,0:T(8,128)(2,1)}), bf16[8,32,1024]{2,1,0:T(8,128)(2,1)}, u32[]{:S(2)}, u32[]{:S(2)}) async-start(bf16[8,32,1024]{2,1,0:T(8,128)(2,1)} %fusion.2), calls=%async_computation.1 | async-start | bytes 1048576 | tf_op jit(solution)/shard_map/all_to_all | solution.py:860
  360.9 28.9 %collective-permute-start.24 = (bf16[256,1024]{1,0:T(8,128)(2,1)}, bf16[256,1024]{1,0:T(8,128)(2,1)}, u32[]{:S(2)}, u32[]{:S(2)}) collective-permute-start(bf16[256,1024]{1,0:T(8,128)(2,1)} %copy-done.57), channel_id=1, source_target_pairs={{0,4},{4,0},{8,12},{12,8},{16,20},{20,16},{24,28},{28,24},{1,5},{5... | collective-permute-start | bytes 1572872 | tf_op jit(solution)/shard_map/ppermute | solution.py:550
  377.2 17.0 %collective-permute-start.30 = (bf16[256,1024]{1,0:T(8,128)(2,1)}, bf16[256,1024]{1,0:T(8,128)(2,1)}, u32[]{:S(2)}, u32[]{:S(2)}) collective-permute-start(bf16[256,1024]{1,0:T(8,128)(2,1)} %add.108), channel_id=1, source_target_pairs={{0,8},{4,12},{8,16},{12,20},{16,24},{20,28},{24,0},{28,4},{1,9},{5... | collective-permute-start | bytes 1572872 | tf_op jit(solution)/shard_map/ppermute | solution.py:576
  381.9 22.2 %collective-permute-start.28 = (bf16[256,1024]{1,0:T(8,128)(2,1)}, bf16[256,1024]{1,0:T(8,128)(2,1)}, u32[]{:S(2)}, u32[]{:S(2)}) collective-permute-start(bf16[256,1024]{1,0:T(8,128)(2,1)} %add.107), channel_id=1, source_target_pairs={{0,24},{4,28},{8,0},{12,4},{16,8},{20,12},{24,16},{28,20},{1,25},{... | collective-permute-start | bytes 1572872 | tf_op jit(solution)/shard_map/ppermute | solution.py:576
  386.3 29.9 %all-to-all-start = ((bf16[8,32,1152]{2,1,0:T(8,128)(2,1)}), bf16[8,32,1152]{2,1,0:T(8,128)(2,1)S(1)}, u32[]{:S(2)}, u32[]{:S(2)}) async-start(bf16[8,32,1152]{2,1,0:T(8,128)(2,1)} %fusion), calls=%async_computation | async-start | bytes 1179648 | tf_op jit(solution)/shard_map/all_to_all | solution.py:860
  (82 other events, 1049.0 us)
Sparse Core Ops, SparseCore 0:
  35.1 81.3 all-gather.2
  196.5 59.5 reduce-scatter.2
  258.8 75.6 reduce-scatter.4

commit v2 on v1

--- a/solution.py
+++ b/solution.py
@@ -56,7 +56,7 @@
     return jax.ShapeDtypeStruct(shape, dtype)
 
 
-def call(body, outs, ins, scratch=(), smem=0, name=None, mib=40, flops=10**6, nbytes=10**4):
+def call(body, outs, ins, scratch=(), smem=0, name=None, mib=20, flops=10**6, nbytes=10**4):
     return pl.pallas_call(
         body,
         out_shape=outs,
@@ -206,11 +206,11 @@
     do_out[...] = dot(branch, wo[...], 1, 1).astype(bf16)
 
 
-def attention_back_body(nb, places, do_s, q, *refs):
+def attention_back_body(marks, places, do_s, q, *refs):
+    nb = len(marks)
     kvs = refs[:nb]
-    (lse, cosine, sine, dq_out) = refs[nb : nb + 4]
-    dkv = refs[nb + 4 : 2 * nb + 4]
-    bias = refs[2 * nb + 4]
+    (lse, cosine, sine, dq_out, near, far, bias) = refs[nb:]
+    dkv = [(far if m % 2 else near).at[m // 2] for m in marks]
     tokens = q.shape[0]
     fill_bias(places, kvs, bias)
     c, s = cosine[...], sine[...]
@@ -239,9 +239,9 @@
 
 
 def finish_body(
-    ka, kb, dq, wq, wk, wv, hgrad, x, gain, cosine, sine, in_out, dkv_out, gp_out
+    near, got, far, dq, wq, wk, wv, hgrad, x, gain, cosine, sine, in_out, dkv_out, gp_out
 ):
-    total = ka[...].astype(f32) + kb[...].astype(f32)
+    total = near[0].astype(f32) + got[0].astype(f32) + far[0].astype(f32)
     c, s = cosine[...], sine[...]
     for at in range(0, KV, 128):
         dkv_out[:, at : at + 128] = turn(total[:, at : at + 128], c, -s).astype(bf16)
@@ -439,6 +439,31 @@
                     ).astype(bf16)
 
 
+def expert_grad_split_body(first, me, offs, acts, xg, pg, near, far):
+    e = pl.program_id(0) + first
+    blocks = offs.shape[1] - 1
+    steps = pl.cdiv(offs[e, blocks], TILE)
+    half, _, _, part, width = near.shape
+    hid = 2 * half * part
+
+    @pl.when(steps == 0)
+    def _():
+        near[...] = jnp.zeros_like(near)
+        far[...] = jnp.zeros_like(far)
+
+    for n in range(1, xg.shape[1] // TILE + 1):
+
+        @pl.when(steps == n)
+        def _(n=n):
+            for i, right in enumerate((xg, xg, pg)):
+                for p in range(half):
+                    for out, place in ((near, me[0] % 2), (far, 1 - me[0] % 2)):
+                        at = pl.multiple_of(i * hid + (2 * p + place) * part, part)
+                        out[p, 0, i] = dot(
+                            acts[0, : n * TILE, pl.ds(at, part)], right[0, : n * TILE, :], 0, 0
+                        ).astype(bf16)
+
+
 def expert_sum_body(blocks, tokens, offs, so, slots, *refs):
     outs, stage = refs[:blocks], refs[blocks]
     local_count, width = so.shape[0], so.shape[2]
@@ -456,7 +481,7 @@
         outs[b][...] = dot(jnp.concatenate(picks, 0), stage[b % 2], 0, 0).astype(bf16)
 
 
-def expert_call(base, rows, grads, router, weights):
+def expert_call(me, base, rows, grads, router, weights):
     hidden_parts, matrices, part, width = weights.shape
     local_count = matrices // 3
     blocks, tokens = len(rows), rows[0].shape[0]
@@ -521,10 +546,28 @@
                 for n in (3 * hid, width, width)
             ],
             out_specs=pl.BlockSpec((hidden_parts, 1, 3, part, width), lambda e: (0, e, 0, 0, 0)),
-            compiler_params=pltpu.CompilerParams(vmem_limit_bytes=48 * MIB),
+            compiler_params=pltpu.CompilerParams(vmem_limit_bytes=60 * MIB),
             cost_estimate=pl.CostEstimate(flops=10**6, bytes_accessed=10**4, transcendentals=0),
             name="expert_grads",
         )(offs, acts, xg, pg)
+
+    def split_grads_of(first, number, acts):
+        shape = (hidden_parts // 2, number, 3, part, width)
+        out_spec = pl.BlockSpec((hidden_parts // 2, 1, 3, part, width), lambda e: (0, e, 0, 0, 0))
+        return pl.pallas_call(
+            functools.partial(expert_grad_split_body, first),
+            grid=(number,),
+            out_shape=(struct(shape), struct(shape)),
+            in_specs=[SMEM, SMEM]
+            + [
+                pl.BlockSpec((1, most, n), lambda e: (e + first, 0, 0))
+                for n in (3 * hid, width, width)
+            ],
+            out_specs=(out_spec, out_spec),
+            compiler_params=pltpu.CompilerParams(vmem_limit_bytes=60 * MIB),
+            cost_estimate=pl.CostEstimate(flops=10**6, bytes_accessed=10**4, transcendentals=0),
+            name="expert_grads",
+        )(me, offs, acts, xg, pg)
 
     def outs_of(so):
         return call(
@@ -534,11 +577,12 @@
             scratch=[pltpu.VMEM((2, local_count * CAP, width), bf16)],
             smem=1,
             name="expert_sum",
+            mib=60,
             flops=10**6,
             nbytes=10**4,
         )
 
-    return rows_back, acts, so, grads_of, outs_of
+    return rows_back, acts, so, grads_of, split_grads_of, outs_of
 
 
 def after(values, first):
@@ -599,10 +643,25 @@
         out_shape=struct((n,) + rest),
         in_specs=[spec, spec],
         out_specs=pl.BlockSpec((1,) + rest, lambda i: (i,) + (0,) * len(rest)),
-        compiler_params=pltpu.CompilerParams(vmem_limit_bytes=40 * MIB),
+        compiler_params=pltpu.CompilerParams(vmem_limit_bytes=10 * MIB),
         cost_estimate=pl.CostEstimate(flops=10**6, bytes_accessed=10**4, transcendentals=0),
         name="take_add",
     )(near, got)
+
+
+def all_add(a, b):
+    rest = a.shape[1:]
+    spec = pl.BlockSpec((1,) + rest, lambda i: (i,) + (0,) * len(rest))
+    return pl.pallas_call(
+        add_body,
+        grid=(a.shape[0],),
+        out_shape=struct(a.shape),
+        in_specs=[spec, spec],
+        out_specs=spec,
+        compiler_params=pltpu.CompilerParams(vmem_limit_bytes=60 * MIB),
+        cost_estimate=pl.CostEstimate(flops=10**6, bytes_accessed=10**4, transcendentals=0),
+        name="all_add",
+    )(a, b)
 
 
 def sum_parts(near, far):
@@ -634,7 +693,7 @@
 
 
 def add(a, b):
-    return call(add_body, struct(a.shape), (a, b), name="add")
+    return call(add_body, struct(a.shape), (a, b), name="add", mib=6)
 
 
 def sum_expert(parts):
@@ -781,6 +840,7 @@
     router_rows = router_weight.T
     for i in range(0, groups, chunk):
         r, *rest = expert_call(
+            me,
             first_expert.reshape(1),
             rows[i : i + chunk],
             grads[i : i + chunk],
@@ -792,14 +852,16 @@
     half_count = (local_count + 1) // 2
 
     def weight_grads(first, number, held):
-        parts = [grads_of(first, number, a) for (_, _, grads_of, _), a in zip(todo, held)]
+        parts = [grads_of(first, number, a) for (_, _, grads_of, _, _), a in zip(todo, held)]
         return parts[0] if len(parts) == 1 else sum(p.astype(f32) for p in parts).astype(bf16)
 
     def matrix_sum(part):
         return lax.psum_scatter(part, "hidden", scatter_dimension=0, tiled=False)
 
+    pairs = [[c + 2 * i for i in range(hidden_parts // 2)] for c in range(2)]
+
     def token_sums(held):
-        return [o for (_, _, _, outs_of), so in zip(todo, held) for o in outs_of(so)]
+        return [o for (_, _, _, _, outs_of), so in zip(todo, held) for o in outs_of(so)]
 
     all_acts, all_so = [t[0] for t in todo], [t[1] for t in todo]
     rest_count = local_count - half_count
@@ -811,22 +873,21 @@
         def work_2(values, held):
             dw_halves.append(matrix_sum(held))
             values, acts = after(values, all_acts)
-            return values, weight_grads(half_count, rest_count, acts)
+            return values, todo[0][3](half_count, rest_count, acts[0])
 
         def work_3(values, held):
-            dw_halves.append(matrix_sum(held))
             values, so = after(values, all_so)
-            return values, token_sums(so)
+            return values, (held, token_sums(so))
 
         dw_halves = []
-        row_parts, outs = sum_expert_beside(
+        row_parts, (dw_rest, outs) = sum_expert_beside(
             rows_back, begin, (work_2, work_3, lambda values, held: (values, held))
         )
         row_parts[0], outs = after(row_parts[0], outs)
     else:
         row_parts = sum_expert(rows_back)
         dw_halves = [matrix_sum(weight_grads(0, local_count, all_acts))]
-        outs = token_sums(all_so)
+        outs, dw_rest = token_sums(all_so), None
 
     hidden_grad, branch, logit_grad, gain_share, out_grad = call(
         functools.partial(hidden_back_body, len(row_parts)),
@@ -840,6 +901,9 @@
         (*row_parts, hidden, gates, cotangent, gain_two, router, out_weight),
         name="hidden_back",
     )
+
+    def across(near, far):
+        return (near, *sum_parts_begin(near, flip(far, "hidden", 1)))
 
     def weight_parts(left, right, sides=()):
         n = right.shape[1] + (SIDE if sides else 0)
@@ -854,40 +918,58 @@
             name="weight_grad",
         )
 
-    def sum_over_mesh(near, got, far):
-        left, got = sum_parts_end(near, got, far)
+    def end_over_mesh(left, got):
         half = sum([v.astype(f32) for v in left], got.astype(f32)).astype(bf16)
         got = lax.all_to_all(half, "expert", split_axis=0, concat_axis=0, tiled=True)
         return jnp.sum(got.astype(f32), axis=0)
 
-    def across(near, far):
-        return (near, *sum_parts_begin(near, flip(far, "hidden", 1)))
-
     spot = jnp.broadcast_to(
         (jnp.arange(SIDE, dtype=jnp.int32) == EXPERTS).astype(bf16)[None, :], (tokens, SIDE)
     )
     first_parts = weight_parts(att, branch, ((ffn, logit_grad), (gain_share, spot)))
     first_parts = across(*first_parts)
     out_grad, first_parts = after(out_grad, first_parts)
-    first_sums = sum_over_mesh(*first_parts)
-    dq, *dkvs = call(
-        functools.partial(attention_back_body, nb),
-        [struct((tokens, width))] + [struct((tokens, 2 * KV))] * nb,
+    first_left, first_got = sum_parts_end(*first_parts)
+    dq, near, far = call(
+        functools.partial(attention_back_body, marks),
+        (
+            struct((tokens, width)),
+            struct((nb // 2, tokens, 2 * KV)),
+            struct((nb // 2, tokens, 2 * KV)),
+        ),
         (places, out_grad, q, *kvs, lse, cosine, sine),
         scratch=[pltpu.VMEM((nb, tokens, tokens), f32)],
         smem=1,
         name="attention_back",
     )
-    ka, kb = sum_hidden(dict(zip(marks, dkvs)))
+    if groups == 8:
+        moe = [flip(o, "expert", 1) for o in outs[4:]]
+        far, (first_got, moe[1], moe[2]) = after(far, [first_got, moe[1], moe[2]])
+        moved = shift(add(outs[2], moe[2]), -1)
+    kv_near, kv_got, kv_far = across(near, far)
+    kb = flip(kv_far, "hidden", 2)
+    dq, kv_far = after(dq, kv_far)
+    query_near, query_got, query_far = across(*weight_parts(normed, dq))
+    kb, query_far = after(kb, query_far)
+    query_left, query_got = sum_parts_end(query_near, query_got, query_far)
+    if dw_rest is not None:
+        near, far = dw_rest
+        kv_far, far = after(kv_far, far)
+        dw_rest = all_add(near, flip(far, "hidden", 1))
+        kb, dw_rest = after(kb, dw_rest)
+        dw_rest, dw_halves[0] = after(dw_rest, dw_halves[0])
+        dw_halves.append(
+            lax.psum_scatter(
+                dw_rest, "hidden", scatter_dimension=0, axis_index_groups=pairs, tiled=False
+            )
+        )
     dw_sum = jnp.concatenate(dw_halves, 0).astype(f32)
-    query_near, query_got, query_far = across(*weight_parts(normed, dq))
-    query_far, kb = after(query_far, kb)
-    query_sum = sum_over_mesh(query_near, query_got, query_far)
     input_grad, dkv, gain_share_one = call(
         finish_body,
         (struct((tokens, width)), struct((tokens, 2 * KV)), struct((tokens, width))),
         (
-            ka,
+            kv_near,
+            kv_got,
             kb,
             dq,
             query_weight,
@@ -900,12 +982,26 @@
             sine,
         ),
         name="finish",
+        mib=60,
         flops=10**6,
         nbytes=10**4,
     )
-    last_sums = sum_over_mesh(*across(*weight_parts(normed, dkv, ((gain_share_one, spot),))))
-    moe = sum_expert(outs)
+    last_near, last_got, last_far = across(*weight_parts(normed, dkv, ((gain_share_one, spot),)))
+    if groups == 8:
+        last_far, (moe[0], moe[3], moved) = after(last_far, [moe[0], moe[3], moved])
+        near = add(add(outs[1], moe[1]), moved)
+        moe = [add(outs[0], moe[0]), shift(near, -1), shift(add(outs[3], moe[3]), 1)]
+    else:
+        moe = sum_expert(outs)
+    first_sums = end_over_mesh(first_left, first_got)
+    query_sum = end_over_mesh(query_left, query_got)
+    last_left, last_got = sum_parts_end(last_near, last_got, last_far)
+    last_got, (first_sums, query_sum) = after(last_got, [first_sums, query_sum])
+    half = sum([v.astype(f32) for v in last_left], last_got.astype(f32)).astype(bf16)
+    got = lax.all_to_all(half, "expert", split_axis=0, concat_axis=0, tiled=True)
     block_out = (hidden + sum(m.astype(f32) for m in moe)).astype(bf16)
+    got, (block_out, dw_out) = after(got, [block_out, [dw_sum[:, i] for i in range(3)]])
+    last_sums = jnp.sum(got.astype(f32), axis=0)
     return (
         block_out,
         input_grad,
@@ -916,9 +1012,7 @@
         first_sums[:, :width],
         first_sums[:, width + EXPERTS],
         first_sums[:, width : width + EXPERTS],
-        dw_sum[:, 0],
-        dw_sum[:, 1],
-        dw_sum[:, 2],
+        *dw_out,
     )
 
 

time: 430 us -> 411 us (0.956); the launches traced: 430 us -> 405 us
  waiting for transfers between devices: 177 us -> 131 us
  Pallas kernels: 128 us -> 143 us
  local copies, waits for them, and re-layouts: 23.2 us -> 32.3 us
    ppermute x28, waiting for transfers between devices: 97 us -> 61.2 us  [flip(): return lax.ppermute(values, axis, [(i, i ^ bit) for i in range(n)])]
    pallas_call x0 -> x2, Pallas kernels: none -> 16.8 us  [the longest x1 12.5 us: split_grads_of(): pl.pallas_call(functools.partial(expert_grad_split_body, first), grid=(nu...]
    ppermute x28, starting transfers between devices: 33 us -> 21.8 us  [flip(): return lax.ppermute(values, axis, [(i, i ^ bit) for i in range(n)])]
    pallas_call x2 -> x1, Pallas kernels: 20.9 us -> 9.83 us  [grads_of(): pl.pallas_call(functools.partial(expert_grad_body, first), grid=(number,)...]
    unnamed x138, local copies, waits for them, and re-layouts: 15.8 us -> 25 us
    ppermute x12, waiting for transfers between devices: 74.4 us -> 67.6 us  [shift(): lax.ppermute(values, 'expert', [(i, (i + 2 * by) % n) for i in range(n)])]
  transfers between devices with their start and end apart: 46 -> 46, of which waited for: 20 -> 21; matrix products, arithmetic and copies ran while one was open for 4% -> 6% of each run, Pallas kernels for 19% -> 23%
where the time goes in v2:
time: 411 us; the launch traced here: 405 us
  Pallas kernels  143 us (35%)
  waiting for transfers between devices  131 us (32%)
  starting transfers between devices  68 us (17%)
  local copies, waits for them, and re-layouts  32.3 us (8%)
  other arithmetic  16.2 us (4%)
  between operations  14.6 us (4%)
    ppermute x12, waiting for transfers between devices, shift(): lax.ppermute(values, 'expert', [(i, (i + 2 * by) % n) for i in range(n)])  67.6 us
    pallas_call x21, Pallas kernels, call(): pl.pallas_call(body, out_shape=outs, in_specs=[SMEM] * smem + [VMEM] * (l...  64.9 us
    ppermute x28, waiting for transfers between devices, flip(): return lax.ppermute(values, axis, [(i, i ^ bit) for i in range(n)])  61.2 us
    pallas_call x1, Pallas kernels, expert_call(): pl.pallas_call(functools.partial(expert_body, blocks, tokens), grid=(loca...  47.3 us
    ppermute x12, starting transfers between devices, shift(): lax.ppermute(values, 'expert', [(i, (i + 2 * by) % n) for i in range(n)])  30.4 us
    unnamed x138, local copies, waits for them, and re-layouts  25 us
    ppermute x28, starting transfers between devices, flip(): return lax.ppermute(values, axis, [(i, i ^ bit) for i in range(n)])  21.8 us
    pallas_call x1, Pallas kernels, split_grads_of(): pl.pallas_call(functools.partial(expert_grad_split_body, first), grid=(nu...  12.5 us
  transfers between devices with their start and end apart: 46, of which 21 were waited for; matrix products, arithmetic and copies ran while one was open for 6% of the time, Pallas kernels for 23%

profile of v2, /device:TPU:0, one launch (start us, length us, event | category | flops | bytes accessed | tf_op | source)
XLA Modules:
  0.0 405.2 jit_solution(10547043951757620660)
XLA Ops:
  25.0 3.3 collective-permute-done.1.refs_9_
  28.3 6.9 %collective-permute-done.refs_1_ = bf16[256,1152]{1,0:T(8,128)(2,1)} collective-permute-done((bf16[256,1152]{1,0:T(8,128)(2,1)S(1)}, bf16[256,1152]{1,0:T(8,128)(2,1)}, u32[]{:S(2)}, u32[]{:S(2)}) %collective-permute-start) | collective-permute-done | bytes 589856 | tf_op jit(solution)/shard_map/ppermute | solution.py:594
  39.4 12.2 %collective-permute-done.6.refs_11_ = bf16[288,1024]{1,0:T(8,128)(2,1)} collective-permute-done((bf16[288,1024]{1,0:T(8,128)(2,1)S(1)}, bf16[288,1024]{1,0:T(8,128)(2,1)}, u32[]{:S(2)}, u32[]{:S(2)}) %collective-permute-start.6) | collective-permute-done | bytes 589856 | tf_op jit(solution)/shard_map/ppermute | solution.py:620
  58.4 5.4 %collective-permute-done.5.refs_10_ = bf16[288,1024]{1,0:T(8,128)(2,1)} collective-permute-done((bf16[288,1024]{1,0:T(8,128)(2,1)}, bf16[288,1024]{1,0:T(8,128)(2,1)}, u32[]{:S(2)}, u32[]{:S(2)}) %collective-permute-start.5) | collective-permute-done | bytes 589856 | tf_op jit(solution)/shard_map/ppermute | solution.py:620
  64.4 13.9 %attend.1 = (f32[256,1024]{1,0:T(8,128)S(1)}, bf16[256,1024]{1,0:T(8,128)(2,1)S(1)}, bf16[256,1024]{1,0:T(8,128)(2,1)S(1)}, f32[256,128]{1,0:T(8,128)S(1)}, f32[256,128]{1,0:T(8,128)S(1)}) custom-call(s32[4]{0:T(128)S(1)} %pad_add_fusion.places, bf16[256,1024]{1,0:T(8,128)(2,1)S(1)} %copy-done.3, bf16[256,1024]{1,0:T(8,128)(2,1)S(1)} %project_q.1.q, ...), custom_call_target="tpu_custom_call" | custom-call | flops 1000000 | bytes 10000 | tf_op jit(solution)/shard_map/attend/pallas_call | solution.py:60
  83.5 3.3 collective-permute-start.13
  86.9 11.4 %collective-permute-done.9.refs_1_ = bf16[256,1024]{1,0:T(8,128)(2,1)} collective-permute-done((bf16[256,1024]{1,0:T(8,128)(2,1)S(1)}, bf16[256,1024]{1,0:T(8,128)(2,1)}, u32[]{:S(2)}, u32[]{:S(2)}) %collective-permute-start.9) | collective-permute-done | bytes 524320 | tf_op jit(solution)/shard_map/ppermute | solution.py:620
  98.3 7.1 %collective-permute-start.12 = (bf16[256,1024]{1,0:T(8,128)(2,1)}, bf16[256,1024]{1,0:T(8,128)(2,1)}, u32[]{:S(2)}, u32[]{:S(2)}) collective-permute-start(bf16[256,1024]{1,0:T(8,128)(2,1)} %collective-permute-done.9.refs_1_), channel_id=1, source_target_pairs={{0,8},{4,12},{8,16},{12,20},{16,24},{20,28},{24,0},{28,4},{1,9},{5... | collective-permute-start | bytes 1572872 | tf_op jit(solution)/shard_map/ppermute | solution.py:620
  110.2 8.1 %collective-permute-done.12.refs_2_ = bf16[256,1024]{1,0:T(8,128)(2,1)} collective-permute-done((bf16[256,1024]{1,0:T(8,128)(2,1)}, bf16[256,1024]{1,0:T(8,128)(2,1)}, u32[]{:S(2)}, u32[]{:S(2)}) %collective-permute-start.12) | collective-permute-done | bytes 524320 | tf_op jit(solution)/shard_map/ppermute | solution.py:620
  119.7 9.9 %collective-permute-done.16.refs_7_ = bf16[256,1024]{1,0:T(8,128)(2,1)} collective-permute-done((bf16[256,1024]{1,0:T(8,128)(2,1)}, bf16[256,1024]{1,0:T(8,128)(2,1)}, u32[]{:S(2)}, u32[]{:S(2)}) %collective-permute-start.16) | collective-permute-done | bytes 524320 | tf_op jit(solution)/shard_map/ppermute | solution.py:594
  129.6 7.8 %collective-permute-done.15.refs_6_ = bf16[256,1024]{1,0:T(8,128)(2,1)} collective-permute-done((bf16[256,1024]{1,0:T(8,128)(2,1)}, bf16[256,1024]{1,0:T(8,128)(2,1)}, u32[]{:S(2)}, u32[]{:S(2)}) %collective-permute-start.15) | collective-permute-done | bytes 524320 | tf_op jit(solution)/shard_map/ppermute | solution.py:594
  137.3 47.3 %experts.1 = (bf16[256,1152]{1,0:T(8,128)(2,1)}, bf16[256,1152]{1,0:T(8,128)(2,1)}, bf16[256,1152]{1,0:T(8,128)(2,1)}, bf16[256,1152]{1,0:T(8,128)(2,1)}, bf16[2...) custom-call(s32[1]{0:T(128)} %bitcast.7.base, ...), custom_call_target="tpu_custom_call" | custom-call | flops 1000000 | bytes 10000 | tf_op jit(solution)/shard_map/experts/pallas_call | solution.py:497
  184.7 9.8 %expert_grads.2 = bf16[4,2,3,128,1024]{4,3,2,1,0:T(8,128)(2,1)} custom-call(s32[4,9]{1,0:T(4,128)} %get-tuple-element.177.offs, bf16[4,1280,1536]{2,1,0:T(8,128)(2,1)} %get-tuple-element.185.acts, bf16[4,1280,1024]{2,1,0:T(8,128)(2,1)} %get-tuple-element.179.xg, bf16[4,1280,1024]{2,1,0:T(8,128)(2,1)} %get-tuple-element.180.pg), custom_call_target="tpu_custom_call" | custom-call | flops 1000000 | bytes 10000 | tf_op jit(solution)/shard_map/expert_grads/pallas_call | solution.py:539
  198.8 3.2 collective-permute-start.19
  204.3 12.5 %expert_grads.3 = (bf16[2,2,3,128,1024]{4,3,2,1,0:T(8,128)(2,1)}, bf16[2,2,3,128,1024]{4,3,2,1,0:T(8,128)(2,1)}) custom-call(s32[1]{0:T(128)} %bitcast.me, s32[4,9]{1,0:T(4,128)} %get-tuple-element.177.offs, bf16[4,1280,1536]{2,1,0:T(8,128)(2,1)} %get-tuple-element.185.acts, bf16[4,1280,1024]{2,1,0:T(8,128)(2,1)} %get-tuple-element.179.xg, ...), custom_call_target="tpu_custom_call" | custom-call | flops 1000000 | bytes 10000 | tf_op jit(solution)/shard_map/expert_grads/pallas_call | solution.py:557
  221.4 7.9 %expert_sum.1 = (bf16[256,1024]{1,0:T(8,128)(2,1)}, bf16[256,1024]{1,0:T(8,128)(2,1)}, bf16[256,1024]{1,0:T(8,128)(2,1)}, bf16[256,1024]{1,0:T(8,128)(2,1)}, bf1...) custom-call(s32[4,9]{1,0:T(4,128)} %get-tuple-element.177.offs, ...), custom_call_target="tpu_custom_call" | custom-call | flops 1000000 | bytes 10000 | tf_op jit(solution)/shard_map/expert_sum/pallas_call | solution.py:60
  229.3 8.6 %collective-permute-done.21.refs_1_ = bf16[256,1152]{1,0:T(8,128)(2,1)} collective-permute-done((bf16[256,1152]{1,0:T(8,128)(2,1)}, bf16[256,1152]{1,0:T(8,128)(2,1)}, u32[]{:S(2)}, u32[]{:S(2)}) %collective-permute-start.21) | collective-permute-done | bytes 589856 | tf_op jit(solution)/shard_map/ppermute | solution.py:620
  240.5 11.5 %collective-permute-done.23.refs_2_ = bf16[256,1152]{1,0:T(8,128)(2,1)S(1)} collective-permute-done((bf16[256,1152]{1,0:T(8,128)(2,1)S(1)}, bf16[256,1152]{1,0:T(8,128)(2,1)S(1)}, u32[]{:S(2)}, u32[]{:S(2)}) %collective-permute-start.23) | collective-permute-done | bytes 589856 | tf_op jit(solution)/shard_map/ppermute | solution.py:620
  265.5 16.1 %attention_back.1 = (bf16[256,1024]{1,0:T(8,128)(2,1)S(1)}, bf16[2,256,1024]{2,1,0:T(8,128)(2,1)S(1)}, bf16[2,256,1024]{2,1,0:T(8,128)(2,1)S(1)}) custom-call(s32[4]{0:T(128)S(1)} %pad_add_fusion.places, bf16[256,1024]{1,0:T(8,128)(2,1)S(1)} %get-tuple-element.240.do_s, bf16[256,1024]{1,0:T(8,128)(2,1)S(1)} %copy-done.5, ...), custom_call_target="tpu_custom_call" | custom-call | flops 1000000 | bytes 10000 | tf_op jit(solution)/shard_map/attention_back/pallas_call | solution.py:60
  281.7 6.7 %collective-permute-done.27.b = bf16[256,1024]{1,0:T(8,128)(2,1)S(1)} collective-permute-done((bf16[256,1024]{1,0:T(8,128)(2,1)S(1)}, bf16[256,1024]{1,0:T(8,128)(2,1)S(1)}, u32[]{:S(2)}, u32[]{:S(2)}) %collective-permute-start.27) | collective-permute-done | bytes 524320 | tf_op jit(solution)/shard_map/ppermute | solution.py:594
  295.2 4.4 %all_add.1 = bf16[2,2,3,128,1024]{4,3,2,1,0:T(8,128)(2,1)} custom-call(bf16[2,2,3,128,1024]{4,3,2,1,0:T(8,128)(2,1)} %get-tuple-element.253.a, bf16[2,2,3,128,1024]{4,3,2,1,0:T(8,128)(2,1)} %collective-permute-done.31.b), custom_call_target="tpu_custom_call" | custom-call | flops 1000000 | bytes 10000 | tf_op jit(solution)/shard_map/all_add/pallas_call | solution.py:655
  302.7 5.8 %collective-permute-done.29.far = bf16[1,256,1024]{2,1,0:T(8,128)(2,1)} collective-permute-done((bf16[1,256,1024]{2,1,0:T(8,128)(2,1)S(1)}, bf16[1,256,1024]{2,1,0:T(8,128)(2,1)}, u32[]{:S(2)}, u32[]{:S(2)}) %collective-permute-start.29) | collective-permute-done | bytes 524320 | tf_op jit(solution)/shard_map/ppermute | solution.py:594
  310.6 4.2 %all-to-all-start = ((bf16[8,32,1152]{2,1,0:T(8,128)(2,1)}), bf16[8,32,1152]{2,1,0:T(8,128)(2,1)}, u32[]{:S(2)}, u32[]{:S(2)}) async-start(bf16[8,32,1152]{2,1,0:T(8,128)(2,1)} %fusion.1), calls=%async_computation | async-start | bytes 1179648 | tf_op jit(solution)/shard_map/all_to_all | solution.py:923
  315.8 6.2 %finish.1 = (bf16[256,1024]{1,0:T(8,128)(2,1)}, bf16[256,1024]{1,0:T(8,128)(2,1)}, bf16[256,1024]{1,0:T(8,128)(2,1)}) custom-call(bf16[2,256,1024]{2,1,0:T(8,128)(2,1)} %copy-done.11, bf16[2,256,1024]{2,1,0:T(8,128)(2,1)} %copy-done.12, bf16[1,256,1024]{2,1,0:T(8,128)(2,1)} %collective-permute-done.29.far, bf16[256,1024]{1,0:T(8,128)(2,1)} %copy-done.25, ...), custom_call_target="tpu_custom_call" | custom-call | flops 1000000 | bytes 10000 | tf_op jit(solution)/shard_map/finish/pallas_call | solution.py:60
  329.2 3.7 collective-permute-start.35
  332.9 7.8 %collective-permute-done.37 = bf16[1,8,32,1024]{3,2,1,0:T(8,128)(2,1)S(1)} collective-permute-done((bf16[1,8,32,1024]{3,2,1,0:T(8,128)(2,1)}, bf16[1,8,32,1024]{3,2,1,0:T(8,128)(2,1)S(1)}, u32[]{:S(2)}, u32[]{:S(2)}) %collective-permute-start.37) | collective-permute-done | bytes 524320 | tf_op jit(solution)/shard_map/ppermute | solution.py:594
  342.8 5.9 %all-to-all-start.1 = ((bf16[8,32,1024]{2,1,0:T(8,128)(2,1)}), bf16[8,32,1024]{2,1,0:T(8,128)(2,1)}, u32[]{:S(2)}, u32[]{:S(2)}) async-start(bf16[8,32,1024]{2,1,0:T(8,128)(2,1)} %fusion.2), calls=%async_computation.1 | async-start | bytes 1048576 | tf_op jit(solution)/shard_map/all_to_all | solution.py:923
  350.7 3.9 collective-permute-done.34.b
  357.1 5.9 %collective-permute-start.38 = (bf16[256,1024]{1,0:T(8,128)(2,1)S(1)}, bf16[256,1024]{1,0:T(8,128)(2,1)}, u32[]{:S(2)}, u32[]{:S(2)}) collective-permute-start(bf16[256,1024]{1,0:T(8,128)(2,1)S(1)} %add.93), channel_id=1, source_target_pairs={{0,24},{4,28},{8,0},{12,4},{16,8},{20,12},{24,16},{28,20},{1,25},{... | collective-permute-start | bytes 1572872 | tf_op jit(solution)/shard_map/ppermute | solution.py:620
  367.0 5.7 %collective-permute-done.36 = bf16[1,8,32,1152]{3,2,1,0:T(8,128)(2,1)} collective-permute-done((bf16[1,8,32,1152]{3,2,1,0:T(8,128)(2,1)}, bf16[1,8,32,1152]{3,2,1,0:T(8,128)(2,1)}, u32[]{:S(2)}, u32[]{:S(2)}) %collective-permute-start.36) | collective-permute-done | bytes 589856 | tf_op jit(solution)/shard_map/ppermute | solution.py:594
  375.0 5.5 %all-to-all-start.2 = ((bf16[8,32,1152]{2,1,0:T(8,128)(2,1)}), bf16[8,32,1152]{2,1,0:T(8,128)(2,1)S(1)}, u32[]{:S(2)}, u32[]{:S(2)}) async-start(bf16[8,32,1152]{2,1,0:T(8,128)(2,1)} %fusion), calls=%async_computation.2 | async-start | bytes 1179648 | tf_op jit(solution)/shard_map/all_to_all | solution.py:1001
  380.6 4.9 %collective-permute-done.39 = bf16[256,1024]{1,0:T(8,128)(2,1)} collective-permute-done((bf16[256,1024]{1,0:T(8,128)(2,1)}, bf16[256,1024]{1,0:T(8,128)(2,1)}, u32[]{:S(2)}, u32[]{:S(2)}) %collective-permute-start.39) | collective-permute-done | bytes 524320 | tf_op jit(solution)/shard_map/ppermute | solution.py:620
  (252 shorter events, 114.0 us)
Async XLA Ops:
  7.2 130.2 %all-gather.3.cloned.1.call-start = ((), (), s32[]{:S(2)}) async-start(), calls=%async_computation.7 | async-start | bytes 15728640 | tf_op jit(solution)/shard_map/all_gather | solution.py:810
  9.8 18.5 %collective-permute-start.1 = (bf16[288,1024]{1,0:T(8,128)(2,1)S(1)}, bf16[288,1024]{1,0:T(8,128)(2,1)}, u32[]{:S(2)}, u32[]{:S(2)}) collective-permute-start(bf16[288,1024]{1,0:T(8,128)(2,1)S(1)} %route.1.refs_8_), channel_id=1, source_target_pairs={{0,8},{4,12},{8,16},{12,20},{16,24},{20,28},{24,0},{28,4},{1,9},{5... | collective-permute-start | bytes 1769480 | tf_op jit(solution)/shard_map/ppermute | solution.py:620
  35.3 273.2 %reduce-scatter.3.cloned.1.call-start = ((), (), s32[]{:S(2)}) async-start(), calls=%async_computation.5 | async-start | bytes 7864320 | tf_op jit(solution)/shard_map/reduce_scatter | solution.py:859
  37.8 26.0 %collective-permute-start.5 = (bf16[288,1024]{1,0:T(8,128)(2,1)}, bf16[288,1024]{1,0:T(8,128)(2,1)}, u32[]{:S(2)}, u32[]{:S(2)}) collective-permute-start(bf16[288,1024]{1,0:T(8,128)(2,1)} %collective-permute-done.1.refs_9_), channel_id=1, source_target_pairs={{0,8},{4,12},{8,16},{12,20},{16,24},{20,28},{24,0},{28,4},{1,9},{5... | collective-permute-start | bytes 1769480 | tf_op jit(solution)/shard_map/ppermute | solution.py:620
  38.3 26.0 %collective-permute-start.3 = (bf16[256,1152]{1,0:T(8,128)(2,1)S(1)}, bf16[256,1152]{1,0:T(8,128)(2,1)}, u32[]{:S(2)}, u32[]{:S(2)}) collective-permute-start(bf16[256,1152]{1,0:T(8,128)(2,1)S(1)} %get-tuple-element.154.refs_0_), channel_id=1, source_target_pairs={{0,1},{1,0},{2,3},{3,2},{4,5},{5,4},{6,7},{7,6},{8,9},{9,8},{10,11... | collective-permute-start | bytes 1769480 | tf_op jit(solution)/shard_map/ppermute | solution.py:594
  38.4 26.0 %collective-permute-start.4 = (bf16[256,1152]{1,0:T(8,128)(2,1)}, bf16[256,1152]{1,0:T(8,128)(2,1)}, u32[]{:S(2)}, u32[]{:S(2)}) collective-permute-start(bf16[256,1152]{1,0:T(8,128)(2,1)} %collective-permute-done.refs_1_), channel_id=1, source_target_pairs={{0,1},{1,0},{2,3},{3,2},{4,5},{5,4},{6,7},{7,6},{8,9},{9,8},{10,11... | collective-permute-start | bytes 1769480 | tf_op jit(solution)/shard_map/ppermute | solution.py:594
  38.9 42.5 %collective-permute-start.7 = (bf16[288,1024]{1,0:T(8,128)(2,1)}, bf16[288,1024]{1,0:T(8,128)(2,1)}, u32[]{:S(2)}, u32[]{:S(2)}) collective-permute-start(bf16[288,1024]{1,0:T(8,128)(2,1)} %collective-permute-done.1.refs_9_), channel_id=1, source_target_pairs={{0,4},{4,0},{8,12},{12,8},{16,20},{20,16},{24,28},{28,24},{1,5},{5... | collective-permute-start | bytes 1769480 | tf_op jit(solution)/shard_map/ppermute | solution.py:594
  51.6 29.8 %collective-permute-start.8 = (bf16[288,1024]{1,0:T(8,128)(2,1)}, bf16[288,1024]{1,0:T(8,128)(2,1)}, u32[]{:S(2)}, u32[]{:S(2)}) collective-permute-start(bf16[288,1024]{1,0:T(8,128)(2,1)} %collective-permute-done.6.refs_11_), channel_id=1, source_target_pairs={{0,4},{4,0},{8,12},{12,8},{16,20},{20,16},{24,28},{28,24},{1,5},{5... | collective-permute-start | bytes 1769480 | tf_op jit(solution)/shard_map/ppermute | solution.py:594
  63.8 34.5 %collective-permute-start.11 = (bf16[288,1024]{1,0:T(8,128)(2,1)}, bf16[288,1024]{1,0:T(8,128)(2,1)S(1)}, u32[]{:S(2)}, u32[]{:S(2)}) collective-permute-start(bf16[288,1024]{1,0:T(8,128)(2,1)} %collective-permute-done.5.refs_10_), channel_id=1, source_target_pairs={{0,4},{4,0},{8,12},{12,8},{16,20},{20,16},{24,28},{28,24},{1,5},{5... | collective-permute-start | bytes 1769480 | tf_op jit(solution)/shard_map/ppermute | solution.py:594
  81.4 16.9 %collective-permute-start.9 = (bf16[256,1024]{1,0:T(8,128)(2,1)S(1)}, bf16[256,1024]{1,0:T(8,128)(2,1)}, u32[]{:S(2)}, u32[]{:S(2)}) collective-permute-start(bf16[256,1024]{1,0:T(8,128)(2,1)S(1)} %get-tuple-element.161.refs_0_), channel_id=1, source_target_pairs={{0,8},{4,12},{8,16},{12,20},{16,24},{20,28},{24,0},{28,4},{1,9},{5... | collective-permute-start | bytes 1572872 | tf_op jit(solution)/shard_map/ppermute | solution.py:620
  83.5 25.9 %collective-permute-start.13 = (bf16[256,1024]{1,0:T(8,128)(2,1)S(1)}, bf16[256,1024]{1,0:T(8,128)(2,1)}, u32[]{:S(2)}, u32[]{:S(2)}) collective-permute-start(bf16[256,1024]{1,0:T(8,128)(2,1)S(1)} %get-tuple-element.161.refs_0_), channel_id=1, source_target_pairs={{0,24},{4,28},{8,0},{12,4},{16,8},{20,12},{24,16},{28,20},{1,25},{... | collective-permute-start | bytes 1572872 | tf_op jit(solution)/shard_map/ppermute | solution.py:620
  98.3 20.0 %collective-permute-start.12 = (bf16[256,1024]{1,0:T(8,128)(2,1)}, bf16[256,1024]{1,0:T(8,128)(2,1)}, u32[]{:S(2)}, u32[]{:S(2)}) collective-permute-start(bf16[256,1024]{1,0:T(8,128)(2,1)} %collective-permute-done.9.refs_1_), channel_id=1, source_target_pairs={{0,8},{4,12},{8,16},{12,20},{16,24},{20,28},{24,0},{28,4},{1,9},{5... | collective-permute-start | bytes 1572872 | tf_op jit(solution)/shard_map/ppermute | solution.py:620
  109.4 20.1 %collective-permute-start.16 = (bf16[256,1024]{1,0:T(8,128)(2,1)}, bf16[256,1024]{1,0:T(8,128)(2,1)}, u32[]{:S(2)}, u32[]{:S(2)}) collective-permute-start(bf16[256,1024]{1,0:T(8,128)(2,1)} %collective-permute-done.13.refs_3_), channel_id=1, source_target_pairs={{0,4},{4,0},{8,12},{12,8},{16,20},{20,16},{24,28},{28,24},{1,5},{5... | collective-permute-start | bytes 1572872 | tf_op jit(solution)/shard_map/ppermute | solution.py:594
  118.3 19.0 %collective-permute-start.15 = (bf16[256,1024]{1,0:T(8,128)(2,1)}, bf16[256,1024]{1,0:T(8,128)(2,1)}, u32[]{:S(2)}, u32[]{:S(2)}) collective-permute-start(bf16[256,1024]{1,0:T(8,128)(2,1)} %collective-permute-done.12.refs_2_), channel_id=1, source_target_pairs={{0,4},{4,0},{8,12},{12,8},{16,20},{20,16},{24,28},{28,24},{1,5},{5... | collective-permute-start | bytes 1572872 | tf_op jit(solution)/shard_map/ppermute | solution.py:594
  195.7 194.0 %reduce-scatter.5.cloned.1.call-start = ((), (), s32[]{:S(2)}) async-start(), calls=%async_computation.6 | async-start | bytes 4718592 | tf_op jit(solution)/shard_map/reduce_scatter | solution.py:962
  198.8 18.0 %collective-permute-start.19 = (bf16[256,1152]{1,0:T(8,128)(2,1)}, bf16[256,1152]{1,0:T(8,128)(2,1)}, u32[]{:S(2)}, u32[]{:S(2)}) collective-permute-start(bf16[256,1152]{1,0:T(8,128)(2,1)} %add.85), channel_id=1, source_target_pairs={{0,24},{4,28},{8,0},{12,4},{16,8},{20,12},{24,16},{28,20},{1,25},{... | collective-permute-start | bytes 1769480 | tf_op jit(solution)/shard_map/ppermute | solution.py:620
  221.3 16.5 %collective-permute-start.21 = (bf16[256,1152]{1,0:T(8,128)(2,1)}, bf16[256,1152]{1,0:T(8,128)(2,1)}, u32[]{:S(2)}, u32[]{:S(2)}) collective-permute-start(bf16[256,1152]{1,0:T(8,128)(2,1)} %add.87), channel_id=1, source_target_pairs={{0,24},{4,28},{8,0},{12,4},{16,8},{20,12},{24,16},{28,20},{1,25},{... | collective-permute-start | bytes 1769480 | tf_op jit(solution)/shard_map/ppermute | solution.py:620
  258.5 36.6 %collective-permute-start.31 = (bf16[2,2,3,128,1024]{4,3,2,1,0:T(8,128)(2,1)S(1)}, bf16[2,2,3,128,1024]{4,3,2,1,0:T(8,128)(2,1)}, u32[]{:S(2)}, u32[]{:S(2)}) collective-permute-start(bf16[2,2,3,128,1024]{4,3,2,1,0:T(8,128)(2,1)S(1)} %copy-done.65), channel_id=1, source_target_pairs={{0,1},{1,0},{2,3},{3,2},{4,5},{5,4},{6,7},{7,6},{8,9},{9,8},{10,11... | collective-permute-start | bytes 9437192 | tf_op jit(solution)/shard_map/ppermute | solution.py:594
  262.3 26.1 %collective-permute-start.25 = (bf16[1,8,32,1152]{3,2,1,0:T(8,128)(2,1)S(1)}, bf16[1,8,32,1152]{3,2,1,0:T(8,128)(2,1)S(1)}, u32[]{:S(2)}, u32[]{:S(2)}) collective-permute-start(bf16[1,8,32,1152]{3,2,1,0:T(8,128)(2,1)S(1)} %take_add.4), channel_id=1, source_target_pairs={{0,2},{1,3},{2,0},{3,1},{4,6},{5,7},{6,4},{7,5},{8,10},{9,11},{10,... | collective-permute-start | bytes 1769480 | tf_op jit(solution)/shard_map/ppermute | solution.py:594
  263.4 18.2 %collective-permute-start.26 = (bf16[256,1024]{1,0:T(8,128)(2,1)S(1)}, bf16[256,1024]{1,0:T(8,128)(2,1)S(1)}, u32[]{:S(2)}, u32[]{:S(2)}) collective-permute-start(bf16[256,1024]{1,0:T(8,128)(2,1)S(1)} %copy-done.67), channel_id=1, source_target_pairs={{0,4},{4,0},{8,12},{12,8},{16,20},{20,16},{24,28},{28,24},{1,5},{5... | collective-permute-start | bytes 1572872 | tf_op jit(solution)/shard_map/ppermute | solution.py:594
  263.4 24.9 %collective-permute-start.27 = (bf16[256,1024]{1,0:T(8,128)(2,1)S(1)}, bf16[256,1024]{1,0:T(8,128)(2,1)S(1)}, u32[]{:S(2)}, u32[]{:S(2)}) collective-permute-start(bf16[256,1024]{1,0:T(8,128)(2,1)S(1)} %copy-done.66), channel_id=1, source_target_pairs={{0,4},{4,0},{8,12},{12,8},{16,20},{20,16},{24,28},{28,24},{1,5},{5... | collective-permute-start | bytes 1572872 | tf_op jit(solution)/shard_map/ppermute | solution.py:594
  310.6 32.2 %all-to-all-start = ((bf16[8,32,1152]{2,1,0:T(8,128)(2,1)}), bf16[8,32,1152]{2,1,0:T(8,128)(2,1)}, u32[]{:S(2)}, u32[]{:S(2)}) async-start(bf16[8,32,1152]{2,1,0:T(8,128)(2,1)} %fusion.1), calls=%async_computation | async-start | bytes 1179648 | tf_op jit(solution)/shard_map/all_to_all | solution.py:923
  314.8 25.8 %collective-permute-start.37 = (bf16[1,8,32,1024]{3,2,1,0:T(8,128)(2,1)}, bf16[1,8,32,1024]{3,2,1,0:T(8,128)(2,1)S(1)}, u32[]{:S(2)}, u32[]{:S(2)}) collective-permute-start(bf16[1,8,32,1024]{3,2,1,0:T(8,128)(2,1)} %take_add.6), channel_id=1, source_target_pairs={{0,2},{1,3},{2,0},{3,1},{4,6},{5,7},{6,4},{7,5},{8,10},{9,11},{10,... | collective-permute-start | bytes 1572872 | tf_op jit(solution)/shard_map/ppermute | solution.py:594
  326.3 22.4 %collective-permute-start.32 = (bf16[2,8,32,1152]{3,2,1,0:T(8,128)(2,1)}, bf16[2,8,32,1152]{3,2,1,0:T(8,128)(2,1)}, u32[]{:S(2)}, u32[]{:S(2)}) collective-permute-start(bf16[2,8,32,1152]{3,2,1,0:T(8,128)(2,1)} %get-tuple-element.260), channel_id=1, source_target_pairs={{0,1},{1,0},{2,3},{3,2},{4,5},{5,4},{6,7},{7,6},{8,9},{9,8},{10,11... | collective-permute-start | bytes 3538952 | tf_op jit(solution)/shard_map/ppermute | solution.py:594
  326.3 24.4 %collective-permute-start.33 = (bf16[256,1024]{1,0:T(8,128)(2,1)}, bf16[256,1024]{1,0:T(8,128)(2,1)S(1)}, u32[]{:S(2)}, u32[]{:S(2)}) collective-permute-start(bf16[256,1024]{1,0:T(8,128)(2,1)} %get-tuple-element.261), channel_id=1, source_target_pairs={{0,4},{4,0},{8,12},{12,8},{16,20},{20,16},{24,28},{28,24},{1,5},{5... | collective-permute-start | bytes 1572872 | tf_op jit(solution)/shard_map/ppermute | solution.py:594
  328.1 26.5 %collective-permute-start.34 = (bf16[256,1024]{1,0:T(8,128)(2,1)}, bf16[256,1024]{1,0:T(8,128)(2,1)}, u32[]{:S(2)}, u32[]{:S(2)}) collective-permute-start(bf16[256,1024]{1,0:T(8,128)(2,1)} %get-tuple-element.262), channel_id=1, source_target_pairs={{0,4},{4,0},{8,12},{12,8},{16,20},{20,16},{24,28},{28,24},{1,5},{5... | collective-permute-start | bytes 1572872 | tf_op jit(solution)/shard_map/ppermute | solution.py:594
  329.2 25.3 %collective-permute-start.35 = (bf16[256,1024]{1,0:T(8,128)(2,1)}, bf16[256,1024]{1,0:T(8,128)(2,1)S(1)}, u32[]{:S(2)}, u32[]{:S(2)}) collective-permute-start(bf16[256,1024]{1,0:T(8,128)(2,1)} %add.90), channel_id=1, source_target_pairs={{0,24},{4,28},{8,0},{12,4},{16,8},{20,12},{24,16},{28,20},{1,25},{... | collective-permute-start | bytes 1572872 | tf_op jit(solution)/shard_map/ppermute | solution.py:620
  342.8 22.4 %all-to-all-start.1 = ((bf16[8,32,1024]{2,1,0:T(8,128)(2,1)}), bf16[8,32,1024]{2,1,0:T(8,128)(2,1)}, u32[]{:S(2)}, u32[]{:S(2)}) async-start(bf16[8,32,1024]{2,1,0:T(8,128)(2,1)} %fusion.2), calls=%async_computation.1 | async-start | bytes 1048576 | tf_op jit(solution)/shard_map/all_to_all | solution.py:923
  354.6 18.2 %collective-permute-start.36 = (bf16[1,8,32,1152]{3,2,1,0:T(8,128)(2,1)}, bf16[1,8,32,1152]{3,2,1,0:T(8,128)(2,1)}, u32[]{:S(2)}, u32[]{:S(2)}) collective-permute-start(bf16[1,8,32,1152]{3,2,1,0:T(8,128)(2,1)} %take_add.7), channel_id=1, source_target_pairs={{0,2},{1,3},{2,0},{3,1},{4,6},{5,7},{6,4},{7,5},{8,10},{9,11},{10,... | collective-permute-start | bytes 1769480 | tf_op jit(solution)/shard_map/ppermute | solution.py:594
  357.1 23.4 %collective-permute-start.38 = (bf16[256,1024]{1,0:T(8,128)(2,1)S(1)}, bf16[256,1024]{1,0:T(8,128)(2,1)}, u32[]{:S(2)}, u32[]{:S(2)}) collective-permute-start(bf16[256,1024]{1,0:T(8,128)(2,1)S(1)} %add.93), channel_id=1, source_target_pairs={{0,24},{4,28},{8,0},{12,4},{16,8},{20,12},{24,16},{28,20},{1,25},{... | collective-permute-start | bytes 1572872 | tf_op jit(solution)/shard_map/ppermute | solution.py:620
  365.0 20.4 %collective-permute-start.39 = (bf16[256,1024]{1,0:T(8,128)(2,1)}, bf16[256,1024]{1,0:T(8,128)(2,1)}, u32[]{:S(2)}, u32[]{:S(2)}) collective-permute-start(bf16[256,1024]{1,0:T(8,128)(2,1)} %add.94), channel_id=1, source_target_pairs={{0,8},{4,12},{8,16},{12,20},{16,24},{20,28},{24,0},{28,4},{1,9},{5... | collective-permute-start | bytes 1572872 | tf_op jit(solution)/shard_map/ppermute | solution.py:620
  375.0 21.9 %all-to-all-start.2 = ((bf16[8,32,1152]{2,1,0:T(8,128)(2,1)}), bf16[8,32,1152]{2,1,0:T(8,128)(2,1)S(1)}, u32[]{:S(2)}, u32[]{:S(2)}) async-start(bf16[8,32,1152]{2,1,0:T(8,128)(2,1)} %fusion), calls=%async_computation.2 | async-start | bytes 1179648 | tf_op jit(solution)/shard_map/all_to_all | solution.py:1001
  (82 other events, 693.7 us)
Sparse Core Ops, SparseCore 0:
  35.4 81.3 all-gather.2
  195.8 59.9 reduce-scatter.2
  308.7 56.2 reduce-scatter.4

commit v3 on v2

--- a/solution.py
+++ b/solution.py
@@ -80,8 +80,11 @@
     earlier = dot(jnp.where(row > col, 1.0, 0.0).astype(bf16), named.astype(bf16), 1, 0)
     code = jnp.where(named > 0.0, jnp.where(earlier < CAP, earlier, -1.0), -2.0)
     out[:tokens, :] = cot[...]
-    out[tokens:, :tokens] = code.T[:EXPERTS].astype(bf16)
-    out[tokens:, tokens:] = jnp.zeros((EXPERTS, width - tokens), bf16)
+    rows = code.T.astype(bf16)
+    half = EXPERTS // 2
+    out[tokens:, :tokens] = rows[:half]
+    out[tokens:, tokens : 2 * tokens] = rows[half:EXPERTS]
+    out[tokens:, 2 * tokens :] = jnp.zeros((half, width - 2 * tokens), bf16)
 
 
 def project_kv_body(place, x, gain, wk, wv, spectrum, seg, kv_out, n_out, c_out, s_out):
@@ -329,7 +332,9 @@
         def _(b=b):
             for load in loads(b):
                 load.wait()
-            code = c_s[b, tokens:, :tokens].astype(f32)
+            code = jnp.concatenate(
+                [c_s[b, tokens:, :tokens], c_s[b, tokens:, tokens : 2 * tokens]], 0
+            ).astype(f32)
             s_t[b] = code
             g_t[b] = gates_of(
                 dot(router[...], x_s[b], 1, 1), jnp.where(code > -1.5, 1.0, 0.0), 0
@@ -511,7 +516,7 @@
         + [pl.BlockSpec((1, blocks, 1, tokens), lambda e: (e, 0, 0, 0)), SMEM],
         scratch_shapes=[
             pltpu.VMEM((blocks, tokens, width), bf16),
-            pltpu.VMEM((blocks, tokens + EXPERTS, width), bf16),
+            pltpu.VMEM((blocks, tokens + EXPERTS // 2, width), bf16),
             pltpu.VMEM((blocks, EXPERTS, tokens), f32),
             pltpu.VMEM((blocks, EXPERTS, tokens), f32),
             pltpu.VMEM((room, width), bf16),
@@ -766,7 +771,7 @@
 
     grad_rows = call(
         route_body,
-        struct((tokens + EXPERTS, width)),
+        struct((tokens + EXPERTS // 2, width)),
         (routes, cotangent),
         name="route",
         flops=10**6,

time: 411 us -> 413 us (level); the launches traced: 405 us -> 412 us
  waiting for transfers between devices: 131 us -> 138 us
  Pallas kernels: 143 us -> 137 us
  starting transfers between devices: 68 us -> 73.4 us
    ppermute x12, waiting for transfers between devices: 67.6 us -> 75.9 us  [shift(): lax.ppermute(values, 'expert', [(i, (i + 2 * by) % n) for i in range(n)])]
    ppermute x12, starting transfers between devices: 30.4 us -> 34.8 us  [shift(): lax.ppermute(values, 'expert', [(i, (i + 2 * by) % n) for i in range(n)])]
    pallas_call x1, Pallas kernels: 47.3 us -> 43.1 us  [expert_call(): pl.pallas_call(functools.partial(expert_body, blocks, tokens), grid=(loca...]
    unnamed x138 -> x136, local copies, waits for them, and re-layouts: 25 us -> 24.5 us
  transfers between devices with their start and end apart: 46 -> 46, of which waited for: 21 -> 22; matrix products, arithmetic and copies ran while one was open for 6% -> 6% of each run, Pallas kernels for 23% -> 23%
where the time goes in v3:
time: 413 us; the launch traced here: 412 us
  waiting for transfers between devices  138 us (33%)
  Pallas kernels  137 us (33%)
  starting transfers between devices  73.4 us (18%)
  local copies, waits for them, and re-layouts  31.7 us (8%)
  other arithmetic  16.5 us (4%)
  between operations  14.7 us (4%)
    ppermute x12, waiting for transfers between devices, shift(): lax.ppermute(values, 'expert', [(i, (i + 2 * by) % n) for i in range(n)])  75.9 us
    pallas_call x21, Pallas kernels, call(): pl.pallas_call(body, out_shape=outs, in_specs=[SMEM] * smem + [VMEM] * (l...  64.8 us
    ppermute x28, waiting for transfers between devices, flip(): return lax.ppermute(values, axis, [(i, i ^ bit) for i in range(n)])  59.9 us
    pallas_call x1, Pallas kernels, expert_call(): pl.pallas_call(functools.partial(expert_body, blocks, tokens), grid=(loca...  43.1 us
    ppermute x12, starting transfers between devices, shift(): lax.ppermute(values, 'expert', [(i, (i + 2 * by) % n) for i in range(n)])  34.8 us
    unnamed x136, local copies, waits for them, and re-layouts  24.5 us
    ppermute x28, starting transfers between devices, flip(): return lax.ppermute(values, axis, [(i, i ^ bit) for i in range(n)])  22.9 us
    pallas_call x1, Pallas kernels, split_grads_of(): pl.pallas_call(functools.partial(expert_grad_split_body, first), grid=(nu...  11.7 us
  transfers between devices with their start and end apart: 46, of which 22 were waited for; matrix products, arithmetic and copies ran while one was open for 6% of the time, Pallas kernels for 23%

profile of v3, /device:TPU:0, one launch (start us, length us, event | category | flops | bytes accessed | tf_op | source)
XLA Modules:
  0.0 411.6 jit_solution(17546153626785570242)
XLA Ops:
  21.6 3.2 pad_maximum_fusion
  24.8 9.8 %collective-permute-done.1.refs_9_ = bf16[272,1024]{1,0:T(8,128)(2,1)} collective-permute-done((bf16[272,1024]{1,0:T(8,128)(2,1)S(1)}, bf16[272,1024]{1,0:T(8,128)(2,1)}, u32[]{:S(2)}, u32[]{:S(2)}) %collective-permute-start.1) | collective-permute-done | bytes 557088 | tf_op jit(solution)/shard_map/ppermute | solution.py:625
  39.2 10.3 %collective-permute-done.6.refs_11_ = bf16[272,1024]{1,0:T(8,128)(2,1)} collective-permute-done((bf16[272,1024]{1,0:T(8,128)(2,1)S(1)}, bf16[272,1024]{1,0:T(8,128)(2,1)}, u32[]{:S(2)}, u32[]{:S(2)}) %collective-permute-start.6) | collective-permute-done | bytes 557088 | tf_op jit(solution)/shard_map/ppermute | solution.py:625
  51.1 10.0 %collective-permute-done.5.refs_10_ = bf16[272,1024]{1,0:T(8,128)(2,1)} collective-permute-done((bf16[272,1024]{1,0:T(8,128)(2,1)}, bf16[272,1024]{1,0:T(8,128)(2,1)}, u32[]{:S(2)}, u32[]{:S(2)}) %collective-permute-start.5) | collective-permute-done | bytes 557088 | tf_op jit(solution)/shard_map/ppermute | solution.py:625
  69.0 14.0 %attend.1 = (f32[256,1024]{1,0:T(8,128)S(1)}, bf16[256,1024]{1,0:T(8,128)(2,1)S(1)}, bf16[256,1024]{1,0:T(8,128)(2,1)S(1)}, f32[256,128]{1,0:T(8,128)S(1)}, f32[256,128]{1,0:T(8,128)S(1)}) custom-call(s32[4]{0:T(128)S(1)} %pad_add_fusion.places, bf16[256,1024]{1,0:T(8,128)(2,1)S(1)} %copy-done.3, bf16[256,1024]{1,0:T(8,128)(2,1)S(1)} %project_q.1.q, ...), custom_call_target="tpu_custom_call" | custom-call | flops 1000000 | bytes 10000 | tf_op jit(solution)/shard_map/attend/pallas_call | solution.py:60
  87.4 3.3 collective-permute-start.13
  90.6 12.3 %collective-permute-done.9.refs_1_ = bf16[256,1024]{1,0:T(8,128)(2,1)} collective-permute-done((bf16[256,1024]{1,0:T(8,128)(2,1)S(1)}, bf16[256,1024]{1,0:T(8,128)(2,1)}, u32[]{:S(2)}, u32[]{:S(2)}) %collective-permute-start.9) | collective-permute-done | bytes 524320 | tf_op jit(solution)/shard_map/ppermute | solution.py:625
  103.0 7.5 %collective-permute-start.12 = (bf16[256,1024]{1,0:T(8,128)(2,1)}, bf16[256,1024]{1,0:T(8,128)(2,1)}, u32[]{:S(2)}, u32[]{:S(2)}) collective-permute-start(bf16[256,1024]{1,0:T(8,128)(2,1)} %collective-permute-done.9.refs_1_), channel_id=1, source_target_pairs={{0,8},{4,12},{8,16},{12,20},{16,24},{20,28},{24,0},{28,4},{1,9},{5... | collective-permute-start | bytes 1572872 | tf_op jit(solution)/shard_map/ppermute | solution.py:625
  114.8 8.4 %collective-permute-done.12.refs_2_ = bf16[256,1024]{1,0:T(8,128)(2,1)} collective-permute-done((bf16[256,1024]{1,0:T(8,128)(2,1)}, bf16[256,1024]{1,0:T(8,128)(2,1)}, u32[]{:S(2)}, u32[]{:S(2)}) %collective-permute-start.12) | collective-permute-done | bytes 524320 | tf_op jit(solution)/shard_map/ppermute | solution.py:625
  124.1 11.2 %collective-permute-done.16.refs_7_ = bf16[256,1024]{1,0:T(8,128)(2,1)} collective-permute-done((bf16[256,1024]{1,0:T(8,128)(2,1)}, bf16[256,1024]{1,0:T(8,128)(2,1)}, u32[]{:S(2)}, u32[]{:S(2)}) %collective-permute-start.16) | collective-permute-done | bytes 524320 | tf_op jit(solution)/shard_map/ppermute | solution.py:599
  135.3 7.1 %collective-permute-done.15.refs_6_ = bf16[256,1024]{1,0:T(8,128)(2,1)} collective-permute-done((bf16[256,1024]{1,0:T(8,128)(2,1)}, bf16[256,1024]{1,0:T(8,128)(2,1)}, u32[]{:S(2)}, u32[]{:S(2)}) %collective-permute-start.15) | collective-permute-done | bytes 524320 | tf_op jit(solution)/shard_map/ppermute | solution.py:599
  142.4 43.1 %experts.1 = (bf16[256,1152]{1,0:T(8,128)(2,1)}, bf16[256,1152]{1,0:T(8,128)(2,1)}, bf16[256,1152]{1,0:T(8,128)(2,1)}, bf16[256,1152]{1,0:T(8,128)(2,1)}, bf16[2...) custom-call(s32[1]{0:T(128)} %bitcast.7.base, ...), custom_call_target="tpu_custom_call" | custom-call | flops 1000000 | bytes 10000 | tf_op jit(solution)/shard_map/experts/pallas_call | solution.py:502
  185.7 9.0 %expert_grads.2 = bf16[4,2,3,128,1024]{4,3,2,1,0:T(8,128)(2,1)} custom-call(s32[4,9]{1,0:T(4,128)} %get-tuple-element.177.offs, bf16[4,1280,1536]{2,1,0:T(8,128)(2,1)} %get-tuple-element.185.acts, bf16[4,1280,1024]{2,1,0:T(8,128)(2,1)} %get-tuple-element.179.xg, bf16[4,1280,1024]{2,1,0:T(8,128)(2,1)} %get-tuple-element.180.pg), custom_call_target="tpu_custom_call" | custom-call | flops 1000000 | bytes 10000 | tf_op jit(solution)/shard_map/expert_grads/pallas_call | solution.py:544
  205.0 11.7 %expert_grads.3 = (bf16[2,2,3,128,1024]{4,3,2,1,0:T(8,128)(2,1)}, bf16[2,2,3,128,1024]{4,3,2,1,0:T(8,128)(2,1)}) custom-call(s32[1]{0:T(128)} %bitcast.me, s32[4,9]{1,0:T(4,128)} %get-tuple-element.177.offs, bf16[4,1280,1536]{2,1,0:T(8,128)(2,1)} %get-tuple-element.185.acts, bf16[4,1280,1024]{2,1,0:T(8,128)(2,1)} %get-tuple-element.179.xg, ...), custom_call_target="tpu_custom_call" | custom-call | flops 1000000 | bytes 10000 | tf_op jit(solution)/shard_map/expert_grads/pallas_call | solution.py:562
  221.0 6.3 %collective-permute-start.21 = (bf16[256,1152]{1,0:T(8,128)(2,1)}, bf16[256,1152]{1,0:T(8,128)(2,1)}, u32[]{:S(2)}, u32[]{:S(2)}) collective-permute-start(bf16[256,1152]{1,0:T(8,128)(2,1)} %add.87), channel_id=1, source_target_pairs={{0,24},{4,28},{8,0},{12,4},{16,8},{20,12},{24,16},{28,20},{1,25},{... | collective-permute-start | bytes 1769480 | tf_op jit(solution)/shard_map/ppermute | solution.py:625
  227.3 7.9 %expert_sum.1 = (bf16[256,1024]{1,0:T(8,128)(2,1)}, bf16[256,1024]{1,0:T(8,128)(2,1)}, bf16[256,1024]{1,0:T(8,128)(2,1)}, bf16[256,1024]{1,0:T(8,128)(2,1)}, bf1...) custom-call(s32[4,9]{1,0:T(4,128)} %get-tuple-element.177.offs, ...), custom_call_target="tpu_custom_call" | custom-call | flops 1000000 | bytes 10000 | tf_op jit(solution)/shard_map/expert_sum/pallas_call | solution.py:60
  235.2 6.1 %collective-permute-done.21.refs_1_ = bf16[256,1152]{1,0:T(8,128)(2,1)} collective-permute-done((bf16[256,1152]{1,0:T(8,128)(2,1)}, bf16[256,1152]{1,0:T(8,128)(2,1)}, u32[]{:S(2)}, u32[]{:S(2)}) %collective-permute-start.21) | collective-permute-done | bytes 589856 | tf_op jit(solution)/shard_map/ppermute | solution.py:625
  246.4 11.6 %collective-permute-done.23.refs_2_ = bf16[256,1152]{1,0:T(8,128)(2,1)S(1)} collective-permute-done((bf16[256,1152]{1,0:T(8,128)(2,1)S(1)}, bf16[256,1152]{1,0:T(8,128)(2,1)S(1)}, u32[]{:S(2)}, u32[]{:S(2)}) %collective-permute-start.23) | collective-permute-done | bytes 589856 | tf_op jit(solution)/shard_map/ppermute | solution.py:625
  271.0 16.1 %attention_back.1 = (bf16[256,1024]{1,0:T(8,128)(2,1)S(1)}, bf16[2,256,1024]{2,1,0:T(8,128)(2,1)S(1)}, bf16[2,256,1024]{2,1,0:T(8,128)(2,1)S(1)}) custom-call(s32[4]{0:T(128)S(1)} %pad_add_fusion.places, bf16[256,1024]{1,0:T(8,128)(2,1)S(1)} %get-tuple-element.240.do_s, bf16[256,1024]{1,0:T(8,128)(2,1)S(1)} %copy-done.5, ...), custom_call_target="tpu_custom_call" | custom-call | flops 1000000 | bytes 10000 | tf_op jit(solution)/shard_map/attention_back/pallas_call | solution.py:60
  287.2 6.7 %collective-permute-done.27.b = bf16[256,1024]{1,0:T(8,128)(2,1)S(1)} collective-permute-done((bf16[256,1024]{1,0:T(8,128)(2,1)S(1)}, bf16[256,1024]{1,0:T(8,128)(2,1)S(1)}, u32[]{:S(2)}, u32[]{:S(2)}) %collective-permute-start.27) | collective-permute-done | bytes 524320 | tf_op jit(solution)/shard_map/ppermute | solution.py:599
  301.2 4.4 %all_add.1 = bf16[2,2,3,128,1024]{4,3,2,1,0:T(8,128)(2,1)} custom-call(bf16[2,2,3,128,1024]{4,3,2,1,0:T(8,128)(2,1)} %get-tuple-element.253.a, bf16[2,2,3,128,1024]{4,3,2,1,0:T(8,128)(2,1)} %collective-permute-done.31.b), custom_call_target="tpu_custom_call" | custom-call | flops 1000000 | bytes 10000 | tf_op jit(solution)/shard_map/all_add/pallas_call | solution.py:660
  308.8 5.2 %collective-permute-done.29.far = bf16[1,256,1024]{2,1,0:T(8,128)(2,1)} collective-permute-done((bf16[1,256,1024]{2,1,0:T(8,128)(2,1)S(1)}, bf16[1,256,1024]{2,1,0:T(8,128)(2,1)}, u32[]{:S(2)}, u32[]{:S(2)}) %collective-permute-start.29) | collective-permute-done | bytes 524320 | tf_op jit(solution)/shard_map/ppermute | solution.py:599
  316.1 4.2 %all-to-all-start = ((bf16[8,32,1152]{2,1,0:T(8,128)(2,1)}), bf16[8,32,1152]{2,1,0:T(8,128)(2,1)}, u32[]{:S(2)}, u32[]{:S(2)}) async-start(bf16[8,32,1152]{2,1,0:T(8,128)(2,1)} %fusion.1), calls=%async_computation | async-start | bytes 1179648 | tf_op jit(solution)/shard_map/all_to_all | solution.py:928
  321.9 6.2 %finish.1 = (bf16[256,1024]{1,0:T(8,128)(2,1)}, bf16[256,1024]{1,0:T(8,128)(2,1)}, bf16[256,1024]{1,0:T(8,128)(2,1)}) custom-call(bf16[2,256,1024]{2,1,0:T(8,128)(2,1)} %copy-done.11, bf16[2,256,1024]{2,1,0:T(8,128)(2,1)} %copy-done.12, bf16[1,256,1024]{2,1,0:T(8,128)(2,1)} %collective-permute-done.29.far, bf16[256,1024]{1,0:T(8,128)(2,1)} %copy-done.25, ...), custom_call_target="tpu_custom_call" | custom-call | flops 1000000 | bytes 10000 | tf_op jit(solution)/shard_map/finish/pallas_call | solution.py:60
  335.3 3.7 collective-permute-start.35
  338.9 7.2 %collective-permute-done.37 = bf16[1,8,32,1024]{3,2,1,0:T(8,128)(2,1)S(1)} collective-permute-done((bf16[1,8,32,1024]{3,2,1,0:T(8,128)(2,1)}, bf16[1,8,32,1024]{3,2,1,0:T(8,128)(2,1)S(1)}, u32[]{:S(2)}, u32[]{:S(2)}) %collective-permute-start.37) | collective-permute-done | bytes 524320 | tf_op jit(solution)/shard_map/ppermute | solution.py:599
  348.2 5.9 %all-to-all-start.1 = ((bf16[8,32,1024]{2,1,0:T(8,128)(2,1)}), bf16[8,32,1024]{2,1,0:T(8,128)(2,1)}, u32[]{:S(2)}, u32[]{:S(2)}) async-start(bf16[8,32,1024]{2,1,0:T(8,128)(2,1)} %fusion.2), calls=%async_computation.1 | async-start | bytes 1048576 | tf_op jit(solution)/shard_map/all_to_all | solution.py:928
  356.2 4.6 %collective-permute-done.34.b = bf16[256,1024]{1,0:T(8,128)(2,1)} collective-permute-done((bf16[256,1024]{1,0:T(8,128)(2,1)}, bf16[256,1024]{1,0:T(8,128)(2,1)}, u32[]{:S(2)}, u32[]{:S(2)}) %collective-permute-start.34) | collective-permute-done | bytes 524320 | tf_op jit(solution)/shard_map/ppermute | solution.py:599
  362.2 5.8 %collective-permute-start.38 = (bf16[256,1024]{1,0:T(8,128)(2,1)S(1)}, bf16[256,1024]{1,0:T(8,128)(2,1)}, u32[]{:S(2)}, u32[]{:S(2)}) collective-permute-start(bf16[256,1024]{1,0:T(8,128)(2,1)S(1)} %add.93), channel_id=1, source_target_pairs={{0,24},{4,28},{8,0},{12,4},{16,8},{20,12},{24,16},{28,20},{1,25},{... | collective-permute-start | bytes 1572872 | tf_op jit(solution)/shard_map/ppermute | solution.py:625
  372.0 6.7 %collective-permute-done.36 = bf16[1,8,32,1152]{3,2,1,0:T(8,128)(2,1)} collective-permute-done((bf16[1,8,32,1152]{3,2,1,0:T(8,128)(2,1)}, bf16[1,8,32,1152]{3,2,1,0:T(8,128)(2,1)}, u32[]{:S(2)}, u32[]{:S(2)}) %collective-permute-start.36) | collective-permute-done | bytes 589856 | tf_op jit(solution)/shard_map/ppermute | solution.py:599
  381.1 5.5 %all-to-all-start.2 = ((bf16[8,32,1152]{2,1,0:T(8,128)(2,1)}), bf16[8,32,1152]{2,1,0:T(8,128)(2,1)S(1)}, u32[]{:S(2)}, u32[]{:S(2)}) async-start(bf16[8,32,1152]{2,1,0:T(8,128)(2,1)} %fusion), calls=%async_computation.2 | async-start | bytes 1179648 | tf_op jit(solution)/shard_map/all_to_all | solution.py:1006
  386.6 5.2 %collective-permute-done.39 = bf16[256,1024]{1,0:T(8,128)(2,1)} collective-permute-done((bf16[256,1024]{1,0:T(8,128)(2,1)}, bf16[256,1024]{1,0:T(8,128)(2,1)}, u32[]{:S(2)}, u32[]{:S(2)}) %collective-permute-start.39) | collective-permute-done | bytes 524320 | tf_op jit(solution)/shard_map/ppermute | solution.py:625
  (250 shorter events, 116.8 us)
Async XLA Ops:
  7.2 135.2 %all-gather.3.cloned.1.call-start = ((), (), s32[]{:S(2)}) async-start(), calls=%async_computation.7 | async-start | bytes 15728640 | tf_op jit(solution)/shard_map/all_gather | solution.py:815
  14.7 19.8 %collective-permute-start = (bf16[256,1152]{1,0:T(8,128)(2,1)S(1)}, bf16[256,1152]{1,0:T(8,128)(2,1)}, u32[]{:S(2)}, u32[]{:S(2)}) collective-permute-start(bf16[256,1152]{1,0:T(8,128)(2,1)S(1)} %get-tuple-element.154.refs_0_), channel_id=1, source_target_pairs={{0,2},{1,3},{2,0},{3,1},{4,6},{5,7},{6,4},{7,5},{8,10},{9,11},{10,... | collective-permute-start | bytes 1769480 | tf_op jit(solution)/shard_map/ppermute | solution.py:599
  34.6 279.5 %reduce-scatter.3.cloned.1.call-start = ((), (), s32[]{:S(2)}) async-start(), calls=%async_computation.5 | async-start | bytes 7864320 | tf_op jit(solution)/shard_map/reduce_scatter | solution.py:864
  36.4 24.6 %collective-permute-start.5 = (bf16[272,1024]{1,0:T(8,128)(2,1)}, bf16[272,1024]{1,0:T(8,128)(2,1)}, u32[]{:S(2)}, u32[]{:S(2)}) collective-permute-start(bf16[272,1024]{1,0:T(8,128)(2,1)} %collective-permute-done.1.refs_9_), channel_id=1, source_target_pairs={{0,8},{4,12},{8,16},{12,20},{16,24},{20,28},{24,0},{28,4},{1,9},{5... | collective-permute-start | bytes 1671176 | tf_op jit(solution)/shard_map/ppermute | solution.py:625
  37.2 31.7 %collective-permute-start.3 = (bf16[256,1152]{1,0:T(8,128)(2,1)S(1)}, bf16[256,1152]{1,0:T(8,128)(2,1)}, u32[]{:S(2)}, u32[]{:S(2)}) collective-permute-start(bf16[256,1152]{1,0:T(8,128)(2,1)S(1)} %get-tuple-element.154.refs_0_), channel_id=1, source_target_pairs={{0,1},{1,0},{2,3},{3,2},{4,5},{5,4},{6,7},{7,6},{8,9},{9,8},{10,11... | collective-permute-start | bytes 1769480 | tf_op jit(solution)/shard_map/ppermute | solution.py:599
  37.2 31.8 %collective-permute-start.4 = (bf16[256,1152]{1,0:T(8,128)(2,1)}, bf16[256,1152]{1,0:T(8,128)(2,1)}, u32[]{:S(2)}, u32[]{:S(2)}) collective-permute-start(bf16[256,1152]{1,0:T(8,128)(2,1)} %collective-permute-done.refs_1_), channel_id=1, source_target_pairs={{0,1},{1,0},{2,3},{3,2},{4,5},{5,4},{6,7},{7,6},{8,9},{9,8},{10,11... | collective-permute-start | bytes 1769480 | tf_op jit(solution)/shard_map/ppermute | solution.py:599
  37.7 48.4 %collective-permute-start.7 = (bf16[272,1024]{1,0:T(8,128)(2,1)}, bf16[272,1024]{1,0:T(8,128)(2,1)}, u32[]{:S(2)}, u32[]{:S(2)}) collective-permute-start(bf16[272,1024]{1,0:T(8,128)(2,1)} %collective-permute-done.1.refs_9_), channel_id=1, source_target_pairs={{0,4},{4,0},{8,12},{12,8},{16,20},{20,16},{24,28},{28,24},{1,5},{5... | collective-permute-start | bytes 1671176 | tf_op jit(solution)/shard_map/ppermute | solution.py:599
  49.5 36.6 %collective-permute-start.8 = (bf16[272,1024]{1,0:T(8,128)(2,1)}, bf16[272,1024]{1,0:T(8,128)(2,1)}, u32[]{:S(2)}, u32[]{:S(2)}) collective-permute-start(bf16[272,1024]{1,0:T(8,128)(2,1)} %collective-permute-done.6.refs_11_), channel_id=1, source_target_pairs={{0,4},{4,0},{8,12},{12,8},{16,20},{20,16},{24,28},{28,24},{1,5},{5... | collective-permute-start | bytes 1671176 | tf_op jit(solution)/shard_map/ppermute | solution.py:599
  61.1 29.6 %collective-permute-start.11 = (bf16[272,1024]{1,0:T(8,128)(2,1)}, bf16[272,1024]{1,0:T(8,128)(2,1)}, u32[]{:S(2)}, u32[]{:S(2)}) collective-permute-start(bf16[272,1024]{1,0:T(8,128)(2,1)} %collective-permute-done.5.refs_10_), channel_id=1, source_target_pairs={{0,4},{4,0},{8,12},{12,8},{16,20},{20,16},{24,28},{28,24},{1,5},{5... | collective-permute-start | bytes 1671176 | tf_op jit(solution)/shard_map/ppermute | solution.py:599
  86.1 16.8 %collective-permute-start.9 = (bf16[256,1024]{1,0:T(8,128)(2,1)S(1)}, bf16[256,1024]{1,0:T(8,128)(2,1)}, u32[]{:S(2)}, u32[]{:S(2)}) collective-permute-start(bf16[256,1024]{1,0:T(8,128)(2,1)S(1)} %get-tuple-element.161.refs_0_), channel_id=1, source_target_pairs={{0,8},{4,12},{8,16},{12,20},{16,24},{20,28},{24,0},{28,4},{1,9},{5... | collective-permute-start | bytes 1572872 | tf_op jit(solution)/shard_map/ppermute | solution.py:625
  87.4 25.5 %collective-permute-start.13 = (bf16[256,1024]{1,0:T(8,128)(2,1)S(1)}, bf16[256,1024]{1,0:T(8,128)(2,1)}, u32[]{:S(2)}, u32[]{:S(2)}) collective-permute-start(bf16[256,1024]{1,0:T(8,128)(2,1)S(1)} %get-tuple-element.161.refs_0_), channel_id=1, source_target_pairs={{0,24},{4,28},{8,0},{12,4},{16,8},{20,12},{24,16},{28,20},{1,25},{... | collective-permute-start | bytes 1572872 | tf_op jit(solution)/shard_map/ppermute | solution.py:625
  103.0 20.1 %collective-permute-start.12 = (bf16[256,1024]{1,0:T(8,128)(2,1)}, bf16[256,1024]{1,0:T(8,128)(2,1)}, u32[]{:S(2)}, u32[]{:S(2)}) collective-permute-start(bf16[256,1024]{1,0:T(8,128)(2,1)} %collective-permute-done.9.refs_1_), channel_id=1, source_target_pairs={{0,8},{4,12},{8,16},{12,20},{16,24},{20,28},{24,0},{28,4},{1,9},{5... | collective-permute-start | bytes 1572872 | tf_op jit(solution)/shard_map/ppermute | solution.py:625
  112.9 22.5 %collective-permute-start.16 = (bf16[256,1024]{1,0:T(8,128)(2,1)}, bf16[256,1024]{1,0:T(8,128)(2,1)}, u32[]{:S(2)}, u32[]{:S(2)}) collective-permute-start(bf16[256,1024]{1,0:T(8,128)(2,1)} %collective-permute-done.13.refs_3_), channel_id=1, source_target_pairs={{0,4},{4,0},{8,12},{12,8},{16,20},{20,16},{24,28},{28,24},{1,5},{5... | collective-permute-start | bytes 1572872 | tf_op jit(solution)/shard_map/ppermute | solution.py:599
  123.1 19.3 %collective-permute-start.15 = (bf16[256,1024]{1,0:T(8,128)(2,1)}, bf16[256,1024]{1,0:T(8,128)(2,1)}, u32[]{:S(2)}, u32[]{:S(2)}) collective-permute-start(bf16[256,1024]{1,0:T(8,128)(2,1)} %collective-permute-done.12.refs_2_), channel_id=1, source_target_pairs={{0,4},{4,0},{8,12},{12,8},{16,20},{20,16},{24,28},{28,24},{1,5},{5... | collective-permute-start | bytes 1572872 | tf_op jit(solution)/shard_map/ppermute | solution.py:599
  197.1 199.0 %reduce-scatter.5.cloned.1.call-start = ((), (), s32[]{:S(2)}) async-start(), calls=%async_computation.6 | async-start | bytes 4718592 | tf_op jit(solution)/shard_map/reduce_scatter | solution.py:967
  221.0 20.4 %collective-permute-start.21 = (bf16[256,1152]{1,0:T(8,128)(2,1)}, bf16[256,1152]{1,0:T(8,128)(2,1)}, u32[]{:S(2)}, u32[]{:S(2)}) collective-permute-start(bf16[256,1152]{1,0:T(8,128)(2,1)} %add.87), channel_id=1, source_target_pairs={{0,24},{4,28},{8,0},{12,4},{16,8},{20,12},{24,16},{28,20},{1,25},{... | collective-permute-start | bytes 1769480 | tf_op jit(solution)/shard_map/ppermute | solution.py:625
  227.3 16.5 %collective-permute-start.20 = (bf16[256,1152]{1,0:T(8,128)(2,1)}, bf16[256,1152]{1,0:T(8,128)(2,1)}, u32[]{:S(2)}, u32[]{:S(2)}) collective-permute-start(bf16[256,1152]{1,0:T(8,128)(2,1)} %get-tuple-element.190), channel_id=1, source_target_pairs={{0,4},{4,0},{8,12},{12,8},{16,20},{20,16},{24,28},{28,24},{1,5},{5... | collective-permute-start | bytes 1769480 | tf_op jit(solution)/shard_map/ppermute | solution.py:599
  264.6 36.6 %collective-permute-start.31 = (bf16[2,2,3,128,1024]{4,3,2,1,0:T(8,128)(2,1)S(1)}, bf16[2,2,3,128,1024]{4,3,2,1,0:T(8,128)(2,1)}, u32[]{:S(2)}, u32[]{:S(2)}) collective-permute-start(bf16[2,2,3,128,1024]{4,3,2,1,0:T(8,128)(2,1)S(1)} %copy-done.64), channel_id=1, source_target_pairs={{0,1},{1,0},{2,3},{3,2},{4,5},{5,4},{6,7},{7,6},{8,9},{9,8},{10,11... | collective-permute-start | bytes 9437192 | tf_op jit(solution)/shard_map/ppermute | solution.py:599
  268.3 25.5 %collective-permute-start.25 = (bf16[1,8,32,1152]{3,2,1,0:T(8,128)(2,1)S(1)}, bf16[1,8,32,1152]{3,2,1,0:T(8,128)(2,1)S(1)}, u32[]{:S(2)}, u32[]{:S(2)}) collective-permute-start(bf16[1,8,32,1152]{3,2,1,0:T(8,128)(2,1)S(1)} %take_add.4), channel_id=1, source_target_pairs={{0,2},{1,3},{2,0},{3,1},{4,6},{5,7},{6,4},{7,5},{8,10},{9,11},{10,... | collective-permute-start | bytes 1769480 | tf_op jit(solution)/shard_map/ppermute | solution.py:599
  268.9 18.2 %collective-permute-start.26 = (bf16[256,1024]{1,0:T(8,128)(2,1)S(1)}, bf16[256,1024]{1,0:T(8,128)(2,1)S(1)}, u32[]{:S(2)}, u32[]{:S(2)}) collective-permute-start(bf16[256,1024]{1,0:T(8,128)(2,1)S(1)} %copy-done.66), channel_id=1, source_target_pairs={{0,4},{4,0},{8,12},{12,8},{16,20},{20,16},{24,28},{28,24},{1,5},{5... | collective-permute-start | bytes 1572872 | tf_op jit(solution)/shard_map/ppermute | solution.py:599
  269.5 24.4 %collective-permute-start.27 = (bf16[256,1024]{1,0:T(8,128)(2,1)S(1)}, bf16[256,1024]{1,0:T(8,128)(2,1)S(1)}, u32[]{:S(2)}, u32[]{:S(2)}) collective-permute-start(bf16[256,1024]{1,0:T(8,128)(2,1)S(1)} %copy-done.65), channel_id=1, source_target_pairs={{0,4},{4,0},{8,12},{12,8},{16,20},{20,16},{24,28},{28,24},{1,5},{5... | collective-permute-start | bytes 1572872 | tf_op jit(solution)/shard_map/ppermute | solution.py:599
  316.1 32.1 %all-to-all-start = ((bf16[8,32,1152]{2,1,0:T(8,128)(2,1)}), bf16[8,32,1152]{2,1,0:T(8,128)(2,1)}, u32[]{:S(2)}, u32[]{:S(2)}) async-start(bf16[8,32,1152]{2,1,0:T(8,128)(2,1)} %fusion.1), calls=%async_computation | async-start | bytes 1179648 | tf_op jit(solution)/shard_map/all_to_all | solution.py:928
  320.3 25.8 %collective-permute-start.37 = (bf16[1,8,32,1024]{3,2,1,0:T(8,128)(2,1)}, bf16[1,8,32,1024]{3,2,1,0:T(8,128)(2,1)S(1)}, u32[]{:S(2)}, u32[]{:S(2)}) collective-permute-start(bf16[1,8,32,1024]{3,2,1,0:T(8,128)(2,1)} %take_add.6), channel_id=1, source_target_pairs={{0,2},{1,3},{2,0},{3,1},{4,6},{5,7},{6,4},{7,5},{8,10},{9,11},{10,... | collective-permute-start | bytes 1572872 | tf_op jit(solution)/shard_map/ppermute | solution.py:599
  332.3 21.8 %collective-permute-start.32 = (bf16[2,8,32,1152]{3,2,1,0:T(8,128)(2,1)}, bf16[2,8,32,1152]{3,2,1,0:T(8,128)(2,1)}, u32[]{:S(2)}, u32[]{:S(2)}) collective-permute-start(bf16[2,8,32,1152]{3,2,1,0:T(8,128)(2,1)} %get-tuple-element.260), channel_id=1, source_target_pairs={{0,1},{1,0},{2,3},{3,2},{4,5},{5,4},{6,7},{7,6},{8,9},{9,8},{10,11... | collective-permute-start | bytes 3538952 | tf_op jit(solution)/shard_map/ppermute | solution.py:599
  332.3 23.8 %collective-permute-start.33 = (bf16[256,1024]{1,0:T(8,128)(2,1)}, bf16[256,1024]{1,0:T(8,128)(2,1)S(1)}, u32[]{:S(2)}, u32[]{:S(2)}) collective-permute-start(bf16[256,1024]{1,0:T(8,128)(2,1)} %get-tuple-element.261), channel_id=1, source_target_pairs={{0,4},{4,0},{8,12},{12,8},{16,20},{20,16},{24,28},{28,24},{1,5},{5... | collective-permute-start | bytes 1572872 | tf_op jit(solution)/shard_map/ppermute | solution.py:599
  334.2 26.6 %collective-permute-start.34 = (bf16[256,1024]{1,0:T(8,128)(2,1)}, bf16[256,1024]{1,0:T(8,128)(2,1)}, u32[]{:S(2)}, u32[]{:S(2)}) collective-permute-start(bf16[256,1024]{1,0:T(8,128)(2,1)} %get-tuple-element.262), channel_id=1, source_target_pairs={{0,4},{4,0},{8,12},{12,8},{16,20},{20,16},{24,28},{28,24},{1,5},{5... | collective-permute-start | bytes 1572872 | tf_op jit(solution)/shard_map/ppermute | solution.py:599
  335.3 25.5 %collective-permute-start.35 = (bf16[256,1024]{1,0:T(8,128)(2,1)}, bf16[256,1024]{1,0:T(8,128)(2,1)S(1)}, u32[]{:S(2)}, u32[]{:S(2)}) collective-permute-start(bf16[256,1024]{1,0:T(8,128)(2,1)} %add.90), channel_id=1, source_target_pairs={{0,24},{4,28},{8,0},{12,4},{16,8},{20,12},{24,16},{28,20},{1,25},{... | collective-permute-start | bytes 1572872 | tf_op jit(solution)/shard_map/ppermute | solution.py:625
  348.2 21.9 %all-to-all-start.1 = ((bf16[8,32,1024]{2,1,0:T(8,128)(2,1)}), bf16[8,32,1024]{2,1,0:T(8,128)(2,1)}, u32[]{:S(2)}, u32[]{:S(2)}) async-start(bf16[8,32,1024]{2,1,0:T(8,128)(2,1)} %fusion.2), calls=%async_computation.1 | async-start | bytes 1048576 | tf_op jit(solution)/shard_map/all_to_all | solution.py:928
  360.7 18.0 %collective-permute-start.36 = (bf16[1,8,32,1152]{3,2,1,0:T(8,128)(2,1)}, bf16[1,8,32,1152]{3,2,1,0:T(8,128)(2,1)}, u32[]{:S(2)}, u32[]{:S(2)}) collective-permute-start(bf16[1,8,32,1152]{3,2,1,0:T(8,128)(2,1)} %take_add.7), channel_id=1, source_target_pairs={{0,2},{1,3},{2,0},{3,1},{4,6},{5,7},{6,4},{7,5},{8,10},{9,11},{10,... | collective-permute-start | bytes 1769480 | tf_op jit(solution)/shard_map/ppermute | solution.py:599
  362.2 24.4 %collective-permute-start.38 = (bf16[256,1024]{1,0:T(8,128)(2,1)S(1)}, bf16[256,1024]{1,0:T(8,128)(2,1)}, u32[]{:S(2)}, u32[]{:S(2)}) collective-permute-start(bf16[256,1024]{1,0:T(8,128)(2,1)S(1)} %add.93), channel_id=1, source_target_pairs={{0,24},{4,28},{8,0},{12,4},{16,8},{20,12},{24,16},{28,20},{1,25},{... | collective-permute-start | bytes 1572872 | tf_op jit(solution)/shard_map/ppermute | solution.py:625
  370.0 21.8 %collective-permute-start.39 = (bf16[256,1024]{1,0:T(8,128)(2,1)}, bf16[256,1024]{1,0:T(8,128)(2,1)}, u32[]{:S(2)}, u32[]{:S(2)}) collective-permute-start(bf16[256,1024]{1,0:T(8,128)(2,1)} %add.94), channel_id=1, source_target_pairs={{0,8},{4,12},{8,16},{12,20},{16,24},{20,28},{24,0},{28,4},{1,9},{5... | collective-permute-start | bytes 1572872 | tf_op jit(solution)/shard_map/ppermute | solution.py:625
  381.1 22.2 %all-to-all-start.2 = ((bf16[8,32,1152]{2,1,0:T(8,128)(2,1)}), bf16[8,32,1152]{2,1,0:T(8,128)(2,1)S(1)}, u32[]{:S(2)}, u32[]{:S(2)}) async-start(bf16[8,32,1152]{2,1,0:T(8,128)(2,1)} %fusion), calls=%async_computation.2 | async-start | bytes 1179648 | tf_op jit(solution)/shard_map/all_to_all | solution.py:1006
  (81 other events, 666.6 us)
Sparse Core Ops, SparseCore 0:
  34.7 80.7 all-gather.2
  197.2 61.7 reduce-scatter.2
  314.2 56.6 reduce-scatter.4
